TPU v7x, 512 devices: a whole 4x4x16 slice. The times are simulated.
512 devices in a mesh: brick: 128 (over z, x, y_hi), rep: 4 (over y_lo, core).
Axes of the slice: x: 4, y: 4 (y_hi: 2, y_lo: 2; y = y_hi * 2 + y_lo), z: 16, core: 2. Of those that a mesh axis runs over, the one named last changes fastest.
Arguments:
- teacher_in: bfloat16 [4096, 6272], P('brick'), may hold values from -6 to 6
- student_in: bfloat16 [4096, 256], P('brick'), may hold values from -6 to 6
- wigner: bfloat16 [235, 65536], P(None, ('brick', 'rep')), may hold values from -2.390625 to 2.390625
- edge_basis: bfloat16 [65536, 128], P(('brick', 'rep')), may hold values from 0 to 1
- teacher_radial: bfloat16 [128, 128], replicated, may hold values from -0.5 to 0.5
- so2_m0: bfloat16 [896, 896], P('rep'), may hold values from -0.1875 to 0.1875
- so2_m1: bfloat16 [2, 768, 768], P(None, 'rep'), may hold values from -0.15625 to 0.15625
- so2_m2: bfloat16 [2, 640, 640], P(None, 'rep'), may hold values from -0.15625 to 0.15625
- w_src: bfloat16 [256, 256], replicated, may hold values from -0.375 to 0.375
- w_dst: bfloat16 [256, 256], replicated, may hold values from -0.375 to 0.375
- w_radial: bfloat16 [128, 256], replicated, may hold values from -0.5 to 0.5
- w_out: bfloat16 [256, 256], replicated, may hold values from -0.375 to 0.375
- w_head: bfloat16 [256, 128], replicated, may hold values from -0.375 to 0.375
- src: int32 [65536], P(('brick', 'rep')), may hold values from 0 to 63, as said below
- dst: int32 [65536], P(('brick', 'rep')), may hold values from 0 to 31, as said below
- edge_count: int32 [512], P(('brick', 'rep')), may hold values from 64 to 128, as said below
- atom_count: int32 [128], P('brick'), may hold values from 16 to 32, as said below
- send_idx: int32 [128, 2, 16], P('brick'), may hold values from 0 to 32, as said below
Outputs:
- teacher_out: bfloat16 [4096, 6272], P(('brick', 'rep'))
- grad_src: float32 [256, 256], replicated
- grad_dst: float32 [256, 256], replicated
- grad_radial: float32 [128, 256], replicated
- grad_out: float32 [256, 256], replicated
- grad_head: float32 [256, 128], replicated
Inputs may be any that keep to these rules, and one draw needn't show every extreme that they name: `src`: for an edge of brick b: below atom_count[b] for an own atom, or 32 to 63 for a ghost slot. `dst`: below atom_count of the edge's brick. `edge_count`: some device's slots are all live. `atom_count`: some brick is full. `send_idx`: an own row below atom_count[b], or 32 for an empty slot; the last slot of every list is empty.
All inputs are finite; a program needn't handle non-finite values.
Results may differ from a plain program's by a relative error of at most 0.0039.
Values may be sent and summed in bfloat16 or wider, within the bound.
No kernel may reach another device: no remote copies, remote signals or barrier semaphores. Data moves between devices by JAX's collectives and lax.ppermute only.
A program may use at most 64 MiB of HBM per device.

v0:
```python
import math

import jax
import jax.numpy as jnp
from jax import lax
from jax.sharding import PartitionSpec as P

LMAX = 6
MMAX = 2
DEG = 16


def from_behind(x, axis, by):
    length = lax.axis_size(axis)
    return lax.ppermute(x, axis, [(i, (i + by) % length) for i in range(length)])


def blocks_of(wig):
    blocks = []
    offset = 0
    for degree in range(LMAX + 1):
        order_cap = min(degree, MMAX)
        row_span = 2 * order_cap + 1
        col_span = 2 * degree + 1
        blocks.append(
            wig[offset : offset + row_span * col_span].reshape(row_span, col_span, wig.shape[1])
        )
        offset = offset + row_span * col_span
    return blocks


def rotate_into(sources, blocks, edge_gain):
    edge_total = sources.shape[0]
    coef_grid = sources.reshape(edge_total, (LMAX + 1) ** 2, -1)
    turned = []
    for degree in range(LMAX + 1):
        coeffs = coef_grid[:, degree * degree : (degree + 1) * (degree + 1), :]
        rotated = jnp.einsum(
            "mje,ejc->emc", blocks[degree], coeffs, preferred_element_type=jnp.float32
        )
        turned.append(rotated * edge_gain[:, None, :])
    centre = jnp.stack([turned[degree][:, min(degree, MMAX)] for degree in range(LMAX + 1)], axis=1)
    vectors = [centre.reshape(edge_total, -1).astype(jnp.bfloat16)]
    for morder in range(1, MMAX + 1):
        upper_part = jnp.stack(
            [turned[degree][:, min(degree, MMAX) + morder] for degree in range(morder, LMAX + 1)],
            axis=1,
        )
        lower_part = jnp.stack(
            [turned[degree][:, min(degree, MMAX) - morder] for degree in range(morder, LMAX + 1)],
            axis=1,
        )
        joined = jnp.concatenate(
            [upper_part.reshape(edge_total, -1), lower_part.reshape(edge_total, -1)], axis=1
        )
        vectors.append(joined.astype(jnp.bfloat16))
    return vectors


def order_mixing(vectors, weights):
    results = [
        jnp.dot(vectors[0], weights[0], preferred_element_type=jnp.float32).astype(jnp.bfloat16)
    ]
    for morder in range(1, MMAX + 1):
        real_part = weights[morder][0]
        imag_part = weights[morder][1]
        coupled = jnp.concatenate(
            [
                jnp.concatenate([real_part, imag_part], axis=1),
                jnp.concatenate([-imag_part, real_part], axis=1),
            ],
            axis=0,
        )
        results.append(
            jnp.dot(vectors[morder], coupled, preferred_element_type=jnp.float32).astype(
                jnp.bfloat16
            )
        )
    return results


def rotate_back(outputs, blocks, edge_mask):
    edge_total = outputs[0].shape[0]
    centre = outputs[0].reshape(edge_total, LMAX + 1, -1)
    side_parts = [None]
    for morder in range(1, MMAX + 1):
        side_parts.append(outputs[morder].reshape(edge_total, 2, LMAX + 1 - morder, -1))
    pieces = []
    for degree in range(LMAX + 1):
        order_cap = min(degree, MMAX)
        entries = []
        for signed in range(-order_cap, order_cap + 1):
            if signed == 0:
                entries.append(centre[:, degree])
            elif signed > 0:
                entries.append(side_parts[signed][:, 0, degree - signed])
            else:
                entries.append(side_parts[-signed][:, 1, degree + signed])
        stacked = jnp.stack(entries, axis=1)
        pieces.append(
            jnp.einsum("mje,emc->ejc", blocks[degree], stacked, preferred_element_type=jnp.float32)
        )
    message = jnp.concatenate(pieces, axis=1) * edge_mask[:, None, None]
    return message.astype(jnp.bfloat16).reshape(edge_total, -1)


def inner_rows(left_side, right_side):
    return lax.dot_general(
        left_side, right_side, (((0,), (0,)), ((), ())), preferred_element_type=jnp.float32
    )


def outer_cols(left_side, right_side):
    return lax.dot_general(
        left_side, right_side, (((1,), (1,)), ((), ())), preferred_element_type=jnp.float32
    )


def per_device(
    teacher_in,
    student_in,
    wigner,
    edge_basis,
    teacher_radial,
    so2_m0,
    so2_m1,
    so2_m2,
    w_src,
    w_dst,
    w_radial,
    w_out,
    w_head,
    src,
    dst,
    edge_count,
    atom_count,
    send_idx,
):
    own_rows = teacher_in.shape[0]
    edge_total = src.shape[0]
    channels = teacher_radial.shape[1]
    bricks = lax.axis_size("brick")
    replicas = lax.axis_size("rep")
    quarter = own_rows // replicas
    row_start = lax.axis_index("rep") * quarter
    inv_degree = 1.0 / math.sqrt(DEG)
    inv_atoms = 1.0 / (own_rows * bricks)
    send_lists = send_idx[0]
    teacher_pad = jnp.concatenate(
        [teacher_in, jnp.zeros((1, teacher_in.shape[1]), jnp.bfloat16)], axis=0
    )
    student_pad = jnp.concatenate(
        [student_in, jnp.zeros((1, student_in.shape[1]), jnp.bfloat16)], axis=0
    )
    left_from = from_behind(
        (
            jnp.take(teacher_pad, send_lists[0], axis=0),
            jnp.take(student_pad, send_lists[0], axis=0),
        ),
        "brick",
        1,
    )
    right_from = from_behind(
        (
            jnp.take(teacher_pad, send_lists[1], axis=0),
            jnp.take(student_pad, send_lists[1], axis=0),
        ),
        "brick",
        -1,
    )
    weights = (
        lax.all_gather(so2_m0, "rep", axis=0, tiled=True),
        lax.all_gather(so2_m1, "rep", axis=1, tiled=True),
        lax.all_gather(so2_m2, "rep", axis=1, tiled=True),
    )
    teacher_ext = jnp.concatenate([teacher_in, left_from[0], right_from[0]], axis=0)
    student_ext = jnp.concatenate([student_in, left_from[1], right_from[1]], axis=0)
    edge_mask = (jnp.arange(edge_total, dtype=jnp.int32) < edge_count[0]).astype(jnp.float32)
    atom_mask = (jnp.arange(own_rows, dtype=jnp.int32) < atom_count[0]).astype(jnp.float32)
    edge_gain = jnp.dot(edge_basis, teacher_radial, preferred_element_type=jnp.float32)
    blocks = blocks_of(wigner)
    vectors = rotate_into(jnp.take(teacher_ext, src, axis=0), blocks, edge_gain)
    outputs = order_mixing(vectors, weights)
    message = rotate_back(outputs, blocks, edge_mask)
    onehot = (dst[None, :] == jnp.arange(own_rows, dtype=jnp.int32)[:, None]).astype(jnp.bfloat16)
    partial_teacher = jnp.dot(onehot, message, preferred_element_type=jnp.float32)
    student_src = jnp.take(student_ext, src, axis=0)
    student_dst = jnp.take(student_in, dst, axis=0)
    hidden = (
        jnp.dot(student_src, w_src, preferred_element_type=jnp.float32)
        + jnp.dot(student_dst, w_dst, preferred_element_type=jnp.float32)
        + jnp.dot(edge_basis, w_radial, preferred_element_type=jnp.float32)
    )
    gated_edges = (jax.nn.silu(hidden) * edge_mask[:, None]).astype(jnp.bfloat16)
    partial_student = jnp.dot(onehot, gated_edges, preferred_element_type=jnp.float32)
    summed_teacher, summed_student = lax.psum((partial_teacher, partial_student), "rep")
    teacher_full = (teacher_in.astype(jnp.float32) + inv_degree * summed_teacher).astype(
        jnp.bfloat16
    )
    pooled = (summed_student * inv_degree).astype(jnp.bfloat16)
    updated = (
        student_in.astype(jnp.float32) + jnp.dot(pooled, w_out, preferred_element_type=jnp.float32)
    ).astype(jnp.bfloat16)
    predicted = jnp.dot(updated, w_head, preferred_element_type=jnp.float32)
    residual = (predicted - teacher_full[:, :channels].astype(jnp.float32)) * atom_mask[:, None]
    scaled = (residual * inv_atoms).astype(jnp.bfloat16)
    teacher_out = lax.dynamic_slice_in_dim(teacher_full, row_start, quarter, 0)
    pooled_part = lax.dynamic_slice_in_dim(pooled, row_start, quarter, 0)
    updated_part = lax.dynamic_slice_in_dim(updated, row_start, quarter, 0)
    scaled_part = lax.dynamic_slice_in_dim(scaled, row_start, quarter, 0)
    grad_head = inner_rows(updated_part, scaled_part)
    upstream = outer_cols(scaled, w_head).astype(jnp.bfloat16)
    grad_out = inner_rows(pooled_part, lax.dynamic_slice_in_dim(upstream, row_start, quarter, 0))
    pooled_grad = outer_cols(upstream, w_out).astype(jnp.bfloat16)
    edge_grad = (
        jnp.take(pooled_grad, dst, axis=0).astype(jnp.float32) * (inv_degree * edge_mask)[:, None]
    )
    logistic = jax.nn.sigmoid(hidden)
    hidden_grad = (edge_grad * logistic * (1.0 + hidden * (1.0 - logistic))).astype(jnp.bfloat16)
    grad_src = inner_rows(student_src, hidden_grad)
    grad_dst = inner_rows(student_dst, hidden_grad)
    grad_radial = inner_rows(edge_basis, hidden_grad)
    totals = lax.psum((grad_src, grad_dst, grad_radial, grad_out, grad_head), ("brick", "rep"))
    return (teacher_out, totals[0], totals[1], totals[2], totals[3], totals[4])


def solution(mesh):
    placed = (
        P("brick", None),
        P("brick", None),
        P(None, ("brick", "rep")),
        P(("brick", "rep"), None),
        P(),
        P("rep", None),
        P(None, "rep", None),
        P(None, "rep", None),
        P(),
        P(),
        P(),
        P(),
        P(),
        P(("brick", "rep")),
        P(("brick", "rep")),
        P(("brick", "rep")),
        P("brick"),
        P("brick", None, None),
    )
    return jax.shard_map(
        per_device,
        mesh=mesh,
        in_specs=placed,
        out_specs=(P(("brick", "rep"), None), P(), P(), P(), P(), P()),
        check_vma=False,
    )
```

profile of v0, /device:TPU:1, one launch (start us, length us, event | category | flops | bytes accessed | tf_op | source)
XLA Modules:
  0.0 726.1 jit_solution(15870657628490498895)
XLA Ops:
  11.4 16.8 %collective-permute-start.1 = (bf16[16,6272]{1,0:T(8,128)(2,1)S(1)}, bf16[16,6272]{1,0:T(8,128)(2,1)S(1)}, u32[]{:S(2)}, u32[]{:S(2)}) collective-permute-start(bf16[16,6272]{1,0:T(8,128)(2,1)S(1)} %broadcast_select_fusion.1), channel_id=1, source_target_pairs={{0,508},{4,0},{8,4},{12,8},{16,12},{20,16},{24,20},{28,24},{32,28}... | collective-permute-start | bytes 602120 | tf_op jit(solution)/shard_map/ppermute | solution.py:15
  29.0 1.9 collective-permute-start
  31.6 9.1 %collective-permute-start.3 = (bf16[16,256]{1,0:T(8,128)(2,1)S(1)}, bf16[16,256]{1,0:T(8,128)(2,1)S(1)}, u32[]{:S(2)}, u32[]{:S(2)}) collective-permute-start(bf16[16,256]{1,0:T(8,128)(2,1)S(1)} %broadcast_select_fusion.9), channel_id=1, source_target_pairs={{0,508},{4,0},{8,4},{12,8},{16,12},{20,16},{24,20},{28,24},{32,28}... | collective-permute-start | bytes 24584 | tf_op jit(solution)/shard_map/ppermute | solution.py:15
  41.3 1.9 collective-permute-start.2
  55.0 1.5 gather_fusion.1
  56.6 2.8 gather_fusion
  59.4 3.1 copy.57
  63.6 1.2 copy.73
  65.7 2.3 copy.67
  70.8 2.2 fusion.71
  79.3 1.2 copy.72
  83.2 1.2 fusion.38
  87.6 2.1 convolution_convert_fusion
  90.6 1.3 fusion.66
  93.2 1.4 fusion.17
  96.4 30.5 %all-gather.6.cloned.1.call-done = bf16[2,768,768]{2,1,0:T(8,128)(2,1)} async-done(((bf16[2,192,768]{2,1,0:T(8,128)(2,1)}), bf16[2,768,768]{2,1,0:T(8,128)(2,1)}) %all-gather.6.cloned.1.call-update) | async-done | bytes 2359312 | tf_op jit(solution)/shard_map/all_gather | solution.py:173
  126.9 1.9 slice_bitcast_fusion
  129.4 2.6 fusion.20
  132.0 1.2 copy.77
  133.9 1.5 constant_dynamic-update-slice_fusion.51
  144.7 1.3 convolution_bitcast_fusion
  146.0 26.2 %concatenate.53 = f32[128,49,128]{2,1,0:T(8,128)} concatenate(f32[128,1,128]{2,1,0:T(1,128)} %copy.91, f32[128,3,128]{2,1,0:T(4,128)} %convolution_bitcast_fusion.5, f32[128,5,128]{2,1,0:T(8,128)} %convolution_bitcast_fusion.4, f32[128,7,128]{2,1,0:T(8,128)} %convolution_bitcast_fusion.3, f32[128,9,128]{2,1,0:T(8,128)S(1)} %convolution_bitcast_fusion.2, ...), dimensions={1} | concatenate | bytes 6422528 | tf_op jit(solution)/shard_map/concatenate | solution.py:103
  172.2 3.7 copy.92
  176.6 1.6 fusion.48
  178.7 10.3 %psum.50 = f32[32,256]{1,0:T(8,128)S(1)} all-reduce(f32[32,256]{1,0:T(8,128)S(1)} %fusion.43), channel_id=1, replica_groups=mesh['brick'=128,'rep'=4] {'rep'}, use_global_device_ids=true, to_apply=%region_1.5 | all-reduce | flops 8192 | bytes 65536 | tf_op jit(solution)/shard_map/psum | solution.py:196
  189.1 45.2 %all-reduce.6.cloned.1.call-done = f32[32,6272]{1,0:T(8,128)} async-done(((f32[32,6272]{1,0:T(8,128)}), f32[32,6272]{1,0:T(8,128)}) %all-reduce.6.cloned.1.call-update) | async-done | bytes 802832 | tf_op jit(solution)/shard_map/psum | solution.py:196
  234.3 1.2 add_convert_fusion
  242.5 469.7 %all-reduce.8.cloned.1.call-done = (f32[256,256]{1,0:T(8,128)}, f32[256,256]{1,0:T(8,128)}, f32[128,256]{0,1:T(8,128)}, f32[256,256]{1,0:T(8,128)}, f32[256,128]{1,0:T(8,128)}) async-done(((f32[256,256]{1,0:T(8,128)}, f32[256,256]{1,0:T(8,128)}, f32[128,256]{0,1:T(8,128)}, f32[256,256]{1,0:T(8,128)}, f32[256,128]{1,0:T(8,128)}), (f32[256,256]{1,0:T(8,128)}, f32[256,256]{1,0:T(8,128)}, f32[128,256]{0,1:T(8,128)}, ...) | async-done | bytes 1048592 | tf_op jit(solution)/shard_map/psum | solution.py:223
  712.2 1.7 copy.93
  713.9 1.7 copy.146
  715.6 1.7 copy.147
  717.2 1.7 copy.148
  (249 shorter events, 56.5 us)
Async XLA Ops:
  7.2 40.9 %copy-start = (bf16[256,256]{1,0:T(8,128)(2,1)S(1)}, bf16[256,256]{1,0:T(8,128)(2,1)}, u32[]{:S(2)}) copy-start(bf16[256,256]{1,0:T(8,128)(2,1)} %param.33) | copy-start | bytes 393220
  7.2 80.4 %all-gather.4.cloned.1.call-start = ((), (), s32[]{:S(2)}) async-start(), calls=%async_computation | async-start | bytes 2007040 | tf_op jit(solution)/shard_map/all_gather | solution.py:172
  7.9 82.7 %all-gather.8.cloned.1.call-start = ((), (), s32[]{:S(2)}) async-start(), calls=%async_computation.2 | async-start | bytes 2048000 | tf_op jit(solution)/shard_map/all_gather | solution.py:174
  8.7 118.3 %all-gather.6.cloned.1.call-start = ((), (), s32[]{:S(2)}) async-start(), calls=%async_computation.1 | async-start | bytes 2949120 | tf_op jit(solution)/shard_map/all_gather | solution.py:173
  11.2 19.7 %copy-start.1 = (bf16[32,256]{1,0:T(8,128)(2,1)S(1)}, bf16[32,256]{1,0:T(8,128)(2,1)}, u32[]{:S(2)}) copy-start(bf16[32,256]{1,0:T(8,128)(2,1)} %param.25) | copy-start | bytes 49156
  11.2 32.1 %copy-start.56 = (s32[128]{0:T(128)S(1)}, s32[128]{0:T(128)}, u32[]{:S(2)}) copy-start(s32[128]{0:T(128)} %param.37) | copy-start | bytes 1540
  11.2 32.1 %copy-start.54 = (s32[128]{0:T(128)S(1)}, s32[128]{0:T(128)}, u32[]{:S(2)}) copy-start(s32[128]{0:T(128)} %param.38) | copy-start | bytes 1540
  11.2 32.2 %copy-start.39 = (bf16[235,128]{1,0:T(8,128)(2,1)S(1)}, bf16[235,128]{1,0:T(8,128)(2,1)}, u32[]{:S(2)}) copy-start(bf16[235,128]{1,0:T(8,128)(2,1)} %param.26) | copy-start | bytes 180484
  11.4 45.2 %collective-permute-start.1 = (bf16[16,6272]{1,0:T(8,128)(2,1)S(1)}, bf16[16,6272]{1,0:T(8,128)(2,1)S(1)}, u32[]{:S(2)}, u32[]{:S(2)}) collective-permute-start(bf16[16,6272]{1,0:T(8,128)(2,1)S(1)} %broadcast_select_fusion.1), channel_id=1, source_target_pairs={{0,508},{4,0},{8,4},{12,8},{16,12},{20,16},{24,20},{28,24},{32,28}... | collective-permute-start | bytes 602120 | tf_op jit(solution)/shard_map/ppermute | solution.py:15
  28.2 19.1 %copy-start.30 = (bf16[128,128]{1,0:T(8,128)(2,1)S(1)}, bf16[128,128]{1,0:T(8,128)(2,1)}, u32[]{:S(2)}) copy-start(bf16[128,128]{1,0:T(8,128)(2,1)} %param.27) | copy-start | bytes 98308
  28.2 19.1 %copy-start.40 = (bf16[128,256]{1,0:T(8,128)(2,1)S(1)}, bf16[128,256]{1,0:T(8,128)(2,1)}, u32[]{:S(2)}) copy-start(bf16[128,256]{1,0:T(8,128)(2,1)} %param.34) | copy-start | bytes 196612
  29.0 27.6 %collective-permute-start = (bf16[16,6272]{1,0:T(8,128)(2,1)S(1)}, bf16[16,6272]{1,0:T(8,128)(2,1)S(1)}, u32[]{:S(2)}, u32[]{:S(2)}) collective-permute-start(bf16[16,6272]{1,0:T(8,128)(2,1)S(1)} %broadcast_select_fusion.2), channel_id=1, source_target_pairs={{0,4},{4,8},{8,12},{12,16},{16,20},{20,24},{24,28},{28,32},{32,36}... | collective-permute-start | bytes 602120 | tf_op jit(solution)/shard_map/ppermute | solution.py:15
  31.6 23.4 %collective-permute-start.3 = (bf16[16,256]{1,0:T(8,128)(2,1)S(1)}, bf16[16,256]{1,0:T(8,128)(2,1)S(1)}, u32[]{:S(2)}, u32[]{:S(2)}) collective-permute-start(bf16[16,256]{1,0:T(8,128)(2,1)S(1)} %broadcast_select_fusion.9), channel_id=1, source_target_pairs={{0,508},{4,0},{8,4},{12,8},{16,12},{20,16},{24,20},{28,24},{32,28}... | collective-permute-start | bytes 24584 | tf_op jit(solution)/shard_map/ppermute | solution.py:15
  41.3 13.7 %collective-permute-start.2 = (bf16[16,256]{1,0:T(8,128)(2,1)S(1)}, bf16[16,256]{1,0:T(8,128)(2,1)S(1)}, u32[]{:S(2)}, u32[]{:S(2)}) collective-permute-start(bf16[16,256]{1,0:T(8,128)(2,1)S(1)} %broadcast_select_fusion.10), channel_id=1, source_target_pairs={{0,4},{4,8},{8,12},{12,16},{16,20},{20,24},{24,28},{28,32},{32,36}... | collective-permute-start | bytes 24584 | tf_op jit(solution)/shard_map/ppermute | solution.py:15
  43.3 191.0 %all-reduce.6.cloned.1.call-start = ((), (), s32[]{:S(2)}) async-start(), calls=%async_computation.3 | async-start | bytes 1605632 | tf_op jit(solution)/shard_map/psum | solution.py:196
  43.4 19.1 %copy-start.48 = (pred[128]{0:T(512)(128)(4,1)}, pred[128]{0:T(512)(128)(4,1)S(1)}, u32[]{:S(2)}) copy-start(pred[128]{0:T(512)(128)(4,1)S(1)} %compare_and_fusion.3) | copy-start | bytes 388
  43.4 6.1 copy-start.46
  46.0 9.1 %copy-start.23 = (bf16[128,256]{1,0:T(8,128)(2,1)}, bf16[128,256]{1,0:T(8,128)(2,1)S(1)}, u32[]{:S(2)}) copy-start(bf16[128,256]{1,0:T(8,128)(2,1)S(1)} %gather_fusion.6) | copy-start | bytes 196612
  46.0 10.6 %copy-start.6 = (bf16[32,6272]{1,0:T(8,128)(2,1)S(1)}, bf16[32,6272]{1,0:T(8,128)(2,1)}, u32[]{:S(2)}) copy-start(bf16[32,6272]{1,0:T(8,128)(2,1)} %param.24) | copy-start | bytes 1204228
  64.8 5.3 copy-start.8
  74.2 4.9 copy-start.13
  137.8 4.7 copy-start.33
  178.1 10.9 %copy-start.26 = (bf16[256,256]{1,0:T(8,128)(2,1)S(1)}, bf16[256,256]{1,0:T(8,128)(2,1)}, u32[]{:S(2)}) copy-start(bf16[256,256]{1,0:T(8,128)(2,1)} %param.35) | copy-start | bytes 393220
  178.1 56.2 %copy-start.7 = (bf16[32,6272]{1,0:T(8,128)(2,1)S(1)}, bf16[32,6272]{1,0:T(8,128)(2,1)}, u32[]{:S(2)}) copy-start(bf16[32,6272]{1,0:T(8,128)(2,1)} %param.24) | copy-start | bytes 1204228
  178.1 57.4 %copy-start.41 = (bf16[256,128]{1,0:T(8,128)(2,1)S(1)}, bf16[256,128]{1,0:T(8,128)(2,1)}, u32[]{:S(2)}) copy-start(bf16[256,128]{1,0:T(8,128)(2,1)} %param.36) | copy-start | bytes 196612
  178.2 57.4 %copy-start.57 = (f32[32]{0:T(128)S(1)}, f32[32]{0:T(128)}, u32[]{:S(2)}) copy-start(f32[32]{0:T(128)} %compare_convert_fusion) | copy-start | bytes 388
  178.2 534.0 %all-reduce.8.cloned.1.call-start = ((), (), s32[]{:S(2)}) async-start(), calls=%async_computation.4 | async-start | bytes 2097152 | tf_op jit(solution)/shard_map/psum | solution.py:223
  178.5 58.5 %copy-start.47 = (pred[128]{0:T(512)(128)(4,1)S(1)}, pred[128]{0:T(512)(128)(4,1)}, u32[]{:S(2)}) copy-start(pred[128]{0:T(512)(128)(4,1)} %copy-done.46) | copy-start | bytes 388
  178.5 58.6 %copy-start.52 = (f32[128]{0:T(128)S(1)}, f32[128]{0:T(128)}, u32[]{:S(2)}) copy-start(f32[128]{0:T(128)} %compare_select_fusion.4) | copy-start | bytes 1540
  189.1 49.0 %copy-start.24 = (bf16[128,256]{1,0:T(8,128)(2,1)S(1)}, bf16[128,256]{1,0:T(8,128)(2,1)}, u32[]{:S(2)}) copy-start(bf16[128,256]{1,0:T(8,128)(2,1)} %copy-done.23) | copy-start | bytes 196612
  189.1 50.0 %copy-start.32 = (bf16[128,128]{1,0:T(8,128)(2,1)S(1)}, bf16[128,128]{1,0:T(8,128)(2,1)}, u32[]{:S(2)}) copy-start(bf16[128,128]{1,0:T(8,128)(2,1)} %param.27) | copy-start | bytes 98308
  712.2 6.7 copy-start.37
  (37 other events, 108.6 us)
Sparse Core Ops, SparseCore 0:
  10.1 39.8 all-gather.3
  52.1 32.6 all-gather.7
  86.9 39.9 all-gather.5
  178.3 56.0 all-reduce.5
  241.9 470.2 all-reduce.7
where the time goes:
time: 728 us; the launch traced here: 726 us
  waiting for transfers between devices  547 us (75%)
  local copies, waits for them, and re-layouts  88.3 us (12%)
  starting transfers between devices  29.9 us (4%)
  matrix products  27.1 us (4%)
  between operations  16 us (2%)
  blocking collectives  10.3 us (1%)
  other arithmetic  7.67 us (1%)
    psum x1, waiting for transfers between devices, per_device(): lax.psum((grad_src, grad_dst, grad_radial, grad_out, grad_head), ('brick'...  470 us
    psum x1, waiting for transfers between devices, per_device(): lax.psum((partial_teacher, partial_student), 'rep')  45.2 us
    all_gather x1, waiting for transfers between devices, per_device(): lax.all_gather(so2_m1, 'rep', axis=1, tiled=True)  30.5 us
    concatenate x2, local copies, waits for them, and re-layouts, rotate_back(): message = jnp.concatenate(pieces, axis=1) * edge_mask[:, None, None]  29.8 us
    ppermute x4, starting transfers between devices, from_behind(): lax.ppermute(x, axis, [(i, (i + by) % length) for i in range(length)])  29.7 us
    unnamed x130, local copies, waits for them, and re-layouts  16.5 us
  transfers between devices with their start and end apart: 9, of which 3 were waited for; matrix products, arithmetic and copies ran while one was open for 8% of the time, Pallas kernels for 0%

commit v1 on v0

v1 whole, which is shorter than its diff:
```python
import functools
import math

import jax
import jax.numpy as jnp
from jax import lax
from jax.experimental import pallas as pl
from jax.experimental.pallas import tpu as pltpu
from jax.sharding import Mesh, PartitionSpec as P

LMAX = 6
MMAX = 2
DEG = 16
C = 128
OWN = 32
EXT = 64
EDGE = 128
SW = 256
KC = 6272
LOW = 7 * 224 + 6 * 192
HIGH = 6 * 192 + 10 * 160
SECTIONS = {0: (224, 0), 1: (192, 224), -1: (192, 416), 2: (160, 608), -2: (160, 768)}
BF = jnp.bfloat16
F32 = jnp.float32
BRICK = ("z", "x", "yh")
REP = ("yl", "core")
PLANE = ("x", "yh", "yl", "core")
VMEM = pl.BlockSpec(memory_space=pltpu.VMEM)
SMEM = pl.BlockSpec(memory_space=pltpu.SMEM)
PARAMS = pltpu.CompilerParams(vmem_limit_bytes=48 * 1024 * 1024)


def offsets():
    found = []
    row = 0
    for degree in range(LMAX + 1):
        found.append(row)
        row += (2 * min(degree, MMAX) + 1) * (2 * degree + 1)
    return found


OFFSET = offsets()


def dot(left, right, over=((1,), (0,))):
    return lax.dot_general(left, right, (over, ((), ())), preferred_element_type=F32)


def dst_onehot(dst_row):
    return dst_row == lax.broadcasted_iota(jnp.int32, (OWN, EDGE), 0)


def live_row(count):
    return lax.broadcasted_iota(jnp.int32, (1, EDGE), 1) < count


def live_col(count):
    return lax.broadcasted_iota(jnp.int32, (EDGE, 1), 0) < count


def send_body(lists_ref, teacher_ref, student_ref, next_ref, prev_ref):
    rows = lax.broadcasted_iota(jnp.int32, (32, OWN), 1)
    pick = (lists_ref[...] == rows).astype(BF)
    teacher = dot(pick, teacher_ref[...]).astype(BF)
    student = dot(pick, student_ref[...]).astype(BF)
    next_ref[:, :KC] = teacher[:16]
    prev_ref[:, :KC] = teacher[16:]
    next_ref[:, KC:] = student[:16]
    prev_ref[:, KC:] = student[16:]


def pack_body(m0_ref, m1_ref, m2_ref, all_ref, low_ref, high_ref):
    at = 0
    for part, wide, high in (
        (m0_ref, 7, 224), (m1_ref.at[0], 6, 192), (m1_ref.at[1], 6, 192),
        (m2_ref.at[0], 5, 160), (m2_ref.at[1], 5, 160),
    ):
        for n in range(wide):
            block = part[:, n * C : (n + 1) * C]
            all_ref[at : at + high] = block
            if at < LOW:
                low_ref[at : at + high] = block
            else:
                high_ref[at - LOW : at - LOW + high] = block
            at += high


def keep_turned(pack_ref, block, start, part, base):
    row = 0
    while row < C:
        which = (start + row) // part
        inside = (start + row) % part
        size = min(C - row, part - inside)
        pack_ref[which, base + inside : base + inside + size] = block[row : row + size]
        row += size


def front_body(
    count_ref, teacher_ref, left_ref, right_ref, student_ref, wig_ref, basis_ref, radial_ref,
    src_ref, dst_ref, m0_ref, wsrc_ref, wdst_ref, wrad_ref,
    pack_ref, small_ref, hidden_ref, ssrc_ref, sdst_ref,
    wigf_ref, turn_ref,
):
    count = count_ref[0]
    wigf_ref[...] = wig_ref[...].astype(F32)
    source = (src_ref[...] == lax.broadcasted_iota(jnp.int32, (EXT, EDGE), 0)).astype(F32)
    target = dst_onehot(dst_ref[...])
    basis = basis_ref[...]
    basis_t = basis.astype(F32).T.astype(BF)
    gain = dot(radial_ref[...], basis_t, ((0,), (0,)))
    for degree in range(LMAX + 1):
        cap = min(degree, MMAX)
        span = 2 * degree + 1
        orders = 2 * cap + 1
        for morder in range(orders):
            for j in range(span):
                row = OFFSET[degree] + morder * span + j
                turn_ref[j * EXT : (j + 1) * EXT, morder * EDGE : (morder + 1) * EDGE] = (
                    source * wigf_ref[row : row + 1, :]
                ).astype(BF)
        parts = []
        for j in range(span):
            lo = (degree * degree + j) * C
            parts += [
                teacher_ref[:, lo : lo + C],
                left_ref[:, lo : lo + C],
                right_ref[:, lo : lo + C],
            ]
        stacked = jnp.concatenate(parts, axis=0)
        turned = dot(stacked, turn_ref[: span * EXT, : orders * EDGE], ((0,), (0,)))
        for morder in range(orders):
            block = (turned[:, morder * EDGE : (morder + 1) * EDGE] * gain).astype(BF)
            signed = morder - cap
            part, base = SECTIONS[signed]
            keep_turned(pack_ref, block, (degree - abs(signed)) * C, part, base)
    invariant = dot(pack_ref[0, :224], m0_ref[0], ((0,), (0,)))
    for r in range(1, 4):
        invariant += dot(pack_ref[r, :224], m0_ref[r], ((0,), (0,)))
    live = live_row(count)
    scatter = jnp.where(target & live, wigf_ref[0:1, :], 0.0).astype(BF)
    student_ext = jnp.concatenate(
        [student_ref[...], left_ref[:, KC:], right_ref[:, KC:]], axis=0
    )
    ssrc = dot(source.astype(BF), student_ext, ((0,), (0,))).astype(BF)
    onehot = target.astype(F32).astype(BF)
    sdst = dot(onehot, student_ref[...], ((0,), (0,))).astype(BF)
    hidden = dot(ssrc, wsrc_ref[...]) + dot(sdst, wdst_ref[...]) + dot(basis, wrad_ref[...])
    gated = jnp.where(live_col(count), hidden * jax.nn.sigmoid(hidden), 0.0).astype(BF)
    small = jnp.concatenate(
        [dot(scatter, invariant.astype(BF)), dot(onehot, gated)], axis=1
    )
    for r in range(4):
        small_ref[r] = small
    hidden_ref[...] = hidden
    ssrc_ref[...] = ssrc
    sdst_ref[...] = sdst


def student_body(
    inv_atoms, count_ref, atoms_ref, rep_ref, smalls_ref, teacher_ref,
    student_ref, wout_ref, whead_ref, hidden_ref, ssrc_ref, sdst_ref, basis_ref, dst_ref,
    grad_ref,
):
    inv_degree = 1.0 / math.sqrt(DEG)
    sums = (smalls_ref[0] + smalls_ref[1]) + (smalls_ref[2] + smalls_ref[3])
    target = (teacher_ref[...].astype(F32) + inv_degree * sums[:, :C]).astype(BF)
    pooled = (sums[:, C:] * inv_degree).astype(BF)
    updated = (student_ref[...].astype(F32) + dot(pooled, wout_ref[...])).astype(BF)
    predicted = dot(updated, whead_ref[...])
    rows = lax.broadcasted_iota(jnp.int32, (OWN, 1), 0)
    residual = jnp.where(rows < atoms_ref[0], predicted - target.astype(F32), 0.0)
    scaled = (residual * inv_atoms).astype(BF)
    upstream = dot(scaled, whead_ref[...], ((1,), (1,))).astype(BF)
    lo = rep_ref[0] * 8
    mine = (rows >= lo) & (rows < lo + 8)
    scaled_part = jnp.where(mine, scaled.astype(F32), 0.0).astype(BF)
    upstream_part = jnp.where(mine, upstream.astype(F32), 0.0).astype(BF)
    grad_head = dot(updated, scaled_part, ((0,), (0,)))
    grad_out = dot(pooled, upstream_part, ((0,), (0,)))
    pooled_grad = dot(upstream, wout_ref[...], ((1,), (1,))).astype(BF)
    onehot = dst_onehot(dst_ref[...]).astype(F32).astype(BF)
    weight = jnp.where(live_col(count_ref[0]), inv_degree, 0.0)
    edge_grad = dot(onehot, pooled_grad, ((0,), (0,))) * weight
    hidden = hidden_ref[...]
    logistic = jax.nn.sigmoid(hidden)
    hidden_grad = (edge_grad * logistic * (1.0 + hidden * (1.0 - logistic))).astype(BF)
    for start, stop, value in (
        (0, 256, dot(ssrc_ref[...], hidden_grad, ((0,), (0,)))),
        (256, 512, dot(sdst_ref[...], hidden_grad, ((0,), (0,)))),
        (512, 768, grad_out),
        (768, 896, dot(basis_ref[...], hidden_grad, ((0,), (0,)))),
        (896, 1024, jnp.concatenate([grad_head[:C], grad_head[C:]], axis=1)),
    ):
        high = grad_ref.shape[1]
        grad_ref[start // high : stop // high] = value.astype(BF).reshape(-1, high, SW)


def spread_body(parts_ref, out_ref):
    total = parts_ref[0].astype(F32)
    for i in range(1, parts_ref.shape[0]):
        total += parts_ref[i].astype(F32)
    total = total.astype(out_ref.dtype)
    for i in range(out_ref.shape[0]):
        out_ref[i] = total


def unpack_body(all_ref, src_ref, dst_ref, radial_ref, out_ref, head_ref):
    values = all_ref[...].astype(F32).reshape(1024, SW)
    src_ref[...] = values[:256]
    dst_ref[...] = values[256:512]
    out_ref[...] = values[512:768]
    radial_ref[...] = values[768:896]
    head_ref[:C] = values[896:, :C]
    head_ref[C:] = values[896:, C:]


def blocks(ref, at, count, high):
    return jnp.concatenate(
        [ref[at + n * high : at + (n + 1) * high] for n in range(count)], axis=1
    )


def mix_body(
    count_ref, rep_ref, pack_ref, own_ref, near_ref, low_ref, high_ref, far_low_ref, far_high_ref,
    wig_ref, dst_ref,
    o0_ref, o1_ref, o2_ref, o3_ref,
    wigf_ref, back_ref, sums_ref,
):
    rep = rep_ref[0]
    live = live_row(count_ref[0])
    target = (dst_onehot(dst_ref[...]) & live).astype(F32)
    wigf_ref[...] = wig_ref[...].astype(F32)
    lows = (own_ref, near_ref, low_ref, far_low_ref)
    highs = (own_ref.at[LOW:], near_ref.at[LOW:], high_ref, far_high_ref)
    over = ((0,), (0,))
    y0 = 0.0
    for k in range(4):
        y0 += dot(pack_ref[rep ^ k, :224], blocks(lows[k], 0, 7, 224), over)
    y0 = y0.astype(BF)
    mixed = [None]
    for wide, base in ((6, 224), (5, 608)):
        size = wide * 32
        real = 0.0
        imag = 0.0
        for k in range(4):
            pair = jnp.concatenate(
                [
                    pack_ref[rep ^ k, base : base + size],
                    pack_ref[rep ^ k, base + size : base + 2 * size],
                ],
                axis=1,
            )
            if wide == 6:
                first = blocks(lows[k], 1568, 6, 192)
                second = blocks(highs[k], 0, 6, 192)
            else:
                first = blocks(highs[k], 1152, 5, 160)
                second = blocks(highs[k], 1952, 5, 160)
            real += dot(pair, first, over)
            imag += dot(pair, second, over)
        plus = (real[:EDGE] - imag[EDGE:]).astype(BF)
        minus = (imag[:EDGE] + real[EDGE:]).astype(BF)
        mixed.append((plus, minus))
    for degree in range(LMAX + 1):
        cap = min(degree, MMAX)
        span = 2 * degree + 1
        orders = 2 * cap + 1
        stacked = []
        for morder in range(orders):
            signed = morder - cap
            if signed == 0:
                stacked.append(y0[:, degree * C : (degree + 1) * C])
            else:
                slot = degree - abs(signed)
                part = mixed[abs(signed)][0 if signed > 0 else 1]
                stacked.append(part[:, slot * C : (slot + 1) * C])
            for j in range(span):
                row = OFFSET[degree] + morder * span + j
                back_ref[j * OWN : (j + 1) * OWN, morder * EDGE : (morder + 1) * EDGE] = (
                    target * wigf_ref[row : row + 1, :]
                ).astype(BF)
        summed = dot(
            back_ref[: span * OWN, : orders * EDGE], jnp.concatenate(stacked, axis=0)
        )
        for j in range(span):
            lo = (degree * degree + j) * C
            sums_ref[:, lo : lo + C] = summed[j * OWN : (j + 1) * OWN]
    for k, out_ref in enumerate((o0_ref, o1_ref, o2_ref, o3_ref)):
        start = pl.multiple_of((rep ^ k) * 8, 8)
        out_ref[...] = sums_ref[pl.ds(start, 8), :].astype(out_ref.dtype)


def finish_body(own_ref, s0_ref, s1_ref, s2_ref, s3_ref, out_ref):
    total = (s0_ref[...] + s1_ref[...].astype(F32)) + (
        s2_ref[...].astype(F32) + s3_ref[...].astype(F32)
    )
    out_ref[...] = (own_ref[...].astype(F32) + total * (1.0 / math.sqrt(DEG))).astype(BF)


def call(body, outs, ins, scratch=(), scalars=0):
    return pl.pallas_call(
        body,
        out_shape=tuple(jax.ShapeDtypeStruct(shape, dtype) for shape, dtype in outs),
        in_specs=[SMEM] * scalars + [VMEM] * (len(ins) - scalars),
        out_specs=tuple(VMEM for _ in outs),
        scratch_shapes=list(scratch),
        compiler_params=PARAMS,
    )(*ins)


def shifted(x, axes, by):
    length = lax.axis_size(axes)
    return lax.ppermute(x, axes, [(i, (i + by) % length) for i in range(length)])


def swapped(x, axes, mask):
    return lax.ppermute(x, axes, [(i, i ^ mask) for i in range(lax.axis_size(axes))])


def exchange(x, axes):
    return lax.all_to_all(x, axes, 0, 0, tiled=True)


def per_device(
    teacher_in, student_in, wigner, edge_basis, teacher_radial, so2_m0, so2_m1, so2_m2,
    w_src, w_dst, w_radial, w_out, w_head, src, dst, edge_count, atom_count, send_idx,
):
    bricks = lax.axis_size(BRICK)
    plane = lax.axis_size(PLANE)
    line = lax.axis_size("z")
    rep = lax.axis_index(REP).astype(jnp.int32)
    rep1 = rep.reshape(1)
    lists = send_idx.reshape(32, 1)
    to_next, to_prev = call(
        send_body, [((16, KC + SW), BF)] * 2, (lists, teacher_in, student_in)
    )
    from_left = shifted(to_next, BRICK, 1)
    from_right = shifted(to_prev, BRICK, -1)
    own, low, high = call(
        pack_body,
        [((LOW + HIGH, C), BF), ((LOW, C), BF), ((HIGH, C), BF)],
        (so2_m0, so2_m1, so2_m2),
    )
    column = exchange(jnp.broadcast_to(so2_m0[None, :, :C], (4, 224, C)), REP)
    near = swapped(own, "core", 1)
    across_low = shifted(low, ("yh", "yl"), 1)
    across_high = shifted(high, ("yh", "yl"), -1)
    far_low = swapped(across_low, "core", 1)
    far_high = swapped(across_high, "core", 1)
    src_row = src.reshape(1, EDGE)
    dst_row = dst.reshape(1, EDGE)
    pack, small, hidden, ssrc, sdst = call(
        front_body,
        [
            ((4, 928, EDGE), BF), ((4, OWN, C + SW), F32), ((EDGE, SW), F32),
            ((EDGE, SW), BF), ((EDGE, SW), BF),
        ],
        (
            edge_count, teacher_in, from_left, from_right, student_in, wigner, edge_basis,
            teacher_radial, src_row, dst_row, column, w_src, w_dst, w_radial,
        ),
        [pltpu.VMEM((235, EDGE), F32), pltpu.VMEM((13 * EXT, 5 * EDGE), BF)],
        1,
    )
    smalls = exchange(small, REP)
    (grads,) = call(
        functools.partial(student_body, 1.0 / (OWN * bricks)),
        [((plane, 1024 // plane, SW), BF)],
        (
            edge_count, atom_count, rep1, smalls, teacher_in[:, :C], student_in, w_out, w_head,
            hidden, ssrc, sdst, edge_basis, dst_row,
        ),
        (),
        3,
    )
    plane_parts = exchange(grads, PLANE)
    (plane_sum,) = call(spread_body, [((line, 1024 // plane, SW), BF)], (plane_parts,))
    shares = call(
        mix_body,
        [((8, KC), F32)] + [((8, KC), BF)] * 3,
        (
            edge_count, rep1, pack, own, near, across_low, across_high, far_low, far_high,
            wigner, dst_row,
        ),
        [
            pltpu.VMEM((235, EDGE), F32),
            pltpu.VMEM((13 * OWN, 5 * EDGE), BF),
            pltpu.VMEM((OWN, KC), F32),
        ],
        2,
    )
    arrived = [shares[0]] + [swapped(shares[k], REP, k) for k in (1, 2, 3)]
    line_parts = exchange(plane_sum, "z")
    (total,) = call(spread_body, [((plane, 1024 // plane, SW), BF)], (line_parts,))
    totals = exchange(total, PLANE)
    grads_out = call(
        unpack_body,
        [((256, SW), F32), ((256, SW), F32), ((128, SW), F32), ((256, SW), F32), ((256, C), F32)],
        (totals,),
    )
    mine = lax.dynamic_slice_in_dim(teacher_in, rep * 8, 8, 0)
    (teacher_out,) = call(finish_body, [((8, KC), BF)], (mine, *arrived))
    return (teacher_out, *grads_out)


def solution(mesh):
    fine = Mesh(mesh.devices.reshape(16, 4, 2, 2, 2), BRICK + REP)
    every = BRICK + REP
    placed = (
        P(BRICK, None),
        P(BRICK, None),
        P(None, every),
        P(every, None),
        P(),
        P(REP, None),
        P(None, REP, None),
        P(None, REP, None),
        P(),
        P(),
        P(),
        P(),
        P(),
        P(every),
        P(every),
        P(every),
        P(BRICK),
        P(BRICK, None, None),
    )
    return jax.shard_map(
        per_device,
        mesh=fine,
        in_specs=placed,
        out_specs=(P(every, None), P(), P(), P(), P(), P()),
        check_vma=False,
    )
```

time: 728 us -> 129 us (0.18)
  waiting for transfers between devices: 547 us -> 27.8 us
  local copies, waits for them, and re-layouts: 88.3 us -> 14.1 us
  starting transfers between devices: 29.9 us -> 67 us
  matrix products: 27.1 us -> 0 us
  Pallas kernels: 0 us -> 15.9 us
  between operations: 16 us -> 2.2 us
  blocking collectives: 10.3 us -> 0 us
  other arithmetic: 7.67 us -> 0 us
    psum x2 -> x0, waiting for transfers between devices: 515 us -> none  [the longest x1 470 us: per_device(): lax.psum((grad_src, grad_dst, grad_radial, grad_out, grad_head), ('brick'...]
    concatenate x4 -> x0, local copies, waits for them, and re-layouts: 30.9 us -> none  [the longest x2 29.8 us: rotate_back(): message = jnp.concatenate(pieces, axis=1) * edge_mask[:, None, None]]
    all_gather x3 -> x0, waiting for transfers between devices: 30.5 us -> none  [the longest x1 30.5 us: per_device(): lax.all_gather(so2_m1, 'rep', axis=1, tiled=True)]
    dot_general x30 -> x0, matrix products: 27.1 us -> none  [the longest x6 6.14 us: rotate_into(): jnp.einsum('mje,ejc->emc', blocks[degree], coeffs, preferred_element_type...]
    all_to_all x0 -> x5, starting transfers between devices: none -> 25.9 us  [exchange(): return lax.all_to_all(x, axes, 0, 0, tiled=True)]
    all_to_all x0 -> x5, waiting for transfers between devices: none -> 18.8 us  [exchange(): return lax.all_to_all(x, axes, 0, 0, tiled=True)]
    pallas_call x0 -> x9, Pallas kernels: none -> 15.9 us  [call(): pl.pallas_call(body, out_shape=tuple((jax.ShapeDtypeStruct(shape, dtype)...]
    gather x9 -> x0, local copies, waits for them, and re-layouts: 11.7 us -> none  [the longest x2 5.87 us: per_device(): vectors = rotate_into(jnp.take(teacher_ext, src, axis=0), blocks, edge_gain)]
  transfers between devices with their start and end apart: 9 -> 15, of which waited for: 3 -> 6; matrix products, arithmetic and copies ran while one was open for 8% -> 1% of each run, Pallas kernels for 0% -> 8%
where the time goes in v1:
time: 129 us; the launch traced here: 127 us
  starting transfers between devices  67 us (52%)
  waiting for transfers between devices  27.8 us (22%)
  Pallas kernels  15.9 us (12%)
  local copies, waits for them, and re-layouts  14.1 us (11%)
  between operations  2.2 us (2%)
    all_to_all x5, starting transfers between devices, exchange(): return lax.all_to_all(x, axes, 0, 0, tiled=True)  25.9 us
    ppermute x4, starting transfers between devices, shifted(): lax.ppermute(x, axes, [(i, (i + by) % length) for i in range(length)])  25.3 us
    all_to_all x5, waiting for transfers between devices, exchange(): return lax.all_to_all(x, axes, 0, 0, tiled=True)  18.8 us
    pallas_call x9, Pallas kernels, call(): pl.pallas_call(body, out_shape=tuple((jax.ShapeDtypeStruct(shape, dtype)...  15.9 us
    ppermute x6, starting transfers between devices, swapped(): lax.ppermute(x, axes, [(i, i ^ mask) for i in range(lax.axis_size(axes))])  15.8 us
    unnamed x40, local copies, waits for them, and re-layouts  11.8 us
    ppermute x4, waiting for transfers between devices, shifted(): lax.ppermute(x, axes, [(i, (i + by) % length) for i in range(length)])  6.84 us
  transfers between devices with their start and end apart: 15, of which 6 were waited for; matrix products, arithmetic and copies ran while one was open for 1% of the time, Pallas kernels for 8%

profile of v1, /device:TPU:1, one launch (start us, length us, event | category | flops | bytes accessed | tf_op | source)
XLA Modules:
  0.0 127.0 jit_solution(12944029734741696763)
XLA Ops:
  1.4 1.0 copy-done
  3.4 5.7 %collective-permute-start = (bf16[16,6528]{1,0:T(8,128)(2,1)S(1)}, bf16[16,6528]{1,0:T(8,128)(2,1)S(1)}, u32[]{:S(2)}, u32[]{:S(2)}) collective-permute-start(bf16[16,6528]{1,0:T(8,128)(2,1)S(1)} %get-tuple-element.25), channel_id=1, source_target_pairs={{0,4},{4,8},{8,12},{12,16},{16,20},{20,24},{24,28},{28,32},{32,36}... | collective-permute-start | bytes 626696 | tf_op jit(solution)/shard_map/ppermute | solution.py:313
  9.1 13.2 %collective-permute-start.1 = (bf16[16,6528]{1,0:T(8,128)(2,1)S(1)}, bf16[16,6528]{1,0:T(8,128)(2,1)S(1)}, u32[]{:S(2)}, u32[]{:S(2)}) collective-permute-start(bf16[16,6528]{1,0:T(8,128)(2,1)S(1)} %get-tuple-element.26), channel_id=1, source_target_pairs={{0,508},{4,0},{8,4},{12,8},{16,12},{20,16},{24,20},{28,24},{32,28}... | collective-permute-start | bytes 626696 | tf_op jit(solution)/shard_map/ppermute | solution.py:313
  23.9 4.3 %all-to-all-start = ((bf16[4,224,128]{2,1,0:T(8,128)(2,1)}), bf16[4,224,128]{2,1,0:T(8,128)(2,1)S(1)}, u32[]{:S(2)}, u32[]{:S(2)}) async-start(bf16[4,224,128]{2,1,0:T(8,128)(2,1)} %broadcast_in_dim.2), calls=%async_computation | async-start | bytes 458752 | tf_op jit(solution)/shard_map/all_to_all | solution.py:321
  28.8 4.2 %all-to-all-done.m0_ref = bf16[4,224,128]{2,1,0:T(8,128)(2,1)S(1)} async-done(((bf16[4,224,128]{2,1,0:T(8,128)(2,1)}), bf16[4,224,128]{2,1,0:T(8,128)(2,1)S(1)}, u32[]{:S(2)}, u32[]{:S(2)}) %all-to-all-start) | async-done | bytes 229408 | tf_op jit(solution)/shard_map/all_to_all | solution.py:321
  34.6 0.9 copy-done.9
  35.5 0.9 copy-done.10
  40.1 2.5 %shard_map.218 = (bf16[4,928,128]{2,1,0:T(8,128)(2,1)S(1)}, f32[4,32,384]{2,1,0:T(8,128)}, f32[128,256]{1,0:T(8,128)S(1)}, bf16[128,256]{1,0:T(8,128)(2,1)S(1)}, bf16[128,256]{1,0:T(8,128)(2,1)S(1)}) custom-call(s32[1]{0:T(128)S(6)} %copy.25.count_ref, bf16[32,6272]{1,0:T(8,128)(2,1)S(1)} %copy-done.1, bf16[16,6528]{1,0:T(8,128)(2,1)S(1)} %collective-permute-done.left_ref, ...), custom_call_target="tpu_custom_call" | custom-call | tf_op jit(solution)/shard_map/pallas_call | solution.py:301
  42.6 4.2 %all-to-all-start.1 = ((f32[4,32,384]{2,1,0:T(8,128)}), f32[4,32,384]{2,1,0:T(8,128)S(1)}, u32[]{:S(2)}, u32[]{:S(2)}) async-start(f32[4,32,384]{2,1,0:T(8,128)} %get-tuple-element.35), calls=%async_computation.1 | async-start | bytes 393216 | tf_op jit(solution)/shard_map/all_to_all | solution.py:321
  47.4 3.8 %all-to-all-done.1.smalls_ref = f32[4,32,384]{2,1,0:T(8,128)S(1)} async-done(((f32[4,32,384]{2,1,0:T(8,128)}), f32[4,32,384]{2,1,0:T(8,128)S(1)}, u32[]{:S(2)}, u32[]{:S(2)}) %all-to-all-start.1) | async-done | bytes 196640 | tf_op jit(solution)/shard_map/all_to_all | solution.py:321
  51.3 1.7 %shard_map.222 = bf16[32,32,256]{2,1,0:T(8,128)(2,1)} custom-call(s32[1]{0:T(128)S(6)} %copy.25.count_ref, s32[1]{0:T(128)S(6)} %copy.26.atoms_ref, s32[1]{0:T(128)} %bitcast.rep_ref, f32[4,32,384]{2,1,0:T(8,128)S(1)} %all-to-all-done.1.smalls_ref, bf16[32,128]{1,0:T(8,128)(2,1)S(1)} %slice.7.teacher_ref, bf16[32,256]{1,0:T(8,128)(2,1)S(1)} %copy-done.8, ...), custom_call_target="tpu_custom_call" | custom-call | tf_op jit(solution)/shard_map/pallas_call | solution.py:301
  53.0 4.4 %all-to-all-start.2 = ((bf16[32,32,256]{2,1,0:T(8,128)(2,1)}), bf16[32,32,256]{2,1,0:T(8,128)(2,1)S(1)}, u32[]{:S(2)}, u32[]{:S(2)}) async-start(bf16[32,32,256]{2,1,0:T(8,128)(2,1)} %shard_map.222), calls=%async_computation.2 | async-start | bytes 1048576 | tf_op jit(solution)/shard_map/all_to_all | solution.py:321
  57.4 1.1 copy-done.2
  58.4 1.0 copy-done.3
  59.4 1.0 copy-done.4
  60.4 1.5 %shard_map.219 = (bf16[5472,128]{1,0:T(8,128)(2,1)S(1)}, bf16[2720,128]{1,0:T(8,128)(2,1)}, bf16[2752,128]{1,0:T(8,128)(2,1)}) custom-call(bf16[224,896]{1,0:T(8,128)(2,1)S(1)} %copy-done.3, bf16[2,192,768]{2,1,0:T(8,128)(2,1)S(1)} %copy-done.2, bf16[2,160,640]{2,1,0:T(8,128)(2,1)S(1)} %copy-done.4), custom_call_target="tpu_custom_call" | custom-call | tf_op jit(solution)/shard_map/pallas_call | solution.py:301
  61.9 4.5 %collective-permute-start.4 = (bf16[2752,128]{1,0:T(8,128)(2,1)}, bf16[2752,128]{1,0:T(8,128)(2,1)}, u32[]{:S(2)}, u32[]{:S(2)}) collective-permute-start(bf16[2752,128]{1,0:T(8,128)(2,1)} %get-tuple-element.30), channel_id=1, source_target_pairs={{0,6},{2,0},{4,2},{6,4},{1,7},{3,1},{5,3},{7,5},{8,14},{10,8},{12,... | collective-permute-start | bytes 2113544 | tf_op jit(solution)/shard_map/ppermute | solution.py:313
  66.4 2.6 %collective-permute-start.2 = (bf16[5472,128]{1,0:T(8,128)(2,1)S(1)}, bf16[5472,128]{1,0:T(8,128)(2,1)}, u32[]{:S(2)}, u32[]{:S(2)}) collective-permute-start(bf16[5472,128]{1,0:T(8,128)(2,1)S(1)} %get-tuple-element.28.own_ref), channel_id=1, source_target_pairs={{0,1},{1,0},{2,3},{3,2},{4,5},{5,4},{6,7},{7,6},{8,9},{9,8},{10,11... | collective-permute-start | bytes 4202504 | tf_op jit(solution)/shard_map/ppermute | solution.py:317
  69.0 1.9 %collective-permute-start.3 = (bf16[2720,128]{1,0:T(8,128)(2,1)}, bf16[2720,128]{1,0:T(8,128)(2,1)}, u32[]{:S(2)}, u32[]{:S(2)}) collective-permute-start(bf16[2720,128]{1,0:T(8,128)(2,1)} %get-tuple-element.29), channel_id=1, source_target_pairs={{0,2},{2,4},{4,6},{6,0},{1,3},{3,5},{5,7},{7,1},{8,10},{10,12},{12... | collective-permute-start | bytes 2088968 | tf_op jit(solution)/shard_map/ppermute | solution.py:313
  71.7 8.3 %all-to-all-start.3 = ((bf16[16,32,256]{2,1,0:T(8,128)(2,1)}), bf16[16,32,256]{2,1,0:T(8,128)(2,1)S(1)}, u32[]{:S(2)}, u32[]{:S(2)}) async-start(bf16[16,32,256]{2,1,0:T(8,128)(2,1)} %shard_map.223), calls=%async_computation.3 | async-start | bytes 524288 | tf_op jit(solution)/shard_map/all_to_all | solution.py:321
  80.1 1.9 %collective-permute-done.4.high_ref = bf16[2752,128]{1,0:T(8,128)(2,1)} collective-permute-done((bf16[2752,128]{1,0:T(8,128)(2,1)}, bf16[2752,128]{1,0:T(8,128)(2,1)}, u32[]{:S(2)}, u32[]{:S(2)}) %collective-permute-start.4) | collective-permute-done | bytes 704544 | tf_op jit(solution)/shard_map/ppermute | solution.py:313
  82.0 2.7 %collective-permute-start.6 = (bf16[2752,128]{1,0:T(8,128)(2,1)}, bf16[2752,128]{1,0:T(8,128)(2,1)}, u32[]{:S(2)}, u32[]{:S(2)}) collective-permute-start(bf16[2752,128]{1,0:T(8,128)(2,1)} %collective-permute-done.4.high_ref), channel_id=1, source_target_pairs={{0,1},{1,0},{2,3},{3,2},{4,5},{5,4},{6,7},{7,6},{8,9},{9,8},{10,11... | collective-permute-start | bytes 2113544 | tf_op jit(solution)/shard_map/ppermute | solution.py:317
  84.7 4.9 %collective-permute-done.3.low_ref = bf16[2720,128]{1,0:T(8,128)(2,1)} collective-permute-done((bf16[2720,128]{1,0:T(8,128)(2,1)}, bf16[2720,128]{1,0:T(8,128)(2,1)}, u32[]{:S(2)}, u32[]{:S(2)}) %collective-permute-start.3) | collective-permute-done | bytes 696352 | tf_op jit(solution)/shard_map/ppermute | solution.py:313
  89.7 2.7 %collective-permute-start.5 = (bf16[2720,128]{1,0:T(8,128)(2,1)}, bf16[2720,128]{1,0:T(8,128)(2,1)}, u32[]{:S(2)}, u32[]{:S(2)}) collective-permute-start(bf16[2720,128]{1,0:T(8,128)(2,1)} %collective-permute-done.3.low_ref), channel_id=1, source_target_pairs={{0,1},{1,0},{2,3},{3,2},{4,5},{5,4},{6,7},{7,6},{8,9},{9,8},{10,11... | collective-permute-start | bytes 2088968 | tf_op jit(solution)/shard_map/ppermute | solution.py:317
  92.4 2.1 %collective-permute-done.5.far_low_ref = bf16[2720,128]{1,0:T(8,128)(2,1)} collective-permute-done((bf16[2720,128]{1,0:T(8,128)(2,1)}, bf16[2720,128]{1,0:T(8,128)(2,1)}, u32[]{:S(2)}, u32[]{:S(2)}) %collective-permute-start.5) | collective-permute-done | bytes 696352 | tf_op jit(solution)/shard_map/ppermute | solution.py:317
  94.5 6.5 %shard_map.220 = (f32[8,6272]{1,0:T(8,128)S(1)}, bf16[8,6272]{1,0:T(8,128)(2,1)}, bf16[8,6272]{1,0:T(8,128)(2,1)}, bf16[8,6272]{1,0:T(8,128)(2,1)}) custom-call(s32[1]{0:T(128)S(6)} %copy.25.count_ref, s32[1]{0:T(128)} %bitcast.rep_ref, bf16[4,928,128]{2,1,0:T(8,128)(2,1)S(1)} %get-tuple-element.27.pack_ref, ...), custom_call_target="tpu_custom_call" | custom-call | tf_op jit(solution)/shard_map/pallas_call | solution.py:301
  101.0 2.3 %collective-permute-start.7 = (bf16[8,6272]{1,0:T(8,128)(2,1)}, bf16[8,6272]{1,0:T(8,128)(2,1)S(1)}, u32[]{:S(2)}, u32[]{:S(2)}) collective-permute-start(bf16[8,6272]{1,0:T(8,128)(2,1)} %get-tuple-element.32), channel_id=1, source_target_pairs={{0,1},{1,0},{2,3},{3,2},{4,5},{5,4},{6,7},{7,6},{8,9},{9,8},{10,11... | collective-permute-start | bytes 301064 | tf_op jit(solution)/shard_map/ppermute | solution.py:317
  103.3 1.9 %collective-permute-start.8 = (bf16[8,6272]{1,0:T(8,128)(2,1)}, bf16[8,6272]{1,0:T(8,128)(2,1)S(1)}, u32[]{:S(2)}, u32[]{:S(2)}) collective-permute-start(bf16[8,6272]{1,0:T(8,128)(2,1)} %get-tuple-element.33), channel_id=1, source_target_pairs={{0,2},{1,3},{2,0},{3,1},{4,6},{5,7},{6,4},{7,5},{8,10},{9,11},{10,... | collective-permute-start | bytes 301064 | tf_op jit(solution)/shard_map/ppermute | solution.py:317
  105.2 3.7 %collective-permute-start.9 = (bf16[8,6272]{1,0:T(8,128)(2,1)}, bf16[8,6272]{1,0:T(8,128)(2,1)S(1)}, u32[]{:S(2)}, u32[]{:S(2)}) collective-permute-start(bf16[8,6272]{1,0:T(8,128)(2,1)} %get-tuple-element.34), channel_id=1, source_target_pairs={{0,3},{1,2},{2,1},{3,0},{4,7},{5,6},{6,5},{7,4},{8,11},{9,10},{10,... | collective-permute-start | bytes 301064 | tf_op jit(solution)/shard_map/ppermute | solution.py:317
  109.8 4.6 %all-to-all-start.4 = ((bf16[32,32,256]{2,1,0:T(8,128)(2,1)}), bf16[32,32,256]{2,1,0:T(8,128)(2,1)S(1)}, u32[]{:S(2)}, u32[]{:S(2)}) async-start(bf16[32,32,256]{2,1,0:T(8,128)(2,1)} %shard_map.224), calls=%async_computation.4 | async-start | bytes 1048576 | tf_op jit(solution)/shard_map/all_to_all | solution.py:321
  115.2 10.8 %all-to-all-done.4.all_ref = bf16[32,32,256]{2,1,0:T(8,128)(2,1)S(1)} async-done(((bf16[32,32,256]{2,1,0:T(8,128)(2,1)}), bf16[32,32,256]{2,1,0:T(8,128)(2,1)S(1)}, u32[]{:S(2)}, u32[]{:S(2)}) %all-to-all-start.4) | async-done | bytes 524320 | tf_op jit(solution)/shard_map/all_to_all | solution.py:321
  126.0 1.0 shard_map.225
  (52 shorter events, 11.0 us)
Async XLA Ops:
  1.4 1.0 copy-start
  2.4 0.7 copy-start.7
  3.1 29.9 %copy-start.1 = (bf16[32,6272]{1,0:T(8,128)(2,1)S(1)}, bf16[32,6272]{1,0:T(8,128)(2,1)}, u32[]{:S(2)}) copy-start(bf16[32,6272]{1,0:T(8,128)(2,1)} %teacher_ref.3) | copy-start | bytes 1204228
  3.4 29.6 %collective-permute-start = (bf16[16,6528]{1,0:T(8,128)(2,1)S(1)}, bf16[16,6528]{1,0:T(8,128)(2,1)S(1)}, u32[]{:S(2)}, u32[]{:S(2)}) collective-permute-start(bf16[16,6528]{1,0:T(8,128)(2,1)S(1)} %get-tuple-element.25), channel_id=1, source_target_pairs={{0,4},{4,8},{8,12},{12,16},{16,20},{20,24},{24,28},{28,32},{32,36}... | collective-permute-start | bytes 626696 | tf_op jit(solution)/shard_map/ppermute | solution.py:313
  9.1 42.1 %copy-start.11 = (bf16[256,256]{1,0:T(8,128)(2,1)S(1)}, bf16[256,256]{1,0:T(8,128)(2,1)}, u32[]{:S(2)}) copy-start(bf16[256,256]{1,0:T(8,128)(2,1)} %wout_ref.1) | copy-start | bytes 393220
  9.1 42.1 %copy-start.13 = (bf16[128,128]{1,0:T(8,128)(2,1)S(1)}, bf16[128,128]{1,0:T(8,128)(2,1)}, u32[]{:S(2)}) copy-start(bf16[128,128]{1,0:T(8,128)(2,1)} %basis_ref.3) | copy-start | bytes 98308
  9.1 42.1 %copy-start.15 = (bf16[256,128]{1,0:T(8,128)(2,1)S(1)}, bf16[256,128]{1,0:T(8,128)(2,1)}, u32[]{:S(2)}) copy-start(bf16[256,128]{1,0:T(8,128)(2,1)} %whead_ref.1) | copy-start | bytes 196612
  9.1 42.1 %copy-start.18 = (s32[128]{0:T(128)S(1)}, s32[128]{0:T(128)}, u32[]{:S(2)}) copy-start(s32[128]{0:T(128)} %param.32) | copy-start | bytes 1540
  9.1 23.9 %collective-permute-start.1 = (bf16[16,6528]{1,0:T(8,128)(2,1)S(1)}, bf16[16,6528]{1,0:T(8,128)(2,1)S(1)}, u32[]{:S(2)}, u32[]{:S(2)}) collective-permute-start(bf16[16,6528]{1,0:T(8,128)(2,1)S(1)} %get-tuple-element.26), channel_id=1, source_target_pairs={{0,508},{4,0},{8,4},{12,8},{16,12},{20,16},{24,20},{28,24},{32,28}... | collective-permute-start | bytes 626696 | tf_op jit(solution)/shard_map/ppermute | solution.py:313
  23.9 9.1 %all-to-all-start = ((bf16[4,224,128]{2,1,0:T(8,128)(2,1)}), bf16[4,224,128]{2,1,0:T(8,128)(2,1)S(1)}, u32[]{:S(2)}, u32[]{:S(2)}) async-start(bf16[4,224,128]{2,1,0:T(8,128)(2,1)} %broadcast_in_dim.2), calls=%async_computation | async-start | bytes 458752 | tf_op jit(solution)/shard_map/all_to_all | solution.py:321
  33.0 0.8 copy-start.5
  34.6 0.9 copy-start.9
  35.5 0.9 copy-start.10
  36.4 0.8 copy-start.12
  37.1 0.8 copy-start.14
  38.0 0.8 copy-start.16
  42.6 8.7 %all-to-all-start.1 = ((f32[4,32,384]{2,1,0:T(8,128)}), f32[4,32,384]{2,1,0:T(8,128)S(1)}, u32[]{:S(2)}, u32[]{:S(2)}) async-start(f32[4,32,384]{2,1,0:T(8,128)} %get-tuple-element.35), calls=%async_computation.1 | async-start | bytes 393216 | tf_op jit(solution)/shard_map/all_to_all | solution.py:321
  53.0 18.0 %all-to-all-start.2 = ((bf16[32,32,256]{2,1,0:T(8,128)(2,1)}), bf16[32,32,256]{2,1,0:T(8,128)(2,1)S(1)}, u32[]{:S(2)}, u32[]{:S(2)}) async-start(bf16[32,32,256]{2,1,0:T(8,128)(2,1)} %shard_map.222), calls=%async_computation.2 | async-start | bytes 1048576 | tf_op jit(solution)/shard_map/all_to_all | solution.py:321
  57.4 1.1 copy-start.2
  58.4 1.0 copy-start.3
  59.4 1.0 copy-start.4
  60.4 34.0 %copy-start.6 = (bf16[235,128]{1,0:T(8,128)(2,1)S(1)}, bf16[235,128]{1,0:T(8,128)(2,1)}, u32[]{:S(2)}) copy-start(bf16[235,128]{1,0:T(8,128)(2,1)} %wig_ref.3) | copy-start | bytes 180484
  61.9 20.1 %collective-permute-start.4 = (bf16[2752,128]{1,0:T(8,128)(2,1)}, bf16[2752,128]{1,0:T(8,128)(2,1)}, u32[]{:S(2)}, u32[]{:S(2)}) collective-permute-start(bf16[2752,128]{1,0:T(8,128)(2,1)} %get-tuple-element.30), channel_id=1, source_target_pairs={{0,6},{2,0},{4,2},{6,4},{1,7},{3,1},{5,3},{7,5},{8,14},{10,8},{12,... | collective-permute-start | bytes 2113544 | tf_op jit(solution)/shard_map/ppermute | solution.py:313
  66.4 28.0 %collective-permute-start.2 = (bf16[5472,128]{1,0:T(8,128)(2,1)S(1)}, bf16[5472,128]{1,0:T(8,128)(2,1)}, u32[]{:S(2)}, u32[]{:S(2)}) collective-permute-start(bf16[5472,128]{1,0:T(8,128)(2,1)S(1)} %get-tuple-element.28.own_ref), channel_id=1, source_target_pairs={{0,1},{1,0},{2,3},{3,2},{4,5},{5,4},{6,7},{7,6},{8,9},{9,8},{10,11... | collective-permute-start | bytes 4202504 | tf_op jit(solution)/shard_map/ppermute | solution.py:317
  69.0 20.7 %collective-permute-start.3 = (bf16[2720,128]{1,0:T(8,128)(2,1)}, bf16[2720,128]{1,0:T(8,128)(2,1)}, u32[]{:S(2)}, u32[]{:S(2)}) collective-permute-start(bf16[2720,128]{1,0:T(8,128)(2,1)} %get-tuple-element.29), channel_id=1, source_target_pairs={{0,2},{2,4},{4,6},{6,0},{1,3},{3,5},{5,7},{7,1},{8,10},{10,12},{12... | collective-permute-start | bytes 2088968 | tf_op jit(solution)/shard_map/ppermute | solution.py:313
  71.7 37.2 %all-to-all-start.3 = ((bf16[16,32,256]{2,1,0:T(8,128)(2,1)}), bf16[16,32,256]{2,1,0:T(8,128)(2,1)S(1)}, u32[]{:S(2)}, u32[]{:S(2)}) async-start(bf16[16,32,256]{2,1,0:T(8,128)(2,1)} %shard_map.223), calls=%async_computation.3 | async-start | bytes 524288 | tf_op jit(solution)/shard_map/all_to_all | solution.py:321
  82.0 12.5 %collective-permute-start.6 = (bf16[2752,128]{1,0:T(8,128)(2,1)}, bf16[2752,128]{1,0:T(8,128)(2,1)}, u32[]{:S(2)}, u32[]{:S(2)}) collective-permute-start(bf16[2752,128]{1,0:T(8,128)(2,1)} %collective-permute-done.4.high_ref), channel_id=1, source_target_pairs={{0,1},{1,0},{2,3},{3,2},{4,5},{5,4},{6,7},{7,6},{8,9},{9,8},{10,11... | collective-permute-start | bytes 2113544 | tf_op jit(solution)/shard_map/ppermute | solution.py:317
  89.7 4.8 %collective-permute-start.5 = (bf16[2720,128]{1,0:T(8,128)(2,1)}, bf16[2720,128]{1,0:T(8,128)(2,1)}, u32[]{:S(2)}, u32[]{:S(2)}) collective-permute-start(bf16[2720,128]{1,0:T(8,128)(2,1)} %collective-permute-done.3.low_ref), channel_id=1, source_target_pairs={{0,1},{1,0},{2,3},{3,2},{4,5},{5,4},{6,7},{7,6},{8,9},{9,8},{10,11... | collective-permute-start | bytes 2088968 | tf_op jit(solution)/shard_map/ppermute | solution.py:317
  101.0 13.4 %collective-permute-start.7 = (bf16[8,6272]{1,0:T(8,128)(2,1)}, bf16[8,6272]{1,0:T(8,128)(2,1)S(1)}, u32[]{:S(2)}, u32[]{:S(2)}) collective-permute-start(bf16[8,6272]{1,0:T(8,128)(2,1)} %get-tuple-element.32), channel_id=1, source_target_pairs={{0,1},{1,0},{2,3},{3,2},{4,5},{5,4},{6,7},{7,6},{8,9},{9,8},{10,11... | collective-permute-start | bytes 301064 | tf_op jit(solution)/shard_map/ppermute | solution.py:317
  103.3 11.2 %collective-permute-start.8 = (bf16[8,6272]{1,0:T(8,128)(2,1)}, bf16[8,6272]{1,0:T(8,128)(2,1)S(1)}, u32[]{:S(2)}, u32[]{:S(2)}) collective-permute-start(bf16[8,6272]{1,0:T(8,128)(2,1)} %get-tuple-element.33), channel_id=1, source_target_pairs={{0,2},{1,3},{2,0},{3,1},{4,6},{5,7},{6,4},{7,5},{8,10},{9,11},{10,... | collective-permute-start | bytes 301064 | tf_op jit(solution)/shard_map/ppermute | solution.py:317
  105.2 9.3 %collective-permute-start.9 = (bf16[8,6272]{1,0:T(8,128)(2,1)}, bf16[8,6272]{1,0:T(8,128)(2,1)S(1)}, u32[]{:S(2)}, u32[]{:S(2)}) collective-permute-start(bf16[8,6272]{1,0:T(8,128)(2,1)} %get-tuple-element.34), channel_id=1, source_target_pairs={{0,3},{1,2},{2,1},{3,0},{4,7},{5,6},{6,5},{7,4},{8,11},{9,10},{10,... | collective-permute-start | bytes 301064 | tf_op jit(solution)/shard_map/ppermute | solution.py:317
  109.8 16.2 %all-to-all-start.4 = ((bf16[32,32,256]{2,1,0:T(8,128)(2,1)}), bf16[32,32,256]{2,1,0:T(8,128)(2,1)S(1)}, u32[]{:S(2)}, u32[]{:S(2)}) async-start(bf16[32,32,256]{2,1,0:T(8,128)(2,1)} %shard_map.224), calls=%async_computation.4 | async-start | bytes 1048576 | tf_op jit(solution)/shard_map/all_to_all | solution.py:321
  (3 other events, 2.0 us)

commit v2 on v1

--- a/solution.py
+++ b/solution.py
@@ -17,6 +17,8 @@
 EDGE = 128
 SW = 256
 KC = 6272
+FULL = 64 << 10
+FRONT = 1024
 LOW = 7 * 224 + 6 * 192
 HIGH = 6 * 192 + 10 * 160
 SECTIONS = {0: (224, 0), 1: (192, 224), -1: (192, 416), 2: (160, 608), -2: (160, 768)}
@@ -26,8 +28,9 @@
 REP = ("yl", "core")
 PLANE = ("x", "yh", "yl", "core")
 VMEM = pl.BlockSpec(memory_space=pltpu.VMEM)
+HBM = pl.BlockSpec(memory_space=pltpu.HBM)
+ANY = pl.BlockSpec(memory_space=pl.ANY)
 SMEM = pl.BlockSpec(memory_space=pltpu.SMEM)
-PARAMS = pltpu.CompilerParams(vmem_limit_bytes=48 * 1024 * 1024)
 
 
 def offsets():
@@ -58,23 +61,50 @@
     return lax.broadcasted_iota(jnp.int32, (EDGE, 1), 0) < count
 
 
-def send_body(lists_ref, teacher_ref, student_ref, next_ref, prev_ref):
-    rows = lax.broadcasted_iota(jnp.int32, (32, OWN), 1)
-    pick = (lists_ref[...] == rows).astype(BF)
-    teacher = dot(pick, teacher_ref[...]).astype(BF)
-    student = dot(pick, student_ref[...]).astype(BF)
-    next_ref[:, :KC] = teacher[:16]
-    prev_ref[:, :KC] = teacher[16:]
-    next_ref[:, KC:] = student[:16]
-    prev_ref[:, KC:] = student[16:]
-
-
-def pack_body(m0_ref, m1_ref, m2_ref, all_ref, low_ref, high_ref):
+def fetch(pairs, sems):
+    copies = [
+        pltpu.make_async_copy(source, target, sems.at[i])
+        for i, (source, target) in enumerate(pairs)
+    ]
+    for copy in copies:
+        copy.start()
+    return copies
+
+
+def start_body(
+    lists_hbm, teacher_hbm, student_hbm, m0_hbm,
+    next_ref, prev_ref, column_ref,
+    lists_ref, teacher_ref, student_ref, m0_ref, sems,
+):
+    copies = fetch(
+        (
+            (lists_hbm, lists_ref), (teacher_hbm, teacher_ref), (student_hbm, student_ref),
+            (m0_hbm.at[:, :C], m0_ref),
+        ),
+        sems,
+    )
+    for copy in copies:
+        copy.wait()
+    rows = lax.broadcasted_iota(jnp.int32, (OWN, 16), 0)
+    for k, out_ref in enumerate((next_ref, prev_ref)):
+        pick = (rows == lists_ref[0, k : k + 1, :]).astype(F32).astype(BF)
+        out_ref[:, :KC] = dot(pick, teacher_ref[...], ((0,), (0,))).astype(BF)
+        out_ref[:, KC:] = dot(pick, student_ref[...], ((0,), (0,))).astype(BF)
+    for r in range(4):
+        column_ref[r] = m0_ref[...]
+
+
+def pack_body(
+    m0_hbm, m1_hbm, m2_hbm, all_ref, low_ref, high_ref, m0_ref, m1_ref, m2_ref, sems
+):
+    copies = fetch(((m0_hbm, m0_ref), (m1_hbm, m1_ref), (m2_hbm, m2_ref)), sems)
     at = 0
-    for part, wide, high in (
-        (m0_ref, 7, 224), (m1_ref.at[0], 6, 192), (m1_ref.at[1], 6, 192),
-        (m2_ref.at[0], 5, 160), (m2_ref.at[1], 5, 160),
+    for part, wide, high, ready in (
+        (m0_ref, 7, 224, 0), (m1_ref.at[0], 6, 192, 1), (m1_ref.at[1], 6, 192, None),
+        (m2_ref.at[0], 5, 160, 2), (m2_ref.at[1], 5, 160, None),
     ):
+        if ready is not None:
+            copies[ready].wait()
         for n in range(wide):
             block = part[:, n * C : (n + 1) * C]
             all_ref[at : at + high] = block
@@ -96,11 +126,18 @@
 
 
 def front_body(
-    count_ref, teacher_ref, left_ref, right_ref, student_ref, wig_ref, basis_ref, radial_ref,
-    src_ref, dst_ref, m0_ref, wsrc_ref, wdst_ref, wrad_ref,
-    pack_ref, small_ref, hidden_ref, ssrc_ref, sdst_ref,
-    wigf_ref, turn_ref,
+    count_ref, left_ref, right_ref, m0_ref, *refs
 ):
+    raw = refs[:10]
+    pack_ref, small_ref, hidden_ref, ssrc_ref, sdst_ref = refs[10:15]
+    held = refs[15:25]
+    wigf_ref, turn_ref, sems = refs[25:]
+    (
+        teacher_ref, student_ref, wig_ref, basis_ref, radial_ref, src_ref, dst_ref, wsrc_ref,
+        wdst_ref, wrad_ref,
+    ) = held
+    for copy in fetch(tuple(zip(raw, held)), sems):
+        copy.wait()
     count = count_ref[0]
     wigf_ref[...] = wig_ref[...].astype(F32)
     source = (src_ref[...] == lax.broadcasted_iota(jnp.int32, (EXT, EDGE), 0)).astype(F32)
@@ -133,11 +170,6 @@
             signed = morder - cap
             part, base = SECTIONS[signed]
             keep_turned(pack_ref, block, (degree - abs(signed)) * C, part, base)
-    invariant = dot(pack_ref[0, :224], m0_ref[0], ((0,), (0,)))
-    for r in range(1, 4):
-        invariant += dot(pack_ref[r, :224], m0_ref[r], ((0,), (0,)))
-    live = live_row(count)
-    scatter = jnp.where(target & live, wigf_ref[0:1, :], 0.0).astype(BF)
     student_ext = jnp.concatenate(
         [student_ref[...], left_ref[:, KC:], right_ref[:, KC:]], axis=0
     )
@@ -146,21 +178,32 @@
     sdst = dot(onehot, student_ref[...], ((0,), (0,))).astype(BF)
     hidden = dot(ssrc, wsrc_ref[...]) + dot(sdst, wdst_ref[...]) + dot(basis, wrad_ref[...])
     gated = jnp.where(live_col(count), hidden * jax.nn.sigmoid(hidden), 0.0).astype(BF)
-    small = jnp.concatenate(
-        [dot(scatter, invariant.astype(BF)), dot(onehot, gated)], axis=1
-    )
+    invariant = dot(pack_ref[0, :224], m0_ref[0], ((0,), (0,)))
+    for r in range(1, 4):
+        invariant += dot(pack_ref[r, :224], m0_ref[r], ((0,), (0,)))
+    keep = target & live_row(count)
+    scatter = jnp.where(keep, wigf_ref[0:1, :], 0.0).astype(BF)
+    sums = dot(scatter, invariant.astype(BF))
+    pooled = dot(onehot, gated)
     for r in range(4):
-        small_ref[r] = small
+        small_ref[r, :, :C] = sums
+        small_ref[r, :, C:] = pooled
     hidden_ref[...] = hidden
     ssrc_ref[...] = ssrc
     sdst_ref[...] = sdst
 
 
-def student_body(
-    inv_atoms, count_ref, atoms_ref, rep_ref, smalls_ref, teacher_ref,
-    student_ref, wout_ref, whead_ref, hidden_ref, ssrc_ref, sdst_ref, basis_ref, dst_ref,
-    grad_ref,
-):
+def student_body(inv_atoms, count_ref, atoms_ref, rep_ref, *refs):
+    raw = list(refs[:10])
+    raw[1] = raw[1].at[:, :C]
+    grad_ref = refs[10]
+    held = refs[11:21]
+    (
+        smalls_ref, teacher_ref, student_ref, wout_ref, whead_ref, hidden_ref, ssrc_ref,
+        sdst_ref, basis_ref, dst_ref,
+    ) = held
+    for copy in fetch(tuple(zip(raw, held)), refs[21]):
+        copy.wait()
     inv_degree = 1.0 / math.sqrt(DEG)
     sums = (smalls_ref[0] + smalls_ref[1]) + (smalls_ref[2] + smalls_ref[3])
     target = (teacher_ref[...].astype(F32) + inv_degree * sums[:, :C]).astype(BF)
@@ -195,7 +238,8 @@
         grad_ref[start // high : stop // high] = value.astype(BF).reshape(-1, high, SW)
 
 
-def spread_body(parts_ref, out_ref):
+def spread_body(parts_ref, *refs):
+    out_ref = refs[-1]
     total = parts_ref[0].astype(F32)
     for i in range(1, parts_ref.shape[0]):
         total += parts_ref[i].astype(F32)
@@ -222,7 +266,7 @@
 
 def mix_body(
     count_ref, rep_ref, pack_ref, own_ref, near_ref, low_ref, high_ref, far_low_ref, far_high_ref,
-    wig_ref, dst_ref,
+    wig_ref, dst_ref, after_ref,
     o0_ref, o1_ref, o2_ref, o3_ref,
     wigf_ref, back_ref, sums_ref,
 ):
@@ -297,15 +341,21 @@
     out_ref[...] = (own_ref[...].astype(F32) + total * (1.0 / math.sqrt(DEG))).astype(BF)
 
 
-def call(body, outs, ins, scratch=(), scalars=0):
+def call(body, outs, ins, scratch=(), scalars=0, raws=0, after=0, flops=0, room=24 << 10):
+    specs = [SMEM] * scalars + [VMEM] * (len(ins) - scalars - raws - after)
     return pl.pallas_call(
         body,
         out_shape=tuple(jax.ShapeDtypeStruct(shape, dtype) for shape, dtype in outs),
-        in_specs=[SMEM] * scalars + [VMEM] * (len(ins) - scalars),
+        in_specs=specs + [HBM] * raws + [ANY] * after,
         out_specs=tuple(VMEM for _ in outs),
         scratch_shapes=list(scratch),
-        compiler_params=PARAMS,
+        compiler_params=pltpu.CompilerParams(vmem_limit_bytes=(FULL - room) << 10),
+        cost_estimate=pl.CostEstimate(flops=flops, bytes_accessed=4096, transcendentals=0),
     )(*ins)
+
+
+def held(arrays):
+    return [pltpu.VMEM(array.shape, array.dtype) for array in arrays]
 
 
 def shifted(x, axes, by):
@@ -330,48 +380,72 @@
     line = lax.axis_size("z")
     rep = lax.axis_index(REP).astype(jnp.int32)
     rep1 = rep.reshape(1)
-    lists = send_idx.reshape(32, 1)
-    to_next, to_prev = call(
-        send_body, [((16, KC + SW), BF)] * 2, (lists, teacher_in, student_in)
+    src_row = src.reshape(1, EDGE)
+    dst_row = dst.reshape(1, EDGE)
+    to_next, to_prev, own_column = call(
+        start_body,
+        [((16, KC + SW), BF), ((16, KC + SW), BF), ((4, 224, C), BF)],
+        (send_idx, teacher_in, student_in, so2_m0),
+        held((send_idx, teacher_in, student_in))
+        + [pltpu.VMEM((224, C), BF), pltpu.SemaphoreType.DMA((4,))],
+        raws=4,
+        room=1024,
     )
     from_left = shifted(to_next, BRICK, 1)
     from_right = shifted(to_prev, BRICK, -1)
-    own, low, high = call(
-        pack_body,
-        [((LOW + HIGH, C), BF), ((LOW, C), BF), ((HIGH, C), BF)],
-        (so2_m0, so2_m1, so2_m2),
-    )
-    column = exchange(jnp.broadcast_to(so2_m0[None, :, :C], (4, 224, C)), REP)
-    near = swapped(own, "core", 1)
-    across_low = shifted(low, ("yh", "yl"), 1)
-    across_high = shifted(high, ("yh", "yl"), -1)
-    far_low = swapped(across_low, "core", 1)
-    far_high = swapped(across_high, "core", 1)
-    src_row = src.reshape(1, EDGE)
-    dst_row = dst.reshape(1, EDGE)
+    column = exchange(own_column, REP)
+    raw = (
+        teacher_in, student_in, wigner, edge_basis, teacher_radial, src_row, dst_row, w_src,
+        w_dst, w_radial,
+    )
     pack, small, hidden, ssrc, sdst = call(
         front_body,
         [
             ((4, 928, EDGE), BF), ((4, OWN, C + SW), F32), ((EDGE, SW), F32),
             ((EDGE, SW), BF), ((EDGE, SW), BF),
         ],
-        (
-            edge_count, teacher_in, from_left, from_right, student_in, wigner, edge_basis,
-            teacher_radial, src_row, dst_row, column, w_src, w_dst, w_radial,
-        ),
-        [pltpu.VMEM((235, EDGE), F32), pltpu.VMEM((13 * EXT, 5 * EDGE), BF)],
-        1,
+        (edge_count, from_left, from_right, column, *raw),
+        held(raw)
+        + [
+            pltpu.VMEM((235, EDGE), F32), pltpu.VMEM((13 * EXT, 5 * EDGE), BF),
+            pltpu.SemaphoreType.DMA((10,)),
+        ],
+        scalars=1,
+        raws=10,
+        flops=1 << 31,
+        room=FRONT,
     )
     smalls = exchange(small, REP)
+    mixings = (so2_m0, so2_m1, so2_m2)
+    own, low, high = call(
+        pack_body,
+        [((LOW + HIGH, C), BF), ((LOW, C), BF), ((HIGH, C), BF)],
+        mixings,
+        held(mixings) + [pltpu.SemaphoreType.DMA((3,))],
+        raws=3,
+        room=1024,
+        flops=1 << 30,
+    )
+    near = swapped(own, "core", 1)
+    across_low = shifted(low, ("yh", "yl"), 1)
+    across_high = shifted(high, ("yh", "yl"), -1)
+    far_low = swapped(across_low, "core", 1)
+    far_high = swapped(across_high, "core", 1)
+    raw = (
+        smalls, teacher_in, student_in, w_out, w_head, hidden, ssrc, sdst, edge_basis, dst_row,
+    )
     (grads,) = call(
         functools.partial(student_body, 1.0 / (OWN * bricks)),
         [((plane, 1024 // plane, SW), BF)],
-        (
-            edge_count, atom_count, rep1, smalls, teacher_in[:, :C], student_in, w_out, w_head,
-            hidden, ssrc, sdst, edge_basis, dst_row,
-        ),
-        (),
-        3,
+        (edge_count, atom_count, rep1, *raw),
+        held((smalls,))
+        + [pltpu.VMEM((OWN, C), BF)]
+        + held(raw[2:])
+        + [pltpu.SemaphoreType.DMA((10,))],
+        scalars=3,
+        raws=10,
+        flops=1 << 30,
+        room=1024,
     )
     plane_parts = exchange(grads, PLANE)
     (plane_sum,) = call(spread_body, [((line, 1024 // plane, SW), BF)], (plane_parts,))
@@ -380,26 +454,30 @@
         [((8, KC), F32)] + [((8, KC), BF)] * 3,
         (
             edge_count, rep1, pack, own, near, across_low, across_high, far_low, far_high,
-            wigner, dst_row,
+            wigner, dst_row, plane_sum,
         ),
         [
             pltpu.VMEM((235, EDGE), F32),
             pltpu.VMEM((13 * OWN, 5 * EDGE), BF),
             pltpu.VMEM((OWN, KC), F32),
         ],
-        2,
-    )
+        scalars=2,
+        after=1,
+        flops=1 << 32,
+    )
+    line_parts = exchange(plane_sum, "z")
+    (total,) = call(
+        spread_body, [((plane, 1024 // plane, SW), BF)], (line_parts, shares[0]), after=1
+    )
+    totals = exchange(total, PLANE)
     arrived = [shares[0]] + [swapped(shares[k], REP, k) for k in (1, 2, 3)]
-    line_parts = exchange(plane_sum, "z")
-    (total,) = call(spread_body, [((plane, 1024 // plane, SW), BF)], (line_parts,))
-    totals = exchange(total, PLANE)
+    mine = lax.dynamic_slice_in_dim(teacher_in, rep * 8, 8, 0)
+    (teacher_out,) = call(finish_body, [((8, KC), BF)], (mine, *arrived))
     grads_out = call(
         unpack_body,
         [((256, SW), F32), ((256, SW), F32), ((128, SW), F32), ((256, SW), F32), ((256, C), F32)],
         (totals,),
     )
-    mine = lax.dynamic_slice_in_dim(teacher_in, rep * 8, 8, 0)
-    (teacher_out,) = call(finish_body, [((8, KC), BF)], (mine, *arrived))
     return (teacher_out, *grads_out)
 
 

time: 129 us -> 119 us (0.922)
  local copies, waits for them, and re-layouts: 14.1 us -> 3.45 us
  Pallas kernels: 15.9 us -> 22 us
  waiting for transfers between devices: 27.8 us -> 22 us
    unnamed x40 -> x12, local copies, waits for them, and re-layouts: 11.8 us -> 2.54 us
    ppermute x4, waiting for transfers between devices: 6.84 us -> 0.01 us  [shifted(): lax.ppermute(x, axes, [(i, (i + by) % length) for i in range(length)])]
    pallas_call x9, Pallas kernels: 15.9 us -> 22 us  [call(): pl.pallas_call(body, out_shape=tuple((jax.ShapeDtypeStruct(shape, dtype)...]
    all_to_all x5, starting transfers between devices: 25.9 us -> 29.1 us  [exchange(): return lax.all_to_all(x, axes, 0, 0, tiled=True)]
    all_to_all x5, waiting for transfers between devices: 18.8 us -> 22 us  [exchange(): return lax.all_to_all(x, axes, 0, 0, tiled=True)]
    ppermute x6, waiting for transfers between devices: 2.12 us -> 0.02 us  [swapped(): lax.ppermute(x, axes, [(i, i ^ mask) for i in range(lax.axis_size(axes))])]
    ppermute x4, starting transfers between devices: 25.3 us -> 24 us  [shifted(): lax.ppermute(x, axes, [(i, (i + by) % length) for i in range(length)])]
  transfers between devices with their start and end apart: 15 -> 15, of which waited for: 6 -> 4; matrix products, arithmetic and copies ran while one was open for 1% -> 1% of each run, Pallas kernels for 8% -> 16%
where the time goes in v2:
time: 119 us; the launch traced here: 117 us
  starting transfers between devices  67.8 us (57%)
  Pallas kernels  22 us (18%)
  waiting for transfers between devices  22 us (18%)
  local copies, waits for them, and re-layouts  3.45 us (3%)
  between operations  2.23 us (2%)
    all_to_all x5, starting transfers between devices, exchange(): return lax.all_to_all(x, axes, 0, 0, tiled=True)  29.1 us
    ppermute x4, starting transfers between devices, shifted(): lax.ppermute(x, axes, [(i, (i + by) % length) for i in range(length)])  24 us
    all_to_all x5, waiting for transfers between devices, exchange(): return lax.all_to_all(x, axes, 0, 0, tiled=True)  22 us
    pallas_call x9, Pallas kernels, call(): pl.pallas_call(body, out_shape=tuple((jax.ShapeDtypeStruct(shape, dtype)...  22 us
    ppermute x6, starting transfers between devices, swapped(): lax.ppermute(x, axes, [(i, i ^ mask) for i in range(lax.axis_size(axes))])  14.7 us
    unnamed x12, local copies, waits for them, and re-layouts  2.54 us
  transfers between devices with their start and end apart: 15, of which 4 were waited for; matrix products, arithmetic and copies ran while one was open for 1% of the time, Pallas kernels for 16%

profile of v2, /device:TPU:1, one launch (start us, length us, event | category | flops | bytes accessed | tf_op | source)
XLA Modules:
  0.0 117.5 jit_solution(10007808475014100874)
XLA Ops:
  0.6 2.1 %shard_map.217 = (bf16[16,6528]{1,0:T(8,128)(2,1)}, bf16[16,6528]{1,0:T(8,128)(2,1)}, bf16[4,224,128]{2,1,0:T(8,128)(2,1)}) custom-call(s32[1,2,16]{2,1,0:T(2,128)} %lists_hbm.1, bf16[32,6272]{1,0:T(8,128)(2,1)} %refs_1_.3, bf16[32,256]{1,0:T(8,128)(2,1)} %refs_2_.3, bf16[224,896]{1,0:T(8,128)(2,1)} %m0_hbm.3), custom_call_target="tpu_custom_call" | custom-call | bytes 4096 | tf_op jit(solution)/shard_map/pallas_call | solution.py:346
  2.8 5.7 %collective-permute-start = (bf16[16,6528]{1,0:T(8,128)(2,1)}, bf16[16,6528]{1,0:T(8,128)(2,1)}, u32[]{:S(2)}, u32[]{:S(2)}) collective-permute-start(bf16[16,6528]{1,0:T(8,128)(2,1)} %get-tuple-element.26), channel_id=1, source_target_pairs={{0,4},{4,8},{8,12},{12,16},{16,20},{20,24},{24,28},{28,32},{32,36}... | collective-permute-start | bytes 626696 | tf_op jit(solution)/shard_map/ppermute | solution.py:363
  8.4 13.0 %collective-permute-start.1 = (bf16[16,6528]{1,0:T(8,128)(2,1)}, bf16[16,6528]{1,0:T(8,128)(2,1)}, u32[]{:S(2)}, u32[]{:S(2)}) collective-permute-start(bf16[16,6528]{1,0:T(8,128)(2,1)} %get-tuple-element.27), channel_id=1, source_target_pairs={{0,508},{4,0},{8,4},{12,8},{16,12},{20,16},{24,20},{28,24},{32,28}... | collective-permute-start | bytes 626696 | tf_op jit(solution)/shard_map/ppermute | solution.py:363
  21.5 4.3 %all-to-all-start = ((bf16[4,224,128]{2,1,0:T(8,128)(2,1)}), bf16[4,224,128]{2,1,0:T(8,128)(2,1)S(1)}, u32[]{:S(2)}, u32[]{:S(2)}) async-start(bf16[4,224,128]{2,1,0:T(8,128)(2,1)} %get-tuple-element.28), calls=%async_computation | async-start | bytes 458752 | tf_op jit(solution)/shard_map/all_to_all | solution.py:371
  25.8 2.9 %shard_map.219 = (bf16[5472,128]{1,0:T(8,128)(2,1)}, bf16[2720,128]{1,0:T(8,128)(2,1)}, bf16[2752,128]{1,0:T(8,128)(2,1)}) custom-call(bf16[224,896]{1,0:T(8,128)(2,1)} %m0_hbm.3, bf16[2,192,768]{2,1,0:T(8,128)(2,1)} %m1_hbm.1, bf16[2,160,640]{2,1,0:T(8,128)(2,1)} %m2_hbm.1), custom_call_target="tpu_custom_call" | custom-call | flops 1073741824 | bytes 4096 | tf_op jit(solution)/shard_map/pallas_call | solution.py:346
  28.7 1.9 %collective-permute-start.4 = (bf16[2752,128]{1,0:T(8,128)(2,1)}, bf16[2752,128]{1,0:T(8,128)(2,1)S(1)}, u32[]{:S(2)}, u32[]{:S(2)}) collective-permute-start(bf16[2752,128]{1,0:T(8,128)(2,1)} %get-tuple-element.32), channel_id=1, source_target_pairs={{0,6},{2,0},{4,2},{6,4},{1,7},{3,1},{5,3},{7,5},{8,14},{10,8},{12,... | collective-permute-start | bytes 2113544 | tf_op jit(solution)/shard_map/ppermute | solution.py:363
  30.7 3.4 %collective-permute-start.3 = (bf16[2720,128]{1,0:T(8,128)(2,1)}, bf16[2720,128]{1,0:T(8,128)(2,1)}, u32[]{:S(2)}, u32[]{:S(2)}) collective-permute-start(bf16[2720,128]{1,0:T(8,128)(2,1)} %get-tuple-element.31), channel_id=1, source_target_pairs={{0,2},{2,4},{4,6},{6,0},{1,3},{3,5},{5,7},{7,1},{8,10},{10,12},{12... | collective-permute-start | bytes 2088968 | tf_op jit(solution)/shard_map/ppermute | solution.py:363
  34.0 2.5 %collective-permute-start.2 = (bf16[5472,128]{1,0:T(8,128)(2,1)}, bf16[5472,128]{1,0:T(8,128)(2,1)}, u32[]{:S(2)}, u32[]{:S(2)}) collective-permute-start(bf16[5472,128]{1,0:T(8,128)(2,1)} %get-tuple-element.30.own_ref), channel_id=1, source_target_pairs={{0,1},{1,0},{2,3},{3,2},{4,5},{5,4},{6,7},{7,6},{8,9},{9,8},{10,11... | collective-permute-start | bytes 4202504 | tf_op jit(solution)/shard_map/ppermute | solution.py:367
  37.2 0.7 copy-done.4
  37.9 4.9 %shard_map.218 = (bf16[4,928,128]{2,1,0:T(8,128)(2,1)}, f32[4,32,384]{2,1,0:T(8,128)}, f32[128,256]{1,0:T(8,128)}, bf16[128,256]{1,0:T(8,128)(2,1)}, bf16[128,256]{1,0:T(8,128)(2,1)}) custom-call(s32[1]{0:T(128)S(6)} %copy.24.count_ref, bf16[16,6528]{1,0:T(8,128)(2,1)} %collective-permute-done.left_ref, bf16[16,6528]{1,0:T(8,128)(2,1)} %collective-permute-done.1.right_ref, ...), custom_call_target="tpu_custom_call" | custom-call | flops 2147483648 | bytes 4096 | tf_op jit(solution)/shard_map/pallas_call | solution.py:346
  42.9 3.4 %all-to-all-start.1 = ((f32[4,32,384]{2,1,0:T(8,128)}), f32[4,32,384]{2,1,0:T(8,128)S(1)}, u32[]{:S(2)}, u32[]{:S(2)}) async-start(f32[4,32,384]{2,1,0:T(8,128)} %get-tuple-element.33), calls=%async_computation.1 | async-start | bytes 393216 | tf_op jit(solution)/shard_map/all_to_all | solution.py:371
  46.9 4.4 %all-to-all-done.1.refs_0_ = f32[4,32,384]{2,1,0:T(8,128)S(1)} async-done(((f32[4,32,384]{2,1,0:T(8,128)}), f32[4,32,384]{2,1,0:T(8,128)S(1)}, u32[]{:S(2)}, u32[]{:S(2)}) %all-to-all-start.1) | async-done | bytes 196640 | tf_op jit(solution)/shard_map/all_to_all | solution.py:371
  51.3 0.7 copy-done.5
  52.0 2.9 %shard_map.220 = bf16[32,32,256]{2,1,0:T(8,128)(2,1)} custom-call(s32[1]{0:T(128)S(6)} %copy.24.count_ref, s32[1]{0:T(128)S(6)} %copy.25.atoms_ref, s32[1]{0:T(128)} %bitcast.rep_ref, f32[4,32,384]{2,1,0:T(8,128)} %copy-done.5, bf16[32,6272]{1,0:T(8,128)(2,1)} %refs_1_.3, bf16[32,256]{1,0:T(8,128)(2,1)} %refs_2_.3, bf16[256,256]{1,0:T(8,128)(2,1)} %refs_3_.3, ...), custom_call_target="tpu_custom_call" | custom-call | flops 1073741824 | bytes 4096 | tf_op jit(solution)/shard_map/pallas_call | solution.py:346
  55.0 5.4 %all-to-all-start.2 = ((bf16[32,32,256]{2,1,0:T(8,128)(2,1)}), bf16[32,32,256]{2,1,0:T(8,128)(2,1)S(1)}, u32[]{:S(2)}, u32[]{:S(2)}) async-start(bf16[32,32,256]{2,1,0:T(8,128)(2,1)} %shard_map.220), calls=%async_computation.2 | async-start | bytes 1048576 | tf_op jit(solution)/shard_map/all_to_all | solution.py:371
  60.4 2.1 %collective-permute-start.6 = (bf16[2752,128]{1,0:T(8,128)(2,1)S(1)}, bf16[2752,128]{1,0:T(8,128)(2,1)}, u32[]{:S(2)}, u32[]{:S(2)}) collective-permute-start(bf16[2752,128]{1,0:T(8,128)(2,1)S(1)} %collective-permute-done.4.high_ref), channel_id=1, source_target_pairs={{0,1},{1,0},{2,3},{3,2},{4,5},{5,4},{6,7},{7,6},{8,9},{9,8},{10,11... | collective-permute-start | bytes 2113544 | tf_op jit(solution)/shard_map/ppermute | solution.py:367
  62.6 2.2 %collective-permute-start.5 = (bf16[2720,128]{1,0:T(8,128)(2,1)}, bf16[2720,128]{1,0:T(8,128)(2,1)}, u32[]{:S(2)}, u32[]{:S(2)}) collective-permute-start(bf16[2720,128]{1,0:T(8,128)(2,1)} %collective-permute-done.3.low_ref), channel_id=1, source_target_pairs={{0,1},{1,0},{2,3},{3,2},{4,5},{5,4},{6,7},{7,6},{8,9},{9,8},{10,11... | collective-permute-start | bytes 2088968 | tf_op jit(solution)/shard_map/ppermute | solution.py:367
  64.8 7.3 %all-to-all-done.2.parts_ref = bf16[32,32,256]{2,1,0:T(8,128)(2,1)S(1)} async-done(((bf16[32,32,256]{2,1,0:T(8,128)(2,1)}), bf16[32,32,256]{2,1,0:T(8,128)(2,1)S(1)}, u32[]{:S(2)}, u32[]{:S(2)}) %all-to-all-start.2) | async-done | bytes 524320 | tf_op jit(solution)/shard_map/all_to_all | solution.py:371
  72.0 0.8 shard_map.221.after_ref
  72.8 8.3 %all-to-all-start.3 = ((bf16[16,32,256]{2,1,0:T(8,128)(2,1)}), bf16[16,32,256]{2,1,0:T(8,128)(2,1)S(1)}, u32[]{:S(2)}, u32[]{:S(2)}) async-start(bf16[16,32,256]{2,1,0:T(8,128)(2,1)} %shard_map.221.after_ref), calls=%async_computation.3 | async-start | bytes 524288 | tf_op jit(solution)/shard_map/all_to_all | solution.py:371
  81.2 1.2 %copy-done.3 = bf16[4,928,128]{2,1,0:T(8,128)(2,1)S(1)} copy-done((bf16[4,928,128]{2,1,0:T(8,128)(2,1)S(1)}, bf16[4,928,128]{2,1,0:T(8,128)(2,1)}, u32[]{:S(2)}) %copy-start.3) | copy-done | bytes 950296
  82.4 5.6 %shard_map.222 = (f32[8,6272]{1,0:T(8,128)S(1)}, bf16[8,6272]{1,0:T(8,128)(2,1)S(1)}, bf16[8,6272]{1,0:T(8,128)(2,1)S(1)}, bf16[8,6272]{1,0:T(8,128)(2,1)S(1)}) custom-call(s32[1]{0:T(128)S(6)} %copy.24.count_ref, s32[1]{0:T(128)} %bitcast.rep_ref, bf16[4,928,128]{2,1,0:T(8,128)(2,1)S(1)} %copy-done.3, bf16[5472,128]{1,0:T(8,128)(2,1)S(1)} %copy-done, ...), custom_call_target="tpu_custom_call" | custom-call | flops 4294967296 | bytes 4096 | tf_op jit(solution)/shard_map/pallas_call | solution.py:346
  88.1 2.0 %collective-permute-start.7 = (bf16[8,6272]{1,0:T(8,128)(2,1)S(1)}, bf16[8,6272]{1,0:T(8,128)(2,1)S(1)}, u32[]{:S(2)}, u32[]{:S(2)}) collective-permute-start(bf16[8,6272]{1,0:T(8,128)(2,1)S(1)} %get-tuple-element.38), channel_id=1, source_target_pairs={{0,1},{1,0},{2,3},{3,2},{4,5},{5,4},{6,7},{7,6},{8,9},{9,8},{10,11... | collective-permute-start | bytes 301064 | tf_op jit(solution)/shard_map/ppermute | solution.py:367
  90.0 2.4 %collective-permute-start.8 = (bf16[8,6272]{1,0:T(8,128)(2,1)S(1)}, bf16[8,6272]{1,0:T(8,128)(2,1)S(1)}, u32[]{:S(2)}, u32[]{:S(2)}) collective-permute-start(bf16[8,6272]{1,0:T(8,128)(2,1)S(1)} %get-tuple-element.39), channel_id=1, source_target_pairs={{0,2},{1,3},{2,0},{3,1},{4,6},{5,7},{6,4},{7,5},{8,10},{9,11},{10,... | collective-permute-start | bytes 301064 | tf_op jit(solution)/shard_map/ppermute | solution.py:367
  92.4 3.5 %collective-permute-start.9 = (bf16[8,6272]{1,0:T(8,128)(2,1)S(1)}, bf16[8,6272]{1,0:T(8,128)(2,1)S(1)}, u32[]{:S(2)}, u32[]{:S(2)}) collective-permute-start(bf16[8,6272]{1,0:T(8,128)(2,1)S(1)} %get-tuple-element.40), channel_id=1, source_target_pairs={{0,3},{1,2},{2,1},{3,0},{4,7},{5,6},{6,5},{7,4},{8,11},{9,10},{10,... | collective-permute-start | bytes 301064 | tf_op jit(solution)/shard_map/ppermute | solution.py:367
  95.9 0.2 all-to-all-done.3.parts_ref
  96.2 0.9 shard_map.224
  97.1 7.7 %all-to-all-start.4 = ((bf16[32,32,256]{2,1,0:T(8,128)(2,1)}), bf16[32,32,256]{2,1,0:T(8,128)(2,1)S(1)}, u32[]{:S(2)}, u32[]{:S(2)}) async-start(bf16[32,32,256]{2,1,0:T(8,128)(2,1)} %shard_map.224), calls=%async_computation.4 | async-start | bytes 1048576 | tf_op jit(solution)/shard_map/all_to_all | solution.py:371
  104.7 0.9 constant_dynamic-slice_fusion.own_ref
  105.7 0.7 shard_map.223
  106.4 10.1 %all-to-all-done.4.all_ref = bf16[32,32,256]{2,1,0:T(8,128)(2,1)S(1)} async-done(((bf16[32,32,256]{2,1,0:T(8,128)(2,1)}), bf16[32,32,256]{2,1,0:T(8,128)(2,1)S(1)}, u32[]{:S(2)}, u32[]{:S(2)}) %all-to-all-start.4) | async-done | bytes 524320 | tf_op jit(solution)/shard_map/all_to_all | solution.py:371
  116.5 1.0 shard_map.225
  (20 shorter events, 0.1 us)
Async XLA Ops:
  2.8 34.5 %collective-permute-start = (bf16[16,6528]{1,0:T(8,128)(2,1)}, bf16[16,6528]{1,0:T(8,128)(2,1)}, u32[]{:S(2)}, u32[]{:S(2)}) collective-permute-start(bf16[16,6528]{1,0:T(8,128)(2,1)} %get-tuple-element.26), channel_id=1, source_target_pairs={{0,4},{4,8},{8,12},{12,16},{16,20},{20,24},{24,28},{28,32},{32,36}... | collective-permute-start | bytes 626696 | tf_op jit(solution)/shard_map/ppermute | solution.py:363
  8.4 28.8 %collective-permute-start.1 = (bf16[16,6528]{1,0:T(8,128)(2,1)}, bf16[16,6528]{1,0:T(8,128)(2,1)}, u32[]{:S(2)}, u32[]{:S(2)}) collective-permute-start(bf16[16,6528]{1,0:T(8,128)(2,1)} %get-tuple-element.27), channel_id=1, source_target_pairs={{0,508},{4,0},{8,4},{12,8},{16,12},{20,16},{24,20},{28,24},{32,28}... | collective-permute-start | bytes 626696 | tf_op jit(solution)/shard_map/ppermute | solution.py:363
  21.5 15.7 %all-to-all-start = ((bf16[4,224,128]{2,1,0:T(8,128)(2,1)}), bf16[4,224,128]{2,1,0:T(8,128)(2,1)S(1)}, u32[]{:S(2)}, u32[]{:S(2)}) async-start(bf16[4,224,128]{2,1,0:T(8,128)(2,1)} %get-tuple-element.28), calls=%async_computation | async-start | bytes 458752 | tf_op jit(solution)/shard_map/all_to_all | solution.py:371
  28.7 31.7 %collective-permute-start.4 = (bf16[2752,128]{1,0:T(8,128)(2,1)}, bf16[2752,128]{1,0:T(8,128)(2,1)S(1)}, u32[]{:S(2)}, u32[]{:S(2)}) collective-permute-start(bf16[2752,128]{1,0:T(8,128)(2,1)} %get-tuple-element.32), channel_id=1, source_target_pairs={{0,6},{2,0},{4,2},{6,4},{1,7},{3,1},{5,3},{7,5},{8,14},{10,8},{12,... | collective-permute-start | bytes 2113544 | tf_op jit(solution)/shard_map/ppermute | solution.py:363
  30.7 31.9 %collective-permute-start.3 = (bf16[2720,128]{1,0:T(8,128)(2,1)}, bf16[2720,128]{1,0:T(8,128)(2,1)}, u32[]{:S(2)}, u32[]{:S(2)}) collective-permute-start(bf16[2720,128]{1,0:T(8,128)(2,1)} %get-tuple-element.31), channel_id=1, source_target_pairs={{0,2},{2,4},{4,6},{6,0},{1,3},{3,5},{5,7},{7,1},{8,10},{10,12},{12... | collective-permute-start | bytes 2088968 | tf_op jit(solution)/shard_map/ppermute | solution.py:363
  34.0 47.2 %collective-permute-start.2 = (bf16[5472,128]{1,0:T(8,128)(2,1)}, bf16[5472,128]{1,0:T(8,128)(2,1)}, u32[]{:S(2)}, u32[]{:S(2)}) collective-permute-start(bf16[5472,128]{1,0:T(8,128)(2,1)} %get-tuple-element.30.own_ref), channel_id=1, source_target_pairs={{0,1},{1,0},{2,3},{3,2},{4,5},{5,4},{6,7},{7,6},{8,9},{9,8},{10,11... | collective-permute-start | bytes 4202504 | tf_op jit(solution)/shard_map/ppermute | solution.py:367
  37.2 0.7 copy-start.4
  42.9 8.5 %all-to-all-start.1 = ((f32[4,32,384]{2,1,0:T(8,128)}), f32[4,32,384]{2,1,0:T(8,128)S(1)}, u32[]{:S(2)}, u32[]{:S(2)}) async-start(f32[4,32,384]{2,1,0:T(8,128)} %get-tuple-element.33), calls=%async_computation.1 | async-start | bytes 393216 | tf_op jit(solution)/shard_map/all_to_all | solution.py:371
  51.3 0.7 copy-start.5
  54.9 26.3 %copy-start = (bf16[5472,128]{1,0:T(8,128)(2,1)S(1)}, bf16[5472,128]{1,0:T(8,128)(2,1)}, u32[]{:S(2)}) copy-start(bf16[5472,128]{1,0:T(8,128)(2,1)} %get-tuple-element.30.own_ref) | copy-start | bytes 4202500
  55.0 26.3 %copy-start.1 = (bf16[235,128]{1,0:T(8,128)(2,1)S(1)}, bf16[235,128]{1,0:T(8,128)(2,1)}, u32[]{:S(2)}) copy-start(bf16[235,128]{1,0:T(8,128)(2,1)} %wig_ref.1) | copy-start | bytes 180484
  55.0 26.3 %copy-start.2 = (s32[128]{0:T(128)S(1)}, s32[128]{0:T(128)}, u32[]{:S(2)}) copy-start(s32[128]{0:T(128)} %param.32) | copy-start | bytes 1540
  55.0 17.1 %all-to-all-start.2 = ((bf16[32,32,256]{2,1,0:T(8,128)(2,1)}), bf16[32,32,256]{2,1,0:T(8,128)(2,1)S(1)}, u32[]{:S(2)}, u32[]{:S(2)}) async-start(bf16[32,32,256]{2,1,0:T(8,128)(2,1)} %shard_map.220), calls=%async_computation.2 | async-start | bytes 1048576 | tf_op jit(solution)/shard_map/all_to_all | solution.py:371
  60.4 20.8 %collective-permute-start.6 = (bf16[2752,128]{1,0:T(8,128)(2,1)S(1)}, bf16[2752,128]{1,0:T(8,128)(2,1)}, u32[]{:S(2)}, u32[]{:S(2)}) collective-permute-start(bf16[2752,128]{1,0:T(8,128)(2,1)S(1)} %collective-permute-done.4.high_ref), channel_id=1, source_target_pairs={{0,1},{1,0},{2,3},{3,2},{4,5},{5,4},{6,7},{7,6},{8,9},{9,8},{10,11... | collective-permute-start | bytes 2113544 | tf_op jit(solution)/shard_map/ppermute | solution.py:367
  62.6 18.6 %collective-permute-start.5 = (bf16[2720,128]{1,0:T(8,128)(2,1)}, bf16[2720,128]{1,0:T(8,128)(2,1)}, u32[]{:S(2)}, u32[]{:S(2)}) collective-permute-start(bf16[2720,128]{1,0:T(8,128)(2,1)} %collective-permute-done.3.low_ref), channel_id=1, source_target_pairs={{0,1},{1,0},{2,3},{3,2},{4,5},{5,4},{6,7},{7,6},{8,9},{9,8},{10,11... | collective-permute-start | bytes 2088968 | tf_op jit(solution)/shard_map/ppermute | solution.py:367
  72.8 23.3 %all-to-all-start.3 = ((bf16[16,32,256]{2,1,0:T(8,128)(2,1)}), bf16[16,32,256]{2,1,0:T(8,128)(2,1)S(1)}, u32[]{:S(2)}, u32[]{:S(2)}) async-start(bf16[16,32,256]{2,1,0:T(8,128)(2,1)} %shard_map.221.after_ref), calls=%async_computation.3 | async-start | bytes 524288 | tf_op jit(solution)/shard_map/all_to_all | solution.py:371
  81.2 1.2 %copy-start.3 = (bf16[4,928,128]{2,1,0:T(8,128)(2,1)S(1)}, bf16[4,928,128]{2,1,0:T(8,128)(2,1)}, u32[]{:S(2)}) copy-start(bf16[4,928,128]{2,1,0:T(8,128)(2,1)} %get-tuple-element.29.pack_ref) | copy-start | bytes 2850820
  88.1 17.6 %collective-permute-start.7 = (bf16[8,6272]{1,0:T(8,128)(2,1)S(1)}, bf16[8,6272]{1,0:T(8,128)(2,1)S(1)}, u32[]{:S(2)}, u32[]{:S(2)}) collective-permute-start(bf16[8,6272]{1,0:T(8,128)(2,1)S(1)} %get-tuple-element.38), channel_id=1, source_target_pairs={{0,1},{1,0},{2,3},{3,2},{4,5},{5,4},{6,7},{7,6},{8,9},{9,8},{10,11... | collective-permute-start | bytes 301064 | tf_op jit(solution)/shard_map/ppermute | solution.py:367
  90.0 15.6 %collective-permute-start.8 = (bf16[8,6272]{1,0:T(8,128)(2,1)S(1)}, bf16[8,6272]{1,0:T(8,128)(2,1)S(1)}, u32[]{:S(2)}, u32[]{:S(2)}) collective-permute-start(bf16[8,6272]{1,0:T(8,128)(2,1)S(1)} %get-tuple-element.39), channel_id=1, source_target_pairs={{0,2},{1,3},{2,0},{3,1},{4,6},{5,7},{6,4},{7,5},{8,10},{9,11},{10,... | collective-permute-start | bytes 301064 | tf_op jit(solution)/shard_map/ppermute | solution.py:367
  92.4 13.2 %collective-permute-start.9 = (bf16[8,6272]{1,0:T(8,128)(2,1)S(1)}, bf16[8,6272]{1,0:T(8,128)(2,1)S(1)}, u32[]{:S(2)}, u32[]{:S(2)}) collective-permute-start(bf16[8,6272]{1,0:T(8,128)(2,1)S(1)} %get-tuple-element.40), channel_id=1, source_target_pairs={{0,3},{1,2},{2,1},{3,0},{4,7},{5,6},{6,5},{7,4},{8,11},{9,10},{10,... | collective-permute-start | bytes 301064 | tf_op jit(solution)/shard_map/ppermute | solution.py:367
  97.1 19.4 %all-to-all-start.4 = ((bf16[32,32,256]{2,1,0:T(8,128)(2,1)}), bf16[32,32,256]{2,1,0:T(8,128)(2,1)S(1)}, u32[]{:S(2)}, u32[]{:S(2)}) async-start(bf16[32,32,256]{2,1,0:T(8,128)(2,1)} %shard_map.224), calls=%async_computation.4 | async-start | bytes 1048576 | tf_op jit(solution)/shard_map/all_to_all | solution.py:371

commit v3 on v2

v3 whole, which is shorter than its diff:
```python
import functools
import math

import jax
import jax.numpy as jnp
from jax import lax
from jax.experimental import pallas as pl
from jax.experimental.pallas import tpu as pltpu
from jax.sharding import Mesh, PartitionSpec as P

LMAX = 6
MMAX = 2
DEG = 16
C = 128
OWN = 32
EXT = 64
EDGE = 128
SW = 256
KC = 6272
FULL = 64 << 10
LOW = 7 * 224 + 6 * 192
HIGH = 6 * 192 + 10 * 160
SECTIONS = {0: (224, 0), 1: (192, 224), -1: (192, 416), 2: (160, 608), -2: (160, 768)}
BF = jnp.bfloat16
F32 = jnp.float32
BRICK = ("z", "x", "yh")
REP = ("yl", "core")
PLANE = ("x", "yh", "yl", "core")
VMEM = pl.BlockSpec(memory_space=pltpu.VMEM)
HBM = pl.BlockSpec(memory_space=pltpu.HBM)
ANY = pl.BlockSpec(memory_space=pl.ANY)
SMEM = pl.BlockSpec(memory_space=pltpu.SMEM)


def offsets():
    found = []
    row = 0
    for degree in range(LMAX + 1):
        found.append(row)
        row += (2 * min(degree, MMAX) + 1) * (2 * degree + 1)
    return found


OFFSET = offsets()


def dot(left, right, over=((1,), (0,))):
    return lax.dot_general(left, right, (over, ((), ())), preferred_element_type=F32)


def live_row(count):
    return lax.broadcasted_iota(jnp.int32, (1, EDGE), 1) < count


def fetch(pairs, sems):
    copies = [
        pltpu.make_async_copy(source, target, sems.at[i])
        for i, (source, target) in enumerate(pairs)
    ]
    for copy in copies:
        copy.start()
    return copies


def start_body(
    count_ref, lists_hbm, teacher_hbm, student_hbm, m0_hbm, basis_hbm, wig_hbm, src_hbm, dst_hbm,
    next_ref, prev_ref, meta_ref,
    lists_ref, teacher_ref, student_ref, m0_ref, basis_ref, wig_ref, src_ref, dst_ref,
    wigf_ref, rows_ref, sems,
):
    copies = fetch(
        (
            (lists_hbm, lists_ref), (teacher_hbm, teacher_ref), (student_hbm, student_ref),
            (m0_hbm.at[:, :C], m0_ref), (basis_hbm, basis_ref), (wig_hbm, wig_ref),
            (src_hbm, src_ref), (dst_hbm, dst_ref),
        ),
        sems,
    )
    for copy in copies:
        copy.wait()
    rows = lax.broadcasted_iota(jnp.int32, (OWN, 16), 0)
    for k, out_ref in enumerate((next_ref, prev_ref)):
        pick = (rows == lists_ref[0, k : k + 1, :]).astype(F32).astype(BF)
        out_ref[:, :KC] = dot(pick, teacher_ref[...], ((0,), (0,))).astype(BF)
        out_ref[:, KC:] = dot(pick, student_ref[...], ((0,), (0,))).astype(BF)
    wigf_ref[...] = wig_ref[...].astype(F32)
    rows_ref[...] = jnp.zeros_like(rows_ref)
    for degree in range(LMAX + 1):
        span = 2 * degree + 1
        row = OFFSET[degree] + min(degree, MMAX) * span
        rows_ref[degree * degree : degree * degree + span] = wigf_ref[row : row + span]
    rows_ref[49:50] = src_ref[...].astype(F32)
    rows_ref[50:51] = live_dst(dst_ref[...], count_ref[0])
    edges = rows_ref[...].astype(BF)
    for r in range(4):
        meta_ref[r, :224] = m0_ref[...]
        meta_ref[r, 224:352] = basis_ref[...]
        meta_ref[r, 352:] = edges


def live_dst(dst_row, count):
    return jnp.where(live_row(count), dst_row, EXT).astype(F32)


def pack_body(m0_hbm, m1_hbm, m2_hbm, low_ref, high_ref, m0_ref, m1_ref, m2_ref, sems):
    copies = fetch(((m0_hbm, m0_ref), (m1_hbm, m1_ref), (m2_hbm, m2_ref)), sems)
    at = 0
    for part, wide, high, ready in (
        (m0_ref, 7, 224, 0), (m1_ref.at[0], 6, 192, 1), (m1_ref.at[1], 6, 192, None),
        (m2_ref.at[0], 5, 160, 2), (m2_ref.at[1], 5, 160, None),
    ):
        if ready is not None:
            copies[ready].wait()
        for n in range(wide):
            block = part[:, n * C : (n + 1) * C]
            if at < LOW:
                low_ref[at : at + high] = block
            else:
                high_ref[at - LOW : at - LOW + high] = block
            at += high


def coefficients(refs, degree):
    parts = []
    for j in range(2 * degree + 1):
        lo = (degree * degree + j) * C
        parts += [ref[:, lo : lo + C] for ref in refs]
    return jnp.concatenate(parts, axis=0)


def gain_of(basis, radial):
    return dot(radial, basis.astype(F32).T.astype(BF), ((0,), (0,)))


def keep_turned(pack_ref, block, start, part, base):
    row = 0
    while row < C:
        which = (start + row) // part
        inside = (start + row) % part
        size = min(C - row, part - inside)
        pack_ref[which, base + inside : base + inside + size] = block[row : row + size]
        row += size


def early_body(inv_atoms, atoms_ref, rep_ref, *refs):
    raw = refs[:11]
    grad_ref = refs[11]
    held = refs[12:23]
    turn_ref, rotated_ref, hidden_ref, ssrc_ref, sdst_ref, target_ref, sems = refs[23:]
    (
        meta_ref, left_ref, right_ref, teacher_ref, student_ref, radial_ref, wsrc_ref, wdst_ref,
        wrad_ref, wout_ref, whead_ref,
    ) = held
    for copy in fetch(tuple(zip(raw, held)), sems):
        copy.wait()
    every = 4 * EDGE
    edges = [meta_ref[q, 352:416].astype(F32) for q in range(4)]
    ext_rows = lax.broadcasted_iota(jnp.int32, (EXT, EDGE), 0).astype(F32)
    sources = [(edges[q][49:50] == ext_rows).astype(F32) for q in range(4)]
    targets = [(edges[q][50:51] == ext_rows[:OWN]).astype(F32) for q in range(4)]
    gains = jnp.concatenate(
        [gain_of(meta_ref[q, 224:352], radial_ref[...]) for q in range(4)], axis=1
    )
    for degree in range(LMAX + 1):
        span = 2 * degree + 1
        for q in range(4):
            for j in range(span):
                row = degree * degree + j
                turn_ref[j * EXT : (j + 1) * EXT, q * EDGE : (q + 1) * EDGE] = (
                    sources[q] * edges[q][row : row + 1]
                ).astype(BF)
        stacked = coefficients((teacher_ref, left_ref, right_ref), degree)
        turned = dot(stacked, turn_ref[: span * EXT], ((0,), (0,)))
        rotated_ref[degree * C : (degree + 1) * C] = (turned * gains).astype(BF)
    column = jnp.concatenate([meta_ref[q, :224] for q in range(4)], axis=0)
    invariant = dot(rotated_ref[...], column, ((0,), (0,))).astype(BF)
    scatter = jnp.concatenate([targets[q] * edges[q][0:1] for q in range(4)], axis=1).astype(BF)
    invariants = dot(scatter, invariant)
    student_ext = jnp.concatenate(
        [student_ref[...], left_ref[:, KC:], right_ref[:, KC:]], axis=0
    )
    basis = jnp.concatenate([meta_ref[q, 224:352] for q in range(4)], axis=0)
    source = jnp.concatenate(sources, axis=1).astype(BF)
    onehot = jnp.concatenate(targets, axis=1).astype(BF)
    ssrc = dot(source, student_ext, ((0,), (0,))).astype(BF)
    sdst = dot(onehot, student_ref[...], ((0,), (0,))).astype(BF)
    hidden = dot(ssrc, wsrc_ref[...]) + dot(sdst, wdst_ref[...]) + dot(basis, wrad_ref[...])
    gated = (hidden * jax.nn.sigmoid(hidden)).astype(BF)
    hidden_ref[...] = hidden
    ssrc_ref[...] = ssrc
    sdst_ref[...] = sdst
    for q in range(4):
        target_ref[q] = targets[q].astype(BF)

    inv_degree = 1.0 / math.sqrt(DEG)
    target = (teacher_ref[:, :C].astype(F32) + inv_degree * invariants).astype(BF)
    pooled = (dot(onehot, gated) * inv_degree).astype(BF)
    updated = (student_ref[...].astype(F32) + dot(pooled, wout_ref[...])).astype(BF)
    predicted = dot(updated, whead_ref[...])
    rows = lax.broadcasted_iota(jnp.int32, (OWN, 1), 0)
    residual = jnp.where(rows < atoms_ref[0], predicted - target.astype(F32), 0.0)
    scaled = (residual * inv_atoms).astype(BF)
    upstream = dot(scaled, whead_ref[...], ((1,), (1,))).astype(BF)
    rep = rep_ref[0]
    mine = (rows >= rep * 8) & (rows < rep * 8 + 8)
    scaled_part = jnp.where(mine, scaled.astype(F32), 0.0).astype(BF)
    upstream_part = jnp.where(mine, upstream.astype(F32), 0.0).astype(BF)
    grad_head = dot(updated, scaled_part, ((0,), (0,)))
    grad_out = dot(pooled, upstream_part, ((0,), (0,)))
    pooled_grad = dot(upstream, wout_ref[...], ((1,), (1,))).astype(BF)
    own = pl.ds(pl.multiple_of(rep * EDGE, EDGE), EDGE)
    edge_grad = dot(target_ref[rep], pooled_grad, ((0,), (0,))) * inv_degree
    hidden = hidden_ref[own, :]
    logistic = jax.nn.sigmoid(hidden)
    hidden_grad = (edge_grad * logistic * (1.0 + hidden * (1.0 - logistic))).astype(BF)
    high = grad_ref.shape[1]
    for start, stop, value in (
        (0, 256, dot(ssrc_ref[own, :], hidden_grad, ((0,), (0,)))),
        (256, 512, dot(sdst_ref[own, :], hidden_grad, ((0,), (0,)))),
        (512, 768, grad_out),
        (768, 896, dot(meta_ref[rep, 224:352], hidden_grad, ((0,), (0,)))),
        (896, 1024, jnp.concatenate([grad_head[:C], grad_head[C:]], axis=1)),
    ):
        grad_ref[start // high : stop // high] = value.astype(BF).reshape(-1, high, SW)


def rotate_body(count_ref, rep_ref, *refs):
    raw = refs[:8]
    after_ref, keep_ref, give_ref = refs[8:11]
    held = refs[11:19]
    pack_ref, wigf_ref, turn_ref, sems = refs[19:]
    teacher_ref, left_ref, right_ref, wig_ref, basis_ref, radial_ref, src_ref, dst_ref = held
    for copy in fetch(tuple(zip(raw, held)), sems):
        copy.wait()
    rep = rep_ref[0]
    wigf_ref[:235] = wig_ref[...].astype(F32)
    wigf_ref[235:] = jnp.broadcast_to(live_dst(dst_ref[...], count_ref[0]), (5, EDGE))
    source = (src_ref[...] == lax.broadcasted_iota(jnp.int32, (EXT, EDGE), 0)).astype(F32)
    gain = gain_of(basis_ref[...], radial_ref[...])
    for degree in range(LMAX + 1):
        cap = min(degree, MMAX)
        span = 2 * degree + 1
        orders = 2 * cap + 1
        for morder in range(orders):
            for j in range(span):
                row = OFFSET[degree] + morder * span + j
                turn_ref[j * EXT : (j + 1) * EXT, morder * EDGE : (morder + 1) * EDGE] = (
                    source * wigf_ref[row : row + 1, :]
                ).astype(BF)
        stacked = coefficients((teacher_ref, left_ref, right_ref), degree)
        turned = dot(stacked, turn_ref[: span * EXT, : orders * EDGE], ((0,), (0,)))
        for morder in range(orders):
            block = (turned[:, morder * EDGE : (morder + 1) * EDGE] * gain).astype(BF)
            signed = morder - cap
            part, base = SECTIONS[signed]
            keep_turned(pack_ref, block, (degree - abs(signed)) * C, part, base)
    edges = wigf_ref[...].astype(BF)
    for out_ref, first in ((keep_ref, 0), (give_ref, 1)):
        out_ref[:928] = pack_ref[rep ^ first]
        out_ref[928:1856] = pack_ref[rep ^ (first + 2)]
        out_ref[1856:] = edges


def spread_body(parts_ref, *refs):
    out_ref = refs[-1]
    total = parts_ref[0].astype(F32)
    for i in range(1, parts_ref.shape[0]):
        total += parts_ref[i].astype(F32)
    total = total.astype(out_ref.dtype)
    for i in range(out_ref.shape[0]):
        out_ref[i] = total


def unpack_body(all_ref, src_ref, dst_ref, radial_ref, out_ref, head_ref):
    values = all_ref[...].astype(F32).reshape(1024, SW)
    src_ref[...] = values[:256]
    dst_ref[...] = values[256:512]
    out_ref[...] = values[512:768]
    radial_ref[...] = values[768:896]
    head_ref[:C] = values[896:, :C]
    head_ref[C:] = values[896:, C:]


def blocks(ref, at, count, high):
    return jnp.concatenate(
        [ref[at + n * high : at + (n + 1) * high] for n in range(count)], axis=1
    )


def mix_body(
    rep_ref, keep_ref, got_ref, low_ref, high_ref, far_low_ref, far_high_ref, after_ref,
    o0_ref, o1_ref, o2_ref, o3_ref,
    wigf_ref, back_ref, sums_ref,
):
    rep = rep_ref[0]
    groups = (keep_ref, got_ref)
    own_rows = lax.broadcasted_iota(jnp.int32, (OWN, EDGE), 0).astype(F32)
    targets = []
    for g in range(2):
        wigf_ref[g] = groups[g][1856:].astype(F32)
        targets.append((wigf_ref[g, 235:236] == own_rows).astype(F32))
    lows = (low_ref, far_low_ref)
    highs = (high_ref, far_high_ref)
    over = ((0,), (0,))

    def rows(k, base, size):
        at = 928 * k + base
        return [group[at : at + size] for group in groups]

    y0 = 0.0
    for k in range(2):
        y0 += dot(jnp.concatenate(rows(k, 0, 224), axis=1), blocks(lows[k], 0, 7, 224), over)
    y0 = y0.astype(BF)
    mixed = [None]
    both = 2 * EDGE
    for wide, base in ((6, 224), (5, 608)):
        size = wide * 32
        real = 0.0
        imag = 0.0
        for k in range(2):
            pair = jnp.concatenate(rows(k, base, size) + rows(k, base + size, size), axis=1)
            if wide == 6:
                first = blocks(lows[k], 1568, 6, 192)
                second = blocks(highs[k], 0, 6, 192)
            else:
                first = blocks(highs[k], 1152, 5, 160)
                second = blocks(highs[k], 1952, 5, 160)
            real += dot(pair, first, over)
            imag += dot(pair, second, over)
        plus = (real[:both] - imag[both:]).astype(BF)
        minus = (imag[:both] + real[both:]).astype(BF)
        mixed.append((plus, minus))
    for degree in range(LMAX + 1):
        cap = min(degree, MMAX)
        span = 2 * degree + 1
        orders = 2 * cap + 1
        stacked = []
        for morder in range(orders):
            signed = morder - cap
            if signed == 0:
                stacked.append(y0[:, degree * C : (degree + 1) * C])
            else:
                slot = degree - abs(signed)
                part = mixed[abs(signed)][0 if signed > 0 else 1]
                stacked.append(part[:, slot * C : (slot + 1) * C])
            for j in range(span):
                row = OFFSET[degree] + morder * span + j
                for g in range(2):
                    lane = morder * both + g * EDGE
                    back_ref[j * OWN : (j + 1) * OWN, lane : lane + EDGE] = (
                        targets[g] * wigf_ref[g, row : row + 1, :]
                    ).astype(BF)
        summed = dot(
            back_ref[: span * OWN, : orders * both], jnp.concatenate(stacked, axis=0)
        )
        for j in range(span):
            lo = (degree * degree + j) * C
            sums_ref[:, lo : lo + C] = summed[j * OWN : (j + 1) * OWN]
    for k, out_ref in enumerate((o0_ref, o1_ref, o2_ref, o3_ref)):
        start = pl.multiple_of((rep ^ k) * 8, 8)
        out_ref[...] = sums_ref[pl.ds(start, 8), :].astype(out_ref.dtype)


def finish_body(own_ref, s0_ref, s1_ref, s2_ref, s3_ref, out_ref):
    total = (s0_ref[...] + s1_ref[...].astype(F32)) + (
        s2_ref[...].astype(F32) + s3_ref[...].astype(F32)
    )
    out_ref[...] = (own_ref[...].astype(F32) + total * (1.0 / math.sqrt(DEG))).astype(BF)


def call(body, outs, ins, scratch=(), scalars=0, raws=0, after=0, flops=0, room=24 << 10):
    specs = [SMEM] * scalars + [VMEM] * (len(ins) - scalars - raws - after)
    return pl.pallas_call(
        body,
        out_shape=tuple(jax.ShapeDtypeStruct(shape, dtype) for shape, dtype in outs),
        in_specs=specs + [HBM] * raws + [ANY] * after,
        out_specs=tuple(VMEM for _ in outs),
        scratch_shapes=list(scratch),
        compiler_params=pltpu.CompilerParams(vmem_limit_bytes=(FULL - room) << 10),
        cost_estimate=pl.CostEstimate(flops=flops, bytes_accessed=4096, transcendentals=0),
    )(*ins)


def held(arrays):
    return [pltpu.VMEM(array.shape, array.dtype) for array in arrays]


def shifted(x, axes, by):
    length = lax.axis_size(axes)
    return lax.ppermute(x, axes, [(i, (i + by) % length) for i in range(length)])


def swapped(x, axes, mask):
    return lax.ppermute(x, axes, [(i, i ^ mask) for i in range(lax.axis_size(axes))])


def exchange(x, axes):
    return lax.all_to_all(x, axes, 0, 0, tiled=True)


def per_device(
    teacher_in, student_in, wigner, edge_basis, teacher_radial, so2_m0, so2_m1, so2_m2,
    w_src, w_dst, w_radial, w_out, w_head, src, dst, edge_count, atom_count, send_idx,
):
    bricks = lax.axis_size(BRICK)
    plane = lax.axis_size(PLANE)
    line = lax.axis_size("z")
    rep = lax.axis_index(REP).astype(jnp.int32)
    rep1 = rep.reshape(1)
    src_row = src.reshape(1, EDGE)
    dst_row = dst.reshape(1, EDGE)
    chunk = 1024 // plane
    raw = (send_idx, teacher_in, student_in, so2_m0, edge_basis, wigner, src_row, dst_row)
    to_next, to_prev, own_meta = call(
        start_body,
        [((16, KC + SW), BF), ((16, KC + SW), BF), ((4, 416, C), BF)],
        (edge_count, *raw),
        held(raw[:3])
        + [pltpu.VMEM((224, C), BF)]
        + held(raw[4:])
        + [
            pltpu.VMEM((235, EDGE), F32), pltpu.VMEM((64, EDGE), F32),
            pltpu.SemaphoreType.DMA((8,)),
        ],
        scalars=1,
        raws=8,
        room=1024,
    )
    from_left = shifted(to_next, BRICK, 1)
    from_right = shifted(to_prev, BRICK, -1)
    meta = exchange(own_meta, REP)
    mixings = (so2_m0, so2_m1, so2_m2)
    low, high = call(
        pack_body,
        [((LOW, C), BF), ((HIGH, C), BF)],
        mixings,
        held(mixings) + [pltpu.SemaphoreType.DMA((3,))],
        raws=3,
        flops=1 << 30,
        room=1024,
    )
    raw = (
        meta, from_left, from_right, teacher_in, student_in, teacher_radial, w_src, w_dst,
        w_radial, w_out, w_head,
    )
    (grads,) = call(
        functools.partial(early_body, 1.0 / (OWN * bricks)),
        [((plane, chunk, SW), BF)],
        (atom_count, rep1, *raw),
        held(raw)
        + [
            pltpu.VMEM((13 * EXT, 4 * EDGE), BF), pltpu.VMEM((896, 4 * EDGE), BF),
            pltpu.VMEM((4 * EDGE, SW), F32), pltpu.VMEM((4 * EDGE, SW), BF),
            pltpu.VMEM((4 * EDGE, SW), BF), pltpu.VMEM((4, OWN, EDGE), BF),
            pltpu.SemaphoreType.DMA((11,)),
        ],
        scalars=2,
        raws=11,
        flops=1 << 31,
        room=1024,
    )
    low, high, grads = lax.optimization_barrier((low, high, grads))
    across_low = shifted(low, ("yh", "yl"), 1)
    across_high = shifted(high, ("yh", "yl"), -1)
    plane_parts = exchange(grads, PLANE)
    raw = (
        teacher_in, from_left, from_right, wigner, edge_basis, teacher_radial, src_row, dst_row
    )
    keep, give = call(
        rotate_body,
        [((1856 + 240, EDGE), BF)] * 2,
        (edge_count, rep1, *raw, grads),
        held(raw)
        + [
            pltpu.VMEM((4, 928, EDGE), BF), pltpu.VMEM((240, EDGE), F32),
            pltpu.VMEM((13 * EXT, 5 * EDGE), BF), pltpu.SemaphoreType.DMA((8,)),
        ],
        scalars=2,
        raws=8,
        after=1,
        flops=1 << 31,
        room=4096,
    )
    got = swapped(give, "core", 1)
    plane_parts, keep = lax.optimization_barrier((plane_parts, keep))
    (plane_sum,) = call(spread_body, [((line, chunk, SW), BF)], (plane_parts,))
    shares = call(
        mix_body,
        [((8, KC), F32)] + [((8, KC), BF)] * 3,
        (rep1, keep, got, low, high, across_low, across_high, plane_sum),
        [
            pltpu.VMEM((2, 240, EDGE), F32),
            pltpu.VMEM((13 * OWN, 10 * EDGE), BF),
            pltpu.VMEM((OWN, KC), F32),
        ],
        scalars=1,
        after=1,
        flops=1 << 32,
    )
    line_parts = exchange(plane_sum, "z")
    line_parts, share = lax.optimization_barrier((line_parts, shares[0]))
    (total,) = call(spread_body, [((plane, chunk, SW), BF)], (line_parts,))
    arrived = [share] + [swapped(shares[k], REP, k) for k in (1, 2, 3)]
    totals = exchange(total, PLANE)
    arrived = [share] + [swapped(shares[k], REP, k) for k in (1, 2, 3)]
    mine = lax.dynamic_slice_in_dim(teacher_in, rep * 8, 8, 0)
    (teacher_out,) = call(finish_body, [((8, KC), BF)], (mine, *arrived))
    grads_out = call(
        unpack_body,
        [((256, SW), F32), ((256, SW), F32), ((128, SW), F32), ((256, SW), F32), ((256, C), F32)],
        (totals,),
    )
    return (teacher_out, *grads_out)


def solution(mesh):
    fine = Mesh(mesh.devices.reshape(16, 4, 2, 2, 2), BRICK + REP)
    every = BRICK + REP
    placed = (
        P(BRICK, None),
        P(BRICK, None),
        P(None, every),
        P(every, None),
        P(),
        P(REP, None),
        P(None, REP, None),
        P(None, REP, None),
        P(),
        P(),
        P(),
        P(),
        P(),
        P(every),
        P(every),
        P(every),
        P(BRICK),
        P(BRICK, None, None),
    )
    return jax.shard_map(
        per_device,
        mesh=fine,
        in_specs=placed,
        out_specs=(P(every, None), P(), P(), P(), P(), P()),
        check_vma=False,
    )
```

time: 119 us -> 108 us (0.908)
  waiting for transfers between devices: 22 us -> 15.4 us
  starting transfers between devices: 67.8 us -> 62.6 us
  Pallas kernels: 22 us -> 23.2 us
    all_to_all x5 -> x4, waiting for transfers between devices: 22 us -> 11.5 us  [exchange(): return lax.all_to_all(x, axes, 0, 0, tiled=True)]
    ppermute x4, starting transfers between devices: 24 us -> 18.9 us  [shifted(): lax.ppermute(x, axes, [(i, (i + by) % length) for i in range(length)])]
    ppermute x6 -> x4, starting transfers between devices: 14.7 us -> 9.87 us  [swapped(): lax.ppermute(x, axes, [(i, i ^ mask) for i in range(lax.axis_size(axes))])]
    all_to_all x5 -> x4, starting transfers between devices: 29.1 us -> 33.8 us  [exchange(): return lax.all_to_all(x, axes, 0, 0, tiled=True)]
    ppermute x6 -> x4, waiting for transfers between devices: 0.02 us -> 2.16 us  [swapped(): lax.ppermute(x, axes, [(i, i ^ mask) for i in range(lax.axis_size(axes))])]
    ppermute x4, waiting for transfers between devices: 0.01 us -> 1.74 us  [shifted(): lax.ppermute(x, axes, [(i, (i + by) % length) for i in range(length)])]
    pallas_call x9, Pallas kernels: 22 us -> 23.2 us  [call(): pl.pallas_call(body, out_shape=tuple((jax.ShapeDtypeStruct(shape, dtype)...]
  transfers between devices with their start and end apart: 15 -> 12, of which waited for: 4 -> 5; matrix products, arithmetic and copies ran while one was open for 1% -> 1% of each run, Pallas kernels for 16% -> 13%
where the time goes in v3:
time: 108 us; the launch traced here: 107 us
  starting transfers between devices  62.6 us (58%)
  Pallas kernels  23.2 us (21%)
  waiting for transfers between devices  15.4 us (14%)
  local copies, waits for them, and re-layouts  3.42 us (3%)
  between operations  2.12 us (2%)
    all_to_all x4, starting transfers between devices, exchange(): return lax.all_to_all(x, axes, 0, 0, tiled=True)  33.8 us
    pallas_call x9, Pallas kernels, call(): pl.pallas_call(body, out_shape=tuple((jax.ShapeDtypeStruct(shape, dtype)...  23.2 us
    ppermute x4, starting transfers between devices, shifted(): lax.ppermute(x, axes, [(i, (i + by) % length) for i in range(length)])  18.9 us
    all_to_all x4, waiting for transfers between devices, exchange(): return lax.all_to_all(x, axes, 0, 0, tiled=True)  11.5 us
    ppermute x4, starting transfers between devices, swapped(): lax.ppermute(x, axes, [(i, i ^ mask) for i in range(lax.axis_size(axes))])  9.87 us
    unnamed x12, local copies, waits for them, and re-layouts  2.51 us
    ppermute x4, waiting for transfers between devices, swapped(): lax.ppermute(x, axes, [(i, i ^ mask) for i in range(lax.axis_size(axes))])  2.16 us
  transfers between devices with their start and end apart: 12, of which 5 were waited for; matrix products, arithmetic and copies ran while one was open for 1% of the time, Pallas kernels for 13%

profile of v3, /device:TPU:1, one launch (start us, length us, event | category | flops | bytes accessed | tf_op | source)
XLA Modules:
  0.0 106.8 jit_solution(17057838701926176692)
XLA Ops:
  1.3 2.3 %shard_map.218 = (bf16[16,6528]{1,0:T(8,128)(2,1)}, bf16[16,6528]{1,0:T(8,128)(2,1)}, bf16[4,416,128]{2,1,0:T(8,128)(2,1)}) custom-call(s32[1]{0:T(128)S(6)} %copy.24.count_ref, s32[1,2,16]{2,1,0:T(2,128)} %lists_hbm.1, bf16[32,6272]{1,0:T(8,128)(2,1)} %refs_0_.1, bf16[32,256]{1,0:T(8,128)(2,1)} %refs_4_.2, bf16[224,896]{1,0:T(8,128)(2,1)} %m0_hbm.3, ...), custom_call_target="tpu_custom_call" | custom-call | bytes 4096 | tf_op jit(solution)/shard_map/pallas_call | solution.py:373
  3.6 10.3 %all-to-all-start = ((bf16[4,416,128]{2,1,0:T(8,128)(2,1)}), bf16[4,416,128]{2,1,0:T(8,128)(2,1)S(1)}, u32[]{:S(2)}, u32[]{:S(2)}) async-start(bf16[4,416,128]{2,1,0:T(8,128)(2,1)} %get-tuple-element.31), calls=%async_computation | async-start | bytes 851968 | tf_op jit(solution)/shard_map/all_to_all | solution.py:398
  13.9 1.9 %collective-permute-start = (bf16[16,6528]{1,0:T(8,128)(2,1)}, bf16[16,6528]{1,0:T(8,128)(2,1)S(1)}, u32[]{:S(2)}, u32[]{:S(2)}) collective-permute-start(bf16[16,6528]{1,0:T(8,128)(2,1)} %get-tuple-element.32), channel_id=1, source_target_pairs={{0,4},{4,8},{8,12},{12,16},{16,20},{20,24},{24,28},{28,32},{32,36}... | collective-permute-start | bytes 626696 | tf_op jit(solution)/shard_map/ppermute | solution.py:390
  15.8 10.6 %collective-permute-start.1 = (bf16[16,6528]{1,0:T(8,128)(2,1)}, bf16[16,6528]{1,0:T(8,128)(2,1)S(1)}, u32[]{:S(2)}, u32[]{:S(2)}) collective-permute-start(bf16[16,6528]{1,0:T(8,128)(2,1)} %get-tuple-element.33), channel_id=1, source_target_pairs={{0,508},{4,0},{8,4},{12,8},{16,12},{20,16},{24,20},{28,24},{32,28}... | collective-permute-start | bytes 626696 | tf_op jit(solution)/shard_map/ppermute | solution.py:390
  27.0 2.4 %shard_map.217 = (bf16[2720,128]{1,0:T(8,128)(2,1)}, bf16[2752,128]{1,0:T(8,128)(2,1)}) custom-call(bf16[224,896]{1,0:T(8,128)(2,1)} %m0_hbm.3, bf16[2,192,768]{2,1,0:T(8,128)(2,1)} %m1_hbm.1, bf16[2,160,640]{2,1,0:T(8,128)(2,1)} %m2_hbm.1), custom_call_target="tpu_custom_call" | custom-call | flops 1073741824 | bytes 4096 | tf_op jit(solution)/shard_map/pallas_call | solution.py:373
  29.5 0.7 collective-permute-done.refs_1_
  30.1 1.1 %collective-permute-done.1.refs_2_ = bf16[16,6528]{1,0:T(8,128)(2,1)S(1)} collective-permute-done((bf16[16,6528]{1,0:T(8,128)(2,1)}, bf16[16,6528]{1,0:T(8,128)(2,1)S(1)}, u32[]{:S(2)}, u32[]{:S(2)}) %collective-permute-start.1) | collective-permute-done | bytes 208928 | tf_op jit(solution)/shard_map/ppermute | solution.py:390
  31.2 0.0 all-to-all-done.refs_0_
  31.2 0.7 copy-done.5
  31.9 0.8 copy-done.3
  32.7 5.9 %shard_map.219.refs_8_ = bf16[32,32,256]{2,1,0:T(8,128)(2,1)} custom-call(s32[1]{0:T(128)S(6)} %copy.25.atoms_ref, s32[1]{0:T(128)} %bitcast.rep_ref, bf16[4,416,128]{2,1,0:T(8,128)(2,1)} %copy-done.3, bf16[16,6528]{1,0:T(8,128)(2,1)} %copy-done.4, bf16[16,6528]{1,0:T(8,128)(2,1)} %copy-done.5, bf16[32,6272]{1,0:T(8,128)(2,1)} %refs_0_.1, ...), custom_call_target="tpu_custom_call" | custom-call | flops 2147483648 | bytes 4096 | tf_op jit(solution)/shard_map/pallas_call | solution.py:373
  38.6 4.5 %all-to-all-start.1 = ((bf16[32,32,256]{2,1,0:T(8,128)(2,1)}), bf16[32,32,256]{2,1,0:T(8,128)(2,1)S(1)}, u32[]{:S(2)}, u32[]{:S(2)}) async-start(bf16[32,32,256]{2,1,0:T(8,128)(2,1)} %shard_map.219.refs_8_), calls=%async_computation.1 | async-start | bytes 1048576 | tf_op jit(solution)/shard_map/all_to_all | solution.py:398
  43.1 4.5 %collective-permute-start.4 = (bf16[2752,128]{1,0:T(8,128)(2,1)S(1)}, bf16[2752,128]{1,0:T(8,128)(2,1)S(1)}, u32[]{:S(2)}, u32[]{:S(2)}) collective-permute-start(bf16[2752,128]{1,0:T(8,128)(2,1)S(1)} %copy-done), channel_id=1, source_target_pairs={{0,6},{2,0},{4,2},{6,4},{1,7},{3,1},{5,3},{7,5},{8,14},{10,8},{12,... | collective-permute-start | bytes 2113544 | tf_op jit(solution)/shard_map/ppermute | solution.py:390
  47.7 1.9 %collective-permute-start.3 = (bf16[2720,128]{1,0:T(8,128)(2,1)S(1)}, bf16[2720,128]{1,0:T(8,128)(2,1)}, u32[]{:S(2)}, u32[]{:S(2)}) collective-permute-start(bf16[2720,128]{1,0:T(8,128)(2,1)S(1)} %copy-done.1), channel_id=1, source_target_pairs={{0,2},{2,4},{4,6},{6,0},{1,3},{3,5},{5,7},{7,1},{8,10},{10,12},{12... | collective-permute-start | bytes 2088968 | tf_op jit(solution)/shard_map/ppermute | solution.py:390
  49.6 3.7 %shard_map.220 = (bf16[2096,128]{1,0:T(8,128)(2,1)}, bf16[2096,128]{1,0:T(8,128)(2,1)}) custom-call(s32[1]{0:T(128)S(6)} %copy.24.count_ref, s32[1]{0:T(128)} %bitcast.rep_ref, bf16[32,6272]{1,0:T(8,128)(2,1)} %refs_0_.1, bf16[16,6528]{1,0:T(8,128)(2,1)} %copy-done.4, bf16[16,6528]{1,0:T(8,128)(2,1)} %copy-done.5, bf16[235,128]{1,0:T(8,128)(2,1)} %refs_3_.3, ...), custom_call_target="tpu_custom_call" | custom-call | flops 2147483648 | bytes 4096 | tf_op jit(solution)/shard_map/pallas_call | solution.py:373
  53.4 1.5 %all-to-all-done.1.parts_ref = bf16[32,32,256]{2,1,0:T(8,128)(2,1)S(1)} async-done(((bf16[32,32,256]{2,1,0:T(8,128)(2,1)}), bf16[32,32,256]{2,1,0:T(8,128)(2,1)S(1)}, u32[]{:S(2)}, u32[]{:S(2)}) %all-to-all-start.1) | async-done | bytes 524320 | tf_op jit(solution)/shard_map/all_to_all | solution.py:398
  54.9 0.8 shard_map.221.after_ref
  55.7 12.6 %all-to-all-start.2 = ((bf16[16,32,256]{2,1,0:T(8,128)(2,1)}), bf16[16,32,256]{2,1,0:T(8,128)(2,1)S(1)}, u32[]{:S(2)}, u32[]{:S(2)}) async-start(bf16[16,32,256]{2,1,0:T(8,128)(2,1)} %shard_map.221.after_ref), calls=%async_computation.2 | async-start | bytes 524288 | tf_op jit(solution)/shard_map/all_to_all | solution.py:398
  68.3 2.0 %collective-permute-start.2 = (bf16[2096,128]{1,0:T(8,128)(2,1)}, bf16[2096,128]{1,0:T(8,128)(2,1)}, u32[]{:S(2)}, u32[]{:S(2)}) collective-permute-start(bf16[2096,128]{1,0:T(8,128)(2,1)} %get-tuple-element.38), channel_id=1, source_target_pairs={{0,1},{1,0},{2,3},{3,2},{4,5},{5,4},{6,7},{7,6},{8,9},{9,8},{10,11... | collective-permute-start | bytes 1609736 | tf_op jit(solution)/shard_map/ppermute | solution.py:394
  70.3 2.2 %collective-permute-done.2.got_ref = bf16[2096,128]{1,0:T(8,128)(2,1)} collective-permute-done((bf16[2096,128]{1,0:T(8,128)(2,1)}, bf16[2096,128]{1,0:T(8,128)(2,1)}, u32[]{:S(2)}, u32[]{:S(2)}) %collective-permute-start.2) | collective-permute-done | bytes 536608 | tf_op jit(solution)/shard_map/ppermute | solution.py:394
  72.5 1.0 copy-done.2
  73.5 5.5 %shard_map.222 = (f32[8,6272]{1,0:T(8,128)S(1)}, bf16[8,6272]{1,0:T(8,128)(2,1)S(1)}, bf16[8,6272]{1,0:T(8,128)(2,1)S(1)}, bf16[8,6272]{1,0:T(8,128)(2,1)S(1)}) custom-call(s32[1]{0:T(128)} %bitcast.rep_ref, bf16[2096,128]{1,0:T(8,128)(2,1)S(1)} %copy-done.2, bf16[2096,128]{1,0:T(8,128)(2,1)} %collective-permute-done.2.got_ref, ...), custom_call_target="tpu_custom_call" | custom-call | flops 4294967296 | bytes 4096 | tf_op jit(solution)/shard_map/pallas_call | solution.py:373
  79.1 2.1 %collective-permute-start.5 = (bf16[8,6272]{1,0:T(8,128)(2,1)S(1)}, bf16[8,6272]{1,0:T(8,128)(2,1)S(1)}, u32[]{:S(2)}, u32[]{:S(2)}) collective-permute-start(bf16[8,6272]{1,0:T(8,128)(2,1)S(1)} %get-tuple-element.43), channel_id=1, source_target_pairs={{0,1},{1,0},{2,3},{3,2},{4,5},{5,4},{6,7},{7,6},{8,9},{9,8},{10,11... | collective-permute-start | bytes 301064 | tf_op jit(solution)/shard_map/ppermute | solution.py:394
  81.1 2.3 %collective-permute-start.6 = (bf16[8,6272]{1,0:T(8,128)(2,1)S(1)}, bf16[8,6272]{1,0:T(8,128)(2,1)S(1)}, u32[]{:S(2)}, u32[]{:S(2)}) collective-permute-start(bf16[8,6272]{1,0:T(8,128)(2,1)S(1)} %get-tuple-element.44), channel_id=1, source_target_pairs={{0,2},{1,3},{2,0},{3,1},{4,6},{5,7},{6,4},{7,5},{8,10},{9,11},{10,... | collective-permute-start | bytes 301064 | tf_op jit(solution)/shard_map/ppermute | solution.py:394
  83.4 3.5 %collective-permute-start.7 = (bf16[8,6272]{1,0:T(8,128)(2,1)S(1)}, bf16[8,6272]{1,0:T(8,128)(2,1)S(1)}, u32[]{:S(2)}, u32[]{:S(2)}) collective-permute-start(bf16[8,6272]{1,0:T(8,128)(2,1)S(1)} %get-tuple-element.45), channel_id=1, source_target_pairs={{0,3},{1,2},{2,1},{3,0},{4,7},{5,6},{6,5},{7,4},{8,11},{9,10},{10,... | collective-permute-start | bytes 301064 | tf_op jit(solution)/shard_map/ppermute | solution.py:394
  87.0 0.9 shard_map.224
  87.8 6.3 %all-to-all-start.3 = ((bf16[32,32,256]{2,1,0:T(8,128)(2,1)}), bf16[32,32,256]{2,1,0:T(8,128)(2,1)S(1)}, u32[]{:S(2)}, u32[]{:S(2)}) async-start(bf16[32,32,256]{2,1,0:T(8,128)(2,1)} %shard_map.224), calls=%async_computation.3 | async-start | bytes 1048576 | tf_op jit(solution)/shard_map/all_to_all | solution.py:398
  94.2 0.9 constant_dynamic-slice_fusion.own_ref
  95.1 0.0 collective-permute-done.5.s1_ref
  95.1 0.7 shard_map.223
  95.8 10.0 %all-to-all-done.3.all_ref = bf16[32,32,256]{2,1,0:T(8,128)(2,1)S(1)} async-done(((bf16[32,32,256]{2,1,0:T(8,128)(2,1)}), bf16[32,32,256]{2,1,0:T(8,128)(2,1)S(1)}, u32[]{:S(2)}, u32[]{:S(2)}) %all-to-all-start.3) | async-done | bytes 524320 | tf_op jit(solution)/shard_map/all_to_all | solution.py:398
  105.8 1.0 shard_map.225
  (14 shorter events, 0.0 us)
Async XLA Ops:
  3.6 27.7 %all-to-all-start = ((bf16[4,416,128]{2,1,0:T(8,128)(2,1)}), bf16[4,416,128]{2,1,0:T(8,128)(2,1)S(1)}, u32[]{:S(2)}, u32[]{:S(2)}) async-start(bf16[4,416,128]{2,1,0:T(8,128)(2,1)} %get-tuple-element.31), calls=%async_computation | async-start | bytes 851968 | tf_op jit(solution)/shard_map/all_to_all | solution.py:398
  13.9 16.3 %collective-permute-start = (bf16[16,6528]{1,0:T(8,128)(2,1)}, bf16[16,6528]{1,0:T(8,128)(2,1)S(1)}, u32[]{:S(2)}, u32[]{:S(2)}) collective-permute-start(bf16[16,6528]{1,0:T(8,128)(2,1)} %get-tuple-element.32), channel_id=1, source_target_pairs={{0,4},{4,8},{8,12},{12,16},{16,20},{20,24},{24,28},{28,32},{32,36}... | collective-permute-start | bytes 626696 | tf_op jit(solution)/shard_map/ppermute | solution.py:390
  15.8 15.4 %collective-permute-start.1 = (bf16[16,6528]{1,0:T(8,128)(2,1)}, bf16[16,6528]{1,0:T(8,128)(2,1)S(1)}, u32[]{:S(2)}, u32[]{:S(2)}) collective-permute-start(bf16[16,6528]{1,0:T(8,128)(2,1)} %get-tuple-element.33), channel_id=1, source_target_pairs={{0,508},{4,0},{8,4},{12,8},{16,12},{20,16},{24,20},{28,24},{32,28}... | collective-permute-start | bytes 626696 | tf_op jit(solution)/shard_map/ppermute | solution.py:390
  30.1 2.5 %copy-start.4 = (bf16[16,6528]{1,0:T(8,128)(2,1)}, bf16[16,6528]{1,0:T(8,128)(2,1)S(1)}, u32[]{:S(2)}) copy-start(bf16[16,6528]{1,0:T(8,128)(2,1)S(1)} %collective-permute-done.refs_1_) | copy-start | bytes 626692
  31.2 0.7 copy-start.5
  31.9 0.8 copy-start.3
  32.7 15.0 %copy-start.1 = (bf16[2720,128]{1,0:T(8,128)(2,1)S(1)}, bf16[2720,128]{1,0:T(8,128)(2,1)}, u32[]{:S(2)}) copy-start(bf16[2720,128]{1,0:T(8,128)(2,1)} %get-tuple-element.39.low_ref) | copy-start | bytes 2088964
  38.6 4.5 %copy-start = (bf16[2752,128]{1,0:T(8,128)(2,1)S(1)}, bf16[2752,128]{1,0:T(8,128)(2,1)}, u32[]{:S(2)}) copy-start(bf16[2752,128]{1,0:T(8,128)(2,1)} %get-tuple-element.40.high_ref) | copy-start | bytes 2113540
  38.6 16.3 %all-to-all-start.1 = ((bf16[32,32,256]{2,1,0:T(8,128)(2,1)}), bf16[32,32,256]{2,1,0:T(8,128)(2,1)S(1)}, u32[]{:S(2)}, u32[]{:S(2)}) async-start(bf16[32,32,256]{2,1,0:T(8,128)(2,1)} %shard_map.219.refs_8_), calls=%async_computation.1 | async-start | bytes 1048576 | tf_op jit(solution)/shard_map/all_to_all | solution.py:398
  43.1 29.3 %collective-permute-start.4 = (bf16[2752,128]{1,0:T(8,128)(2,1)S(1)}, bf16[2752,128]{1,0:T(8,128)(2,1)S(1)}, u32[]{:S(2)}, u32[]{:S(2)}) collective-permute-start(bf16[2752,128]{1,0:T(8,128)(2,1)S(1)} %copy-done), channel_id=1, source_target_pairs={{0,6},{2,0},{4,2},{6,4},{1,7},{3,1},{5,3},{7,5},{8,14},{10,8},{12,... | collective-permute-start | bytes 2113544 | tf_op jit(solution)/shard_map/ppermute | solution.py:390
  47.7 24.8 %collective-permute-start.3 = (bf16[2720,128]{1,0:T(8,128)(2,1)S(1)}, bf16[2720,128]{1,0:T(8,128)(2,1)}, u32[]{:S(2)}, u32[]{:S(2)}) collective-permute-start(bf16[2720,128]{1,0:T(8,128)(2,1)S(1)} %copy-done.1), channel_id=1, source_target_pairs={{0,2},{2,4},{4,6},{6,0},{1,3},{3,5},{5,7},{7,1},{8,10},{10,12},{12... | collective-permute-start | bytes 2088968 | tf_op jit(solution)/shard_map/ppermute | solution.py:390
  55.7 31.3 %all-to-all-start.2 = ((bf16[16,32,256]{2,1,0:T(8,128)(2,1)}), bf16[16,32,256]{2,1,0:T(8,128)(2,1)S(1)}, u32[]{:S(2)}, u32[]{:S(2)}) async-start(bf16[16,32,256]{2,1,0:T(8,128)(2,1)} %shard_map.221.after_ref), calls=%async_computation.2 | async-start | bytes 524288 | tf_op jit(solution)/shard_map/all_to_all | solution.py:398
  68.3 4.2 %collective-permute-start.2 = (bf16[2096,128]{1,0:T(8,128)(2,1)}, bf16[2096,128]{1,0:T(8,128)(2,1)}, u32[]{:S(2)}, u32[]{:S(2)}) collective-permute-start(bf16[2096,128]{1,0:T(8,128)(2,1)} %get-tuple-element.38), channel_id=1, source_target_pairs={{0,1},{1,0},{2,3},{3,2},{4,5},{5,4},{6,7},{7,6},{8,9},{9,8},{10,11... | collective-permute-start | bytes 1609736 | tf_op jit(solution)/shard_map/ppermute | solution.py:394
  72.5 1.0 copy-start.2
  79.1 16.0 %collective-permute-start.5 = (bf16[8,6272]{1,0:T(8,128)(2,1)S(1)}, bf16[8,6272]{1,0:T(8,128)(2,1)S(1)}, u32[]{:S(2)}, u32[]{:S(2)}) collective-permute-start(bf16[8,6272]{1,0:T(8,128)(2,1)S(1)} %get-tuple-element.43), channel_id=1, source_target_pairs={{0,1},{1,0},{2,3},{3,2},{4,5},{5,4},{6,7},{7,6},{8,9},{9,8},{10,11... | collective-permute-start | bytes 301064 | tf_op jit(solution)/shard_map/ppermute | solution.py:394
  81.1 14.0 %collective-permute-start.6 = (bf16[8,6272]{1,0:T(8,128)(2,1)S(1)}, bf16[8,6272]{1,0:T(8,128)(2,1)S(1)}, u32[]{:S(2)}, u32[]{:S(2)}) collective-permute-start(bf16[8,6272]{1,0:T(8,128)(2,1)S(1)} %get-tuple-element.44), channel_id=1, source_target_pairs={{0,2},{1,3},{2,0},{3,1},{4,6},{5,7},{6,4},{7,5},{8,10},{9,11},{10,... | collective-permute-start | bytes 301064 | tf_op jit(solution)/shard_map/ppermute | solution.py:394
  83.4 11.7 %collective-permute-start.7 = (bf16[8,6272]{1,0:T(8,128)(2,1)S(1)}, bf16[8,6272]{1,0:T(8,128)(2,1)S(1)}, u32[]{:S(2)}, u32[]{:S(2)}) collective-permute-start(bf16[8,6272]{1,0:T(8,128)(2,1)S(1)} %get-tuple-element.45), channel_id=1, source_target_pairs={{0,3},{1,2},{2,1},{3,0},{4,7},{5,6},{6,5},{7,4},{8,11},{9,10},{10,... | collective-permute-start | bytes 301064 | tf_op jit(solution)/shard_map/ppermute | solution.py:394
  87.8 18.0 %all-to-all-start.3 = ((bf16[32,32,256]{2,1,0:T(8,128)(2,1)}), bf16[32,32,256]{2,1,0:T(8,128)(2,1)S(1)}, u32[]{:S(2)}, u32[]{:S(2)}) async-start(bf16[32,32,256]{2,1,0:T(8,128)(2,1)} %shard_map.224), calls=%async_computation.3 | async-start | bytes 1048576 | tf_op jit(solution)/shard_map/all_to_all | solution.py:398

commit v4 on v3

--- a/solution.py
+++ b/solution.py
@@ -142,22 +142,21 @@
         row += size
 
 
-def early_body(inv_atoms, atoms_ref, rep_ref, *refs):
-    raw = refs[:11]
-    grad_ref = refs[11]
-    held = refs[12:23]
-    turn_ref, rotated_ref, hidden_ref, ssrc_ref, sdst_ref, target_ref, sems = refs[23:]
+def early_body(inv_atoms, atoms_ref, rep_ref, meta_ref, left_ref, right_ref, *refs):
+    raw = refs[:8]
+    grad_ref = refs[8]
+    held = refs[9:17]
+    turn_ref, rotated_ref, hidden_ref, ssrc_ref, sdst_ref, target_ref, sems = refs[17:]
     (
-        meta_ref, left_ref, right_ref, teacher_ref, student_ref, radial_ref, wsrc_ref, wdst_ref,
-        wrad_ref, wout_ref, whead_ref,
+        radial_ref, teacher_ref, student_ref, wsrc_ref, wdst_ref, wrad_ref, wout_ref, whead_ref,
     ) = held
-    for copy in fetch(tuple(zip(raw, held)), sems):
-        copy.wait()
+    copies = fetch(tuple(zip(raw, held)), sems)
     every = 4 * EDGE
     edges = [meta_ref[q, 352:416].astype(F32) for q in range(4)]
     ext_rows = lax.broadcasted_iota(jnp.int32, (EXT, EDGE), 0).astype(F32)
     sources = [(edges[q][49:50] == ext_rows).astype(F32) for q in range(4)]
     targets = [(edges[q][50:51] == ext_rows[:OWN]).astype(F32) for q in range(4)]
+    copies[0].wait()
     gains = jnp.concatenate(
         [gain_of(meta_ref[q, 224:352], radial_ref[...]) for q in range(4)], axis=1
     )
@@ -169,13 +168,17 @@
                 turn_ref[j * EXT : (j + 1) * EXT, q * EDGE : (q + 1) * EDGE] = (
                     sources[q] * edges[q][row : row + 1]
                 ).astype(BF)
+        if degree == 0:
+            copies[1].wait()
         stacked = coefficients((teacher_ref, left_ref, right_ref), degree)
         turned = dot(stacked, turn_ref[: span * EXT], ((0,), (0,)))
         rotated_ref[degree * C : (degree + 1) * C] = (turned * gains).astype(BF)
     column = jnp.concatenate([meta_ref[q, :224] for q in range(4)], axis=0)
-    invariant = dot(rotated_ref[...], column, ((0,), (0,))).astype(BF)
+    invariant = dot(column, rotated_ref[...], ((0,), (0,))).astype(BF)
     scatter = jnp.concatenate([targets[q] * edges[q][0:1] for q in range(4)], axis=1).astype(BF)
-    invariants = dot(scatter, invariant)
+    invariants = dot(scatter, invariant, ((1,), (1,)))
+    for copy in copies[2:]:
+        copy.wait()
     student_ext = jnp.concatenate(
         [student_ref[...], left_ref[:, KC:], right_ref[:, KC:]], axis=0
     )
@@ -224,12 +227,12 @@
         grad_ref[start // high : stop // high] = value.astype(BF).reshape(-1, high, SW)
 
 
-def rotate_body(count_ref, rep_ref, *refs):
-    raw = refs[:8]
-    after_ref, keep_ref, give_ref = refs[8:11]
-    held = refs[11:19]
-    pack_ref, wigf_ref, turn_ref, sems = refs[19:]
-    teacher_ref, left_ref, right_ref, wig_ref, basis_ref, radial_ref, src_ref, dst_ref = held
+def rotate_body(count_ref, rep_ref, left_ref, right_ref, *refs):
+    raw = refs[:6]
+    after_ref, keep_ref, give_ref = refs[6:9]
+    held = refs[9:15]
+    pack_ref, wigf_ref, turn_ref, sems = refs[15:]
+    teacher_ref, wig_ref, basis_ref, radial_ref, src_ref, dst_ref = held
     for copy in fetch(tuple(zip(raw, held)), sems):
         copy.wait()
     rep = rep_ref[0]
@@ -440,43 +443,40 @@
         room=1024,
     )
     raw = (
-        meta, from_left, from_right, teacher_in, student_in, teacher_radial, w_src, w_dst,
-        w_radial, w_out, w_head,
+        teacher_radial, teacher_in, student_in, w_src, w_dst, w_radial, w_out, w_head
     )
     (grads,) = call(
         functools.partial(early_body, 1.0 / (OWN * bricks)),
         [((plane, chunk, SW), BF)],
-        (atom_count, rep1, *raw),
+        (atom_count, rep1, meta, from_left, from_right, *raw),
         held(raw)
         + [
             pltpu.VMEM((13 * EXT, 4 * EDGE), BF), pltpu.VMEM((896, 4 * EDGE), BF),
             pltpu.VMEM((4 * EDGE, SW), F32), pltpu.VMEM((4 * EDGE, SW), BF),
             pltpu.VMEM((4 * EDGE, SW), BF), pltpu.VMEM((4, OWN, EDGE), BF),
-            pltpu.SemaphoreType.DMA((11,)),
+            pltpu.SemaphoreType.DMA((8,)),
         ],
         scalars=2,
-        raws=11,
+        raws=8,
         flops=1 << 31,
-        room=1024,
+        room=2048,
     )
     low, high, grads = lax.optimization_barrier((low, high, grads))
     across_low = shifted(low, ("yh", "yl"), 1)
     across_high = shifted(high, ("yh", "yl"), -1)
     plane_parts = exchange(grads, PLANE)
-    raw = (
-        teacher_in, from_left, from_right, wigner, edge_basis, teacher_radial, src_row, dst_row
-    )
+    raw = (teacher_in, wigner, edge_basis, teacher_radial, src_row, dst_row)
     keep, give = call(
         rotate_body,
         [((1856 + 240, EDGE), BF)] * 2,
-        (edge_count, rep1, *raw, grads),
+        (edge_count, rep1, from_left, from_right, *raw, grads),
         held(raw)
         + [
             pltpu.VMEM((4, 928, EDGE), BF), pltpu.VMEM((240, EDGE), F32),
-            pltpu.VMEM((13 * EXT, 5 * EDGE), BF), pltpu.SemaphoreType.DMA((8,)),
+            pltpu.VMEM((13 * EXT, 5 * EDGE), BF), pltpu.SemaphoreType.DMA((6,)),
         ],
         scalars=2,
-        raws=8,
+        raws=6,
         after=1,
         flops=1 << 31,
         room=4096,
@@ -500,9 +500,11 @@
     line_parts = exchange(plane_sum, "z")
     line_parts, share = lax.optimization_barrier((line_parts, shares[0]))
     (total,) = call(spread_body, [((plane, chunk, SW), BF)], (line_parts,))
-    arrived = [share] + [swapped(shares[k], REP, k) for k in (1, 2, 3)]
+    total, *rest = lax.optimization_barrier((total, *shares[1:]))
+    arrived = [share] + [swapped(rest[k - 1], REP, k) for k in (1, 2, 3)]
     totals = exchange(total, PLANE)
-    arrived = [share] + [swapped(shares[k], REP, k) for k in (1, 2, 3)]
+    total, *rest = lax.optimization_barrier((total, *shares[1:]))
+    arrived = [share] + [swapped(rest[k - 1], REP, k) for k in (1, 2, 3)]
     mine = lax.dynamic_slice_in_dim(teacher_in, rep * 8, 8, 0)
     (teacher_out,) = call(finish_body, [((8, KC), BF)], (mine, *arrived))
     grads_out = call(

time: 108 us -> 111 us (1.028)
  starting transfers between devices: 62.6 us -> 67.9 us
  waiting for transfers between devices: 15.4 us -> 11.8 us
  Pallas kernels: 23.2 us -> 24.4 us
    all_to_all x4, waiting for transfers between devices: 11.5 us -> 3.94 us  [exchange(): return lax.all_to_all(x, axes, 0, 0, tiled=True)]
    all_to_all x4, starting transfers between devices: 33.8 us -> 38.9 us  [exchange(): return lax.all_to_all(x, axes, 0, 0, tiled=True)]
    ppermute x4, waiting for transfers between devices: 2.16 us -> 6.15 us  [swapped(): lax.ppermute(x, axes, [(i, i ^ mask) for i in range(lax.axis_size(axes))])]
    pallas_call x9, Pallas kernels: 23.2 us -> 24.4 us  [call(): pl.pallas_call(body, out_shape=tuple((jax.ShapeDtypeStruct(shape, dtype)...]
    unnamed x12 -> x24, local copies, waits for them, and re-layouts: 2.51 us -> 2.55 us
  transfers between devices with their start and end apart: 12 -> 12, of which waited for: 5 -> 7; matrix products, arithmetic and copies ran while one was open for 1% -> 1% of each run, Pallas kernels for 13% -> 13%
where the time goes in v4:
time: 111 us; the launch traced here: 110 us
  starting transfers between devices  67.9 us (61%)
  Pallas kernels  24.4 us (22%)
  waiting for transfers between devices  11.8 us (11%)
  local copies, waits for them, and re-layouts  3.46 us (3%)
  between operations  2.15 us (2%)
    all_to_all x4, starting transfers between devices, exchange(): return lax.all_to_all(x, axes, 0, 0, tiled=True)  38.9 us
    pallas_call x9, Pallas kernels, call(): pl.pallas_call(body, out_shape=tuple((jax.ShapeDtypeStruct(shape, dtype)...  24.4 us
    ppermute x4, starting transfers between devices, shifted(): lax.ppermute(x, axes, [(i, (i + by) % length) for i in range(length)])  18.9 us
    ppermute x4, starting transfers between devices, swapped(): lax.ppermute(x, axes, [(i, i ^ mask) for i in range(lax.axis_size(axes))])  10.1 us
    ppermute x4, waiting for transfers between devices, swapped(): lax.ppermute(x, axes, [(i, i ^ mask) for i in range(lax.axis_size(axes))])  6.15 us
    all_to_all x4, waiting for transfers between devices, exchange(): return lax.all_to_all(x, axes, 0, 0, tiled=True)  3.94 us
    unnamed x24, local copies, waits for them, and re-layouts  2.55 us
  transfers between devices with their start and end apart: 12, of which 7 were waited for; matrix products, arithmetic and copies ran while one was open for 1% of the time, Pallas kernels for 13%

profile of v4, /device:TPU:1, one launch (start us, length us, event | category | flops | bytes accessed | tf_op | source)
XLA Modules:
  0.0 109.8 jit_solution(6150735114827855191)
XLA Ops:
  1.3 2.3 %shard_map.218 = (bf16[16,6528]{1,0:T(8,128)(2,1)}, bf16[16,6528]{1,0:T(8,128)(2,1)}, bf16[4,416,128]{2,1,0:T(8,128)(2,1)}) custom-call(s32[1]{0:T(128)S(6)} %copy.24.count_ref, s32[1,2,16]{2,1,0:T(2,128)} %lists_hbm.1, bf16[32,6272]{1,0:T(8,128)(2,1)} %refs_0_.3, bf16[32,256]{1,0:T(8,128)(2,1)} %refs_2_.2, bf16[224,896]{1,0:T(8,128)(2,1)} %m0_hbm.3, ...), custom_call_target="tpu_custom_call" | custom-call | bytes 4096 | tf_op jit(solution)/shard_map/pallas_call | solution.py:376
  3.6 10.3 %all-to-all-start = ((bf16[4,416,128]{2,1,0:T(8,128)(2,1)}), bf16[4,416,128]{2,1,0:T(8,128)(2,1)S(1)}, u32[]{:S(2)}, u32[]{:S(2)}) async-start(bf16[4,416,128]{2,1,0:T(8,128)(2,1)} %get-tuple-element.35), calls=%async_computation | async-start | bytes 851968 | tf_op jit(solution)/shard_map/all_to_all | solution.py:401
  13.9 1.9 %collective-permute-start = (bf16[16,6528]{1,0:T(8,128)(2,1)}, bf16[16,6528]{1,0:T(8,128)(2,1)S(1)}, u32[]{:S(2)}, u32[]{:S(2)}) collective-permute-start(bf16[16,6528]{1,0:T(8,128)(2,1)} %get-tuple-element.36), channel_id=1, source_target_pairs={{0,4},{4,8},{8,12},{12,16},{16,20},{20,24},{24,28},{28,32},{32,36}... | collective-permute-start | bytes 626696 | tf_op jit(solution)/shard_map/ppermute | solution.py:393
  15.8 10.6 %collective-permute-start.1 = (bf16[16,6528]{1,0:T(8,128)(2,1)}, bf16[16,6528]{1,0:T(8,128)(2,1)S(1)}, u32[]{:S(2)}, u32[]{:S(2)}) collective-permute-start(bf16[16,6528]{1,0:T(8,128)(2,1)} %get-tuple-element.37), channel_id=1, source_target_pairs={{0,508},{4,0},{8,4},{12,8},{16,12},{20,16},{24,20},{28,24},{32,28}... | collective-permute-start | bytes 626696 | tf_op jit(solution)/shard_map/ppermute | solution.py:393
  27.1 2.4 %shard_map.217 = (bf16[2720,128]{1,0:T(8,128)(2,1)}, bf16[2752,128]{1,0:T(8,128)(2,1)}) custom-call(bf16[224,896]{1,0:T(8,128)(2,1)} %m0_hbm.3, bf16[2,192,768]{2,1,0:T(8,128)(2,1)} %m1_hbm.1, bf16[2,160,640]{2,1,0:T(8,128)(2,1)} %m2_hbm.1), custom_call_target="tpu_custom_call" | custom-call | flops 1073741824 | bytes 4096 | tf_op jit(solution)/shard_map/pallas_call | solution.py:376
  29.5 0.7 collective-permute-done.left_ref
  30.2 1.1 collective-permute-done.1.right_ref
  31.3 0.7 copy-done.11
  32.1 6.4 %shard_map.219.refs_6_ = bf16[32,32,256]{2,1,0:T(8,128)(2,1)} custom-call(s32[1]{0:T(128)S(6)} %copy.25.atoms_ref, s32[1]{0:T(128)} %bitcast.rep_ref, bf16[4,416,128]{2,1,0:T(8,128)(2,1)} %copy-done.9, bf16[16,6528]{1,0:T(8,128)(2,1)} %copy-done.10, bf16[16,6528]{1,0:T(8,128)(2,1)} %copy-done.11, bf16[128,128]{1,0:T(8,128)(2,1)} %refs_3_.3, ...), custom_call_target="tpu_custom_call" | custom-call | flops 2147483648 | bytes 4096 | tf_op jit(solution)/shard_map/pallas_call | solution.py:376
  38.6 4.5 %all-to-all-start.1 = ((bf16[32,32,256]{2,1,0:T(8,128)(2,1)}), bf16[32,32,256]{2,1,0:T(8,128)(2,1)S(1)}, u32[]{:S(2)}, u32[]{:S(2)}) async-start(bf16[32,32,256]{2,1,0:T(8,128)(2,1)} %shard_map.219.refs_6_), calls=%async_computation.1 | async-start | bytes 1048576 | tf_op jit(solution)/shard_map/all_to_all | solution.py:401
  43.1 4.5 %collective-permute-start.4 = (bf16[2752,128]{1,0:T(8,128)(2,1)S(1)}, bf16[2752,128]{1,0:T(8,128)(2,1)S(1)}, u32[]{:S(2)}, u32[]{:S(2)}) collective-permute-start(bf16[2752,128]{1,0:T(8,128)(2,1)S(1)} %copy-done), channel_id=1, source_target_pairs={{0,6},{2,0},{4,2},{6,4},{1,7},{3,1},{5,3},{7,5},{8,14},{10,8},{12,... | collective-permute-start | bytes 2113544 | tf_op jit(solution)/shard_map/ppermute | solution.py:393
  47.7 1.9 %collective-permute-start.3 = (bf16[2720,128]{1,0:T(8,128)(2,1)S(1)}, bf16[2720,128]{1,0:T(8,128)(2,1)S(1)}, u32[]{:S(2)}, u32[]{:S(2)}) collective-permute-start(bf16[2720,128]{1,0:T(8,128)(2,1)S(1)} %copy-done.1), channel_id=1, source_target_pairs={{0,2},{2,4},{4,6},{6,0},{1,3},{3,5},{5,7},{7,1},{8,10},{10,12},{12... | collective-permute-start | bytes 2088968 | tf_op jit(solution)/shard_map/ppermute | solution.py:393
  49.6 4.6 %shard_map.220 = (bf16[2096,128]{1,0:T(8,128)(2,1)}, bf16[2096,128]{1,0:T(8,128)(2,1)}) custom-call(s32[1]{0:T(128)S(6)} %copy.24.count_ref, s32[1]{0:T(128)} %bitcast.rep_ref, bf16[16,6528]{1,0:T(8,128)(2,1)} %copy-done.10, bf16[16,6528]{1,0:T(8,128)(2,1)} %copy-done.11, bf16[32,6272]{1,0:T(8,128)(2,1)} %refs_0_.3, bf16[235,128]{1,0:T(8,128)(2,1)} %refs_1_.3, ...), custom_call_target="tpu_custom_call" | custom-call | flops 2147483648 | bytes 4096 | tf_op jit(solution)/shard_map/pallas_call | solution.py:376
  54.2 0.7 all-to-all-done.1.parts_ref
  54.9 0.8 shard_map.221.after_ref
  55.6 12.6 %all-to-all-start.2 = ((bf16[16,32,256]{2,1,0:T(8,128)(2,1)}), bf16[16,32,256]{2,1,0:T(8,128)(2,1)S(1)}, u32[]{:S(2)}, u32[]{:S(2)}) async-start(bf16[16,32,256]{2,1,0:T(8,128)(2,1)} %shard_map.221.after_ref), calls=%async_computation.2 | async-start | bytes 524288 | tf_op jit(solution)/shard_map/all_to_all | solution.py:401
  68.3 2.2 %collective-permute-start.2 = (bf16[2096,128]{1,0:T(8,128)(2,1)}, bf16[2096,128]{1,0:T(8,128)(2,1)}, u32[]{:S(2)}, u32[]{:S(2)}) collective-permute-start(bf16[2096,128]{1,0:T(8,128)(2,1)} %get-tuple-element.42), channel_id=1, source_target_pairs={{0,1},{1,0},{2,3},{3,2},{4,5},{5,4},{6,7},{7,6},{8,9},{9,8},{10,11... | collective-permute-start | bytes 1609736 | tf_op jit(solution)/shard_map/ppermute | solution.py:397
  70.5 1.9 %collective-permute-done.2.got_ref = bf16[2096,128]{1,0:T(8,128)(2,1)} collective-permute-done((bf16[2096,128]{1,0:T(8,128)(2,1)}, bf16[2096,128]{1,0:T(8,128)(2,1)}, u32[]{:S(2)}, u32[]{:S(2)}) %collective-permute-start.2) | collective-permute-done | bytes 536608 | tf_op jit(solution)/shard_map/ppermute | solution.py:397
  72.5 1.0 copy-done.8
  73.5 5.3 %shard_map.222 = (f32[8,6272]{1,0:T(8,128)S(1)}, bf16[8,6272]{1,0:T(8,128)(2,1)S(1)}, bf16[8,6272]{1,0:T(8,128)(2,1)S(1)}, bf16[8,6272]{1,0:T(8,128)(2,1)S(1)}) custom-call(s32[1]{0:T(128)} %bitcast.rep_ref, bf16[2096,128]{1,0:T(8,128)(2,1)S(1)} %copy-done.8, bf16[2096,128]{1,0:T(8,128)(2,1)} %collective-permute-done.2.got_ref, ...), custom_call_target="tpu_custom_call" | custom-call | flops 4294967296 | bytes 4096 | tf_op jit(solution)/shard_map/pallas_call | solution.py:376
  78.8 0.6 copy-done.6
  79.5 3.2 %all-to-all-done.2.parts_ref = bf16[16,32,256]{2,1,0:T(8,128)(2,1)S(1)} async-done(((bf16[16,32,256]{2,1,0:T(8,128)(2,1)}), bf16[16,32,256]{2,1,0:T(8,128)(2,1)S(1)}, u32[]{:S(2)}, u32[]{:S(2)}) %all-to-all-start.2) | async-done | bytes 262176 | tf_op jit(solution)/shard_map/all_to_all | solution.py:401
  82.7 0.9 shard_map.223
  83.6 11.4 %all-to-all-start.3 = ((bf16[32,32,256]{2,1,0:T(8,128)(2,1)}), bf16[32,32,256]{2,1,0:T(8,128)(2,1)S(1)}, u32[]{:S(2)}, u32[]{:S(2)}) async-start(bf16[32,32,256]{2,1,0:T(8,128)(2,1)} %shard_map.223), calls=%async_computation.3 | async-start | bytes 1048576 | tf_op jit(solution)/shard_map/all_to_all | solution.py:401
  95.0 2.1 %collective-permute-start.5 = (bf16[8,6272]{1,0:T(8,128)(2,1)S(1)}, bf16[8,6272]{1,0:T(8,128)(2,1)S(1)}, u32[]{:S(2)}, u32[]{:S(2)}) collective-permute-start(bf16[8,6272]{1,0:T(8,128)(2,1)S(1)} %copy-done.7), channel_id=1, source_target_pairs={{0,1},{1,0},{2,3},{3,2},{4,5},{5,4},{6,7},{7,6},{8,9},{9,8},{10,11... | collective-permute-start | bytes 301064 | tf_op jit(solution)/shard_map/ppermute | solution.py:397
  97.2 3.4 %collective-permute-start.6 = (bf16[8,6272]{1,0:T(8,128)(2,1)S(1)}, bf16[8,6272]{1,0:T(8,128)(2,1)S(1)}, u32[]{:S(2)}, u32[]{:S(2)}) collective-permute-start(bf16[8,6272]{1,0:T(8,128)(2,1)S(1)} %copy-done.5), channel_id=1, source_target_pairs={{0,2},{1,3},{2,0},{3,1},{4,6},{5,7},{6,4},{7,5},{8,10},{9,11},{10,... | collective-permute-start | bytes 301064 | tf_op jit(solution)/shard_map/ppermute | solution.py:397
  100.6 2.3 %collective-permute-start.7 = (bf16[8,6272]{1,0:T(8,128)(2,1)S(1)}, bf16[8,6272]{1,0:T(8,128)(2,1)S(1)}, u32[]{:S(2)}, u32[]{:S(2)}) collective-permute-start(bf16[8,6272]{1,0:T(8,128)(2,1)S(1)} %copy-done.3), channel_id=1, source_target_pairs={{0,3},{1,2},{2,1},{3,0},{4,7},{5,6},{6,5},{7,4},{8,11},{9,10},{10,... | collective-permute-start | bytes 301064 | tf_op jit(solution)/shard_map/ppermute | solution.py:397
  103.0 0.9 constant_dynamic-slice_fusion.own_ref
  103.9 1.9 %collective-permute-done.6.s2_ref = bf16[8,6272]{1,0:T(8,128)(2,1)S(1)} collective-permute-done((bf16[8,6272]{1,0:T(8,128)(2,1)S(1)}, bf16[8,6272]{1,0:T(8,128)(2,1)S(1)}, u32[]{:S(2)}, u32[]{:S(2)}) %collective-permute-start.6) | collective-permute-done | bytes 100384 | tf_op jit(solution)/shard_map/ppermute | solution.py:397
  105.8 2.3 %collective-permute-done.7.s3_ref = bf16[8,6272]{1,0:T(8,128)(2,1)S(1)} collective-permute-done((bf16[8,6272]{1,0:T(8,128)(2,1)S(1)}, bf16[8,6272]{1,0:T(8,128)(2,1)S(1)}, u32[]{:S(2)}, u32[]{:S(2)}) %collective-permute-start.7) | collective-permute-done | bytes 100384 | tf_op jit(solution)/shard_map/ppermute | solution.py:397
  108.1 0.7 shard_map.224
  108.8 1.0 shard_map.225
  (26 shorter events, 0.2 us)
Async XLA Ops:
  3.6 27.7 %all-to-all-start = ((bf16[4,416,128]{2,1,0:T(8,128)(2,1)}), bf16[4,416,128]{2,1,0:T(8,128)(2,1)S(1)}, u32[]{:S(2)}, u32[]{:S(2)}) async-start(bf16[4,416,128]{2,1,0:T(8,128)(2,1)} %get-tuple-element.35), calls=%async_computation | async-start | bytes 851968 | tf_op jit(solution)/shard_map/all_to_all | solution.py:401
  13.9 16.3 %collective-permute-start = (bf16[16,6528]{1,0:T(8,128)(2,1)}, bf16[16,6528]{1,0:T(8,128)(2,1)S(1)}, u32[]{:S(2)}, u32[]{:S(2)}) collective-permute-start(bf16[16,6528]{1,0:T(8,128)(2,1)} %get-tuple-element.36), channel_id=1, source_target_pairs={{0,4},{4,8},{8,12},{12,16},{16,20},{20,24},{24,28},{28,32},{32,36}... | collective-permute-start | bytes 626696 | tf_op jit(solution)/shard_map/ppermute | solution.py:393
  15.8 15.4 %collective-permute-start.1 = (bf16[16,6528]{1,0:T(8,128)(2,1)}, bf16[16,6528]{1,0:T(8,128)(2,1)S(1)}, u32[]{:S(2)}, u32[]{:S(2)}) collective-permute-start(bf16[16,6528]{1,0:T(8,128)(2,1)} %get-tuple-element.37), channel_id=1, source_target_pairs={{0,508},{4,0},{8,4},{12,8},{16,12},{20,16},{24,20},{28,24},{32,28}... | collective-permute-start | bytes 626696 | tf_op jit(solution)/shard_map/ppermute | solution.py:393
  30.2 1.1 copy-start.10
  31.2 0.7 copy-start.11
  31.3 0.8 copy-start.9
  32.1 15.6 %copy-start.1 = (bf16[2720,128]{1,0:T(8,128)(2,1)S(1)}, bf16[2720,128]{1,0:T(8,128)(2,1)}, u32[]{:S(2)}) copy-start(bf16[2720,128]{1,0:T(8,128)(2,1)} %get-tuple-element.43.low_ref) | copy-start | bytes 2088964
  38.6 4.5 %copy-start = (bf16[2752,128]{1,0:T(8,128)(2,1)S(1)}, bf16[2752,128]{1,0:T(8,128)(2,1)}, u32[]{:S(2)}) copy-start(bf16[2752,128]{1,0:T(8,128)(2,1)} %get-tuple-element.44.high_ref) | copy-start | bytes 2113540
  38.6 16.3 %all-to-all-start.1 = ((bf16[32,32,256]{2,1,0:T(8,128)(2,1)}), bf16[32,32,256]{2,1,0:T(8,128)(2,1)S(1)}, u32[]{:S(2)}, u32[]{:S(2)}) async-start(bf16[32,32,256]{2,1,0:T(8,128)(2,1)} %shard_map.219.refs_6_), calls=%async_computation.1 | async-start | bytes 1048576 | tf_op jit(solution)/shard_map/all_to_all | solution.py:401
  43.1 29.3 %collective-permute-start.4 = (bf16[2752,128]{1,0:T(8,128)(2,1)S(1)}, bf16[2752,128]{1,0:T(8,128)(2,1)S(1)}, u32[]{:S(2)}, u32[]{:S(2)}) collective-permute-start(bf16[2752,128]{1,0:T(8,128)(2,1)S(1)} %copy-done), channel_id=1, source_target_pairs={{0,6},{2,0},{4,2},{6,4},{1,7},{3,1},{5,3},{7,5},{8,14},{10,8},{12,... | collective-permute-start | bytes 2113544 | tf_op jit(solution)/shard_map/ppermute | solution.py:393
  47.7 24.8 %collective-permute-start.3 = (bf16[2720,128]{1,0:T(8,128)(2,1)S(1)}, bf16[2720,128]{1,0:T(8,128)(2,1)S(1)}, u32[]{:S(2)}, u32[]{:S(2)}) collective-permute-start(bf16[2720,128]{1,0:T(8,128)(2,1)S(1)} %copy-done.1), channel_id=1, source_target_pairs={{0,2},{2,4},{4,6},{6,0},{1,3},{3,5},{5,7},{7,1},{8,10},{10,12},{12... | collective-permute-start | bytes 2088968 | tf_op jit(solution)/shard_map/ppermute | solution.py:393
  55.6 27.0 %all-to-all-start.2 = ((bf16[16,32,256]{2,1,0:T(8,128)(2,1)}), bf16[16,32,256]{2,1,0:T(8,128)(2,1)S(1)}, u32[]{:S(2)}, u32[]{:S(2)}) async-start(bf16[16,32,256]{2,1,0:T(8,128)(2,1)} %shard_map.221.after_ref), calls=%async_computation.2 | async-start | bytes 524288 | tf_op jit(solution)/shard_map/all_to_all | solution.py:401
  68.3 4.2 %collective-permute-start.2 = (bf16[2096,128]{1,0:T(8,128)(2,1)}, bf16[2096,128]{1,0:T(8,128)(2,1)}, u32[]{:S(2)}, u32[]{:S(2)}) collective-permute-start(bf16[2096,128]{1,0:T(8,128)(2,1)} %get-tuple-element.42), channel_id=1, source_target_pairs={{0,1},{1,0},{2,3},{3,2},{4,5},{5,4},{6,7},{7,6},{8,9},{9,8},{10,11... | collective-permute-start | bytes 1609736 | tf_op jit(solution)/shard_map/ppermute | solution.py:397
  72.5 1.0 copy-start.8
  78.8 0.6 copy-start.6
  79.4 4.1 %copy-start.2 = (bf16[8,6272]{1,0:T(8,128)(2,1)}, bf16[8,6272]{1,0:T(8,128)(2,1)S(1)}, u32[]{:S(2)}) copy-start(bf16[8,6272]{1,0:T(8,128)(2,1)S(1)} %get-tuple-element.54) | copy-start | bytes 301060
  79.5 4.1 %copy-start.4 = (bf16[8,6272]{1,0:T(8,128)(2,1)}, bf16[8,6272]{1,0:T(8,128)(2,1)S(1)}, u32[]{:S(2)}) copy-start(bf16[8,6272]{1,0:T(8,128)(2,1)S(1)} %get-tuple-element.53) | copy-start | bytes 301060
  83.6 11.4 %copy-start.7 = (bf16[8,6272]{1,0:T(8,128)(2,1)S(1)}, bf16[8,6272]{1,0:T(8,128)(2,1)}, u32[]{:S(2)}) copy-start(bf16[8,6272]{1,0:T(8,128)(2,1)} %copy-done.6) | copy-start | bytes 301060
  83.6 13.6 %copy-start.5 = (bf16[8,6272]{1,0:T(8,128)(2,1)S(1)}, bf16[8,6272]{1,0:T(8,128)(2,1)}, u32[]{:S(2)}) copy-start(bf16[8,6272]{1,0:T(8,128)(2,1)} %copy-done.4) | copy-start | bytes 301060
  83.6 17.0 %copy-start.3 = (bf16[8,6272]{1,0:T(8,128)(2,1)S(1)}, bf16[8,6272]{1,0:T(8,128)(2,1)}, u32[]{:S(2)}) copy-start(bf16[8,6272]{1,0:T(8,128)(2,1)} %copy-done.2) | copy-start | bytes 301060
  83.6 25.2 %all-to-all-start.3 = ((bf16[32,32,256]{2,1,0:T(8,128)(2,1)}), bf16[32,32,256]{2,1,0:T(8,128)(2,1)S(1)}, u32[]{:S(2)}, u32[]{:S(2)}) async-start(bf16[32,32,256]{2,1,0:T(8,128)(2,1)} %shard_map.223), calls=%async_computation.3 | async-start | bytes 1048576 | tf_op jit(solution)/shard_map/all_to_all | solution.py:401
  95.0 8.8 %collective-permute-start.5 = (bf16[8,6272]{1,0:T(8,128)(2,1)S(1)}, bf16[8,6272]{1,0:T(8,128)(2,1)S(1)}, u32[]{:S(2)}, u32[]{:S(2)}) collective-permute-start(bf16[8,6272]{1,0:T(8,128)(2,1)S(1)} %copy-done.7), channel_id=1, source_target_pairs={{0,1},{1,0},{2,3},{3,2},{4,5},{5,4},{6,7},{7,6},{8,9},{9,8},{10,11... | collective-permute-start | bytes 301064 | tf_op jit(solution)/shard_map/ppermute | solution.py:397
  97.2 8.6 %collective-permute-start.6 = (bf16[8,6272]{1,0:T(8,128)(2,1)S(1)}, bf16[8,6272]{1,0:T(8,128)(2,1)S(1)}, u32[]{:S(2)}, u32[]{:S(2)}) collective-permute-start(bf16[8,6272]{1,0:T(8,128)(2,1)S(1)} %copy-done.5), channel_id=1, source_target_pairs={{0,2},{1,3},{2,0},{3,1},{4,6},{5,7},{6,4},{7,5},{8,10},{9,11},{10,... | collective-permute-start | bytes 301064 | tf_op jit(solution)/shard_map/ppermute | solution.py:397
  100.6 7.4 %collective-permute-start.7 = (bf16[8,6272]{1,0:T(8,128)(2,1)S(1)}, bf16[8,6272]{1,0:T(8,128)(2,1)S(1)}, u32[]{:S(2)}, u32[]{:S(2)}) collective-permute-start(bf16[8,6272]{1,0:T(8,128)(2,1)S(1)} %copy-done.3), channel_id=1, source_target_pairs={{0,3},{1,2},{2,1},{3,0},{4,7},{5,6},{6,5},{7,4},{8,11},{9,10},{10,... | collective-permute-start | bytes 301064 | tf_op jit(solution)/shard_map/ppermute | solution.py:397

commit v5 on v3

--- a/solution.py
+++ b/solution.py
@@ -148,10 +148,11 @@
     held = refs[12:23]
     turn_ref, rotated_ref, hidden_ref, ssrc_ref, sdst_ref, target_ref, sems = refs[23:]
     (
-        meta_ref, left_ref, right_ref, teacher_ref, student_ref, radial_ref, wsrc_ref, wdst_ref,
+        meta_ref, radial_ref, teacher_ref, left_ref, right_ref, student_ref, wsrc_ref, wdst_ref,
         wrad_ref, wout_ref, whead_ref,
     ) = held
-    for copy in fetch(tuple(zip(raw, held)), sems):
+    copies = fetch(tuple(zip(raw, held)), sems)
+    for copy in copies[:2]:
         copy.wait()
     every = 4 * EDGE
     edges = [meta_ref[q, 352:416].astype(F32) for q in range(4)]
@@ -169,13 +170,16 @@
                 turn_ref[j * EXT : (j + 1) * EXT, q * EDGE : (q + 1) * EDGE] = (
                     sources[q] * edges[q][row : row + 1]
                 ).astype(BF)
+        if degree == 0:
+            for copy in copies[2:]:
+                copy.wait()
         stacked = coefficients((teacher_ref, left_ref, right_ref), degree)
         turned = dot(stacked, turn_ref[: span * EXT], ((0,), (0,)))
         rotated_ref[degree * C : (degree + 1) * C] = (turned * gains).astype(BF)
     column = jnp.concatenate([meta_ref[q, :224] for q in range(4)], axis=0)
-    invariant = dot(rotated_ref[...], column, ((0,), (0,))).astype(BF)
+    invariant = dot(column, rotated_ref[...], ((0,), (0,))).astype(BF)
     scatter = jnp.concatenate([targets[q] * edges[q][0:1] for q in range(4)], axis=1).astype(BF)
-    invariants = dot(scatter, invariant)
+    invariants = dot(scatter, invariant, ((1,), (1,)))
     student_ext = jnp.concatenate(
         [student_ref[...], left_ref[:, KC:], right_ref[:, KC:]], axis=0
     )
@@ -390,6 +394,14 @@
     return lax.ppermute(x, axes, [(i, (i + by) % length) for i in range(length)])
 
 
+def to_brick(x, by):
+    reps = lax.axis_size(REP)
+    length = lax.axis_size(BRICK) * reps
+    half = reps // 2
+    pairs = [(i, (i + by * reps) % length // reps * reps + (i + half) % reps) for i in range(length)]
+    return lax.ppermute(x, BRICK + REP, pairs)
+
+
 def swapped(x, axes, mask):
     return lax.ppermute(x, axes, [(i, i ^ mask) for i in range(lax.axis_size(axes))])
 
@@ -426,8 +438,8 @@
         raws=8,
         room=1024,
     )
-    from_left = shifted(to_next, BRICK, 1)
-    from_right = shifted(to_prev, BRICK, -1)
+    from_left = to_brick(to_next, 1)
+    from_right = to_brick(to_prev, -1)
     meta = exchange(own_meta, REP)
     mixings = (so2_m0, so2_m1, so2_m2)
     low, high = call(
@@ -440,7 +452,7 @@
         room=1024,
     )
     raw = (
-        meta, from_left, from_right, teacher_in, student_in, teacher_radial, w_src, w_dst,
+        meta, teacher_radial, teacher_in, from_left, from_right, student_in, w_src, w_dst,
         w_radial, w_out, w_head,
     )
     (grads,) = call(

time: 108 us -> 106 us (0.981)
    ppermute x0 -> x2, starting transfers between devices: none -> 12.7 us  [to_brick(): return lax.ppermute(x, BRICK + REP, pairs)]
    ppermute x4 -> x2, starting transfers between devices: 18.9 us -> 6.46 us  [shifted(): lax.ppermute(x, axes, [(i, (i + by) % length) for i in range(length)])]
    ppermute x4 -> x2, waiting for transfers between devices: 1.74 us -> 0.01 us  [shifted(): lax.ppermute(x, axes, [(i, (i + by) % length) for i in range(length)])]
    ppermute x0 -> x2, waiting for transfers between devices: none -> 1.38 us  [to_brick(): return lax.ppermute(x, BRICK + REP, pairs)]
    all_to_all x4, starting transfers between devices: 33.8 us -> 32.6 us  [exchange(): return lax.all_to_all(x, axes, 0, 0, tiled=True)]
where the time goes in v5:
time: 106 us; the launch traced here: 105 us
  starting transfers between devices  61.6 us (58%)
  Pallas kernels  22.8 us (22%)
  waiting for transfers between devices  15.1 us (14%)
  local copies, waits for them, and re-layouts  3.42 us (3%)
  between operations  2.12 us (2%)
    all_to_all x4, starting transfers between devices, exchange(): return lax.all_to_all(x, axes, 0, 0, tiled=True)  32.6 us
    pallas_call x9, Pallas kernels, call(): pl.pallas_call(body, out_shape=tuple((jax.ShapeDtypeStruct(shape, dtype)...  22.8 us
    ppermute x2, starting transfers between devices, to_brick(): return lax.ppermute(x, BRICK + REP, pairs)  12.7 us
    all_to_all x4, waiting for transfers between devices, exchange(): return lax.all_to_all(x, axes, 0, 0, tiled=True)  11.5 us
    ppermute x4, starting transfers between devices, swapped(): lax.ppermute(x, axes, [(i, i ^ mask) for i in range(lax.axis_size(axes))])  9.87 us
    ppermute x2, starting transfers between devices, shifted(): lax.ppermute(x, axes, [(i, (i + by) % length) for i in range(length)])  6.46 us
    unnamed x12, local copies, waits for them, and re-layouts  2.51 us
    ppermute x4, waiting for transfers between devices, swapped(): lax.ppermute(x, axes, [(i, i ^ mask) for i in range(lax.axis_size(axes))])  2.16 us
  transfers between devices with their start and end apart: 12, of which 5 were waited for; matrix products, arithmetic and copies ran while one was open for 1% of the time, Pallas kernels for 13%

profile of v5, /device:TPU:1, one launch (start us, length us, event | category | flops | bytes accessed | tf_op | source)
XLA Modules:
  0.0 104.9 jit_solution(424790461329191844)
XLA Ops:
  1.3 2.3 %shard_map.218 = (bf16[16,6528]{1,0:T(8,128)(2,1)}, bf16[16,6528]{1,0:T(8,128)(2,1)}, bf16[4,416,128]{2,1,0:T(8,128)(2,1)}) custom-call(s32[1]{0:T(128)S(6)} %copy.24.count_ref, s32[1,2,16]{2,1,0:T(2,128)} %lists_hbm.1, bf16[32,6272]{1,0:T(8,128)(2,1)} %refs_0_.1, bf16[32,256]{1,0:T(8,128)(2,1)} %refs_5_.2, bf16[224,896]{1,0:T(8,128)(2,1)} %m0_hbm.3, ...), custom_call_target="tpu_custom_call" | custom-call | bytes 4096 | tf_op jit(solution)/shard_map/pallas_call | solution.py:377
  3.6 10.3 %all-to-all-start = ((bf16[4,416,128]{2,1,0:T(8,128)(2,1)}), bf16[4,416,128]{2,1,0:T(8,128)(2,1)S(1)}, u32[]{:S(2)}, u32[]{:S(2)}) async-start(bf16[4,416,128]{2,1,0:T(8,128)(2,1)} %get-tuple-element.31), calls=%async_computation | async-start | bytes 851968 | tf_op jit(solution)/shard_map/all_to_all | solution.py:410
  13.9 1.9 %collective-permute-start = (bf16[16,6528]{1,0:T(8,128)(2,1)}, bf16[16,6528]{1,0:T(8,128)(2,1)S(1)}, u32[]{:S(2)}, u32[]{:S(2)}) collective-permute-start(bf16[16,6528]{1,0:T(8,128)(2,1)} %get-tuple-element.32), channel_id=1, source_target_pairs={{0,6},{1,7},{2,4},{3,5},{4,10},{5,11},{6,8},{7,9},{8,14},{9,15},{1... | collective-permute-start | bytes 626696 | tf_op jit(solution)/shard_map/ppermute | solution.py:402
  15.8 10.8 %collective-permute-start.1 = (bf16[16,6528]{1,0:T(8,128)(2,1)}, bf16[16,6528]{1,0:T(8,128)(2,1)S(1)}, u32[]{:S(2)}, u32[]{:S(2)}) collective-permute-start(bf16[16,6528]{1,0:T(8,128)(2,1)} %get-tuple-element.33), channel_id=1, source_target_pairs={{0,510},{1,511},{2,508},{3,509},{4,2},{5,3},{6,0},{7,1},{8,6},{9,7... | collective-permute-start | bytes 626696 | tf_op jit(solution)/shard_map/ppermute | solution.py:402
  27.2 2.4 %shard_map.217 = (bf16[2720,128]{1,0:T(8,128)(2,1)}, bf16[2752,128]{1,0:T(8,128)(2,1)}) custom-call(bf16[224,896]{1,0:T(8,128)(2,1)} %m0_hbm.3, bf16[2,192,768]{2,1,0:T(8,128)(2,1)} %m1_hbm.1, bf16[2,160,640]{2,1,0:T(8,128)(2,1)} %m2_hbm.1), custom_call_target="tpu_custom_call" | custom-call | flops 1073741824 | bytes 4096 | tf_op jit(solution)/shard_map/pallas_call | solution.py:377
  29.7 0.4 collective-permute-done.refs_3_.refs_1_
  30.1 1.0 collective-permute-done.1.refs_4_.refs_2_
  31.1 0.7 copy-done.5
  31.8 0.8 copy-done.3
  32.5 5.4 %shard_map.219.refs_8_ = bf16[32,32,256]{2,1,0:T(8,128)(2,1)} custom-call(s32[1]{0:T(128)S(6)} %copy.25.atoms_ref, s32[1]{0:T(128)} %bitcast.rep_ref, bf16[4,416,128]{2,1,0:T(8,128)(2,1)} %copy-done.3, bf16[128,128]{1,0:T(8,128)(2,1)} %refs_5_.3, bf16[32,6272]{1,0:T(8,128)(2,1)} %refs_0_.1, bf16[16,6528]{1,0:T(8,128)(2,1)} %copy-done.4, ...), custom_call_target="tpu_custom_call" | custom-call | flops 2147483648 | bytes 4096 | tf_op jit(solution)/shard_map/pallas_call | solution.py:377
  38.0 4.9 %all-to-all-start.1 = ((bf16[32,32,256]{2,1,0:T(8,128)(2,1)}), bf16[32,32,256]{2,1,0:T(8,128)(2,1)S(1)}, u32[]{:S(2)}, u32[]{:S(2)}) async-start(bf16[32,32,256]{2,1,0:T(8,128)(2,1)} %shard_map.219.refs_8_), calls=%async_computation.1 | async-start | bytes 1048576 | tf_op jit(solution)/shard_map/all_to_all | solution.py:410
  42.9 4.5 %collective-permute-start.4 = (bf16[2752,128]{1,0:T(8,128)(2,1)S(1)}, bf16[2752,128]{1,0:T(8,128)(2,1)S(1)}, u32[]{:S(2)}, u32[]{:S(2)}) collective-permute-start(bf16[2752,128]{1,0:T(8,128)(2,1)S(1)} %copy-done), channel_id=1, source_target_pairs={{0,6},{2,0},{4,2},{6,4},{1,7},{3,1},{5,3},{7,5},{8,14},{10,8},{12,... | collective-permute-start | bytes 2113544 | tf_op jit(solution)/shard_map/ppermute | solution.py:394
  47.4 1.9 %collective-permute-start.3 = (bf16[2720,128]{1,0:T(8,128)(2,1)S(1)}, bf16[2720,128]{1,0:T(8,128)(2,1)}, u32[]{:S(2)}, u32[]{:S(2)}) collective-permute-start(bf16[2720,128]{1,0:T(8,128)(2,1)S(1)} %copy-done.1), channel_id=1, source_target_pairs={{0,2},{2,4},{4,6},{6,0},{1,3},{3,5},{5,7},{7,1},{8,10},{10,12},{12... | collective-permute-start | bytes 2088968 | tf_op jit(solution)/shard_map/ppermute | solution.py:394
  49.4 3.7 %shard_map.220 = (bf16[2096,128]{1,0:T(8,128)(2,1)}, bf16[2096,128]{1,0:T(8,128)(2,1)}) custom-call(s32[1]{0:T(128)S(6)} %copy.24.count_ref, s32[1]{0:T(128)} %bitcast.rep_ref, bf16[32,6272]{1,0:T(8,128)(2,1)} %refs_0_.1, bf16[16,6528]{1,0:T(8,128)(2,1)} %copy-done.4, bf16[16,6528]{1,0:T(8,128)(2,1)} %copy-done.5, bf16[235,128]{1,0:T(8,128)(2,1)} %refs_3_.1, ...), custom_call_target="tpu_custom_call" | custom-call | flops 2147483648 | bytes 4096 | tf_op jit(solution)/shard_map/pallas_call | solution.py:377
  53.1 1.5 %all-to-all-done.1.parts_ref = bf16[32,32,256]{2,1,0:T(8,128)(2,1)S(1)} async-done(((bf16[32,32,256]{2,1,0:T(8,128)(2,1)}), bf16[32,32,256]{2,1,0:T(8,128)(2,1)S(1)}, u32[]{:S(2)}, u32[]{:S(2)}) %all-to-all-start.1) | async-done | bytes 524320 | tf_op jit(solution)/shard_map/all_to_all | solution.py:410
  54.6 0.8 shard_map.221.after_ref
  55.4 11.0 %all-to-all-start.2 = ((bf16[16,32,256]{2,1,0:T(8,128)(2,1)}), bf16[16,32,256]{2,1,0:T(8,128)(2,1)S(1)}, u32[]{:S(2)}, u32[]{:S(2)}) async-start(bf16[16,32,256]{2,1,0:T(8,128)(2,1)} %shard_map.221.after_ref), calls=%async_computation.2 | async-start | bytes 524288 | tf_op jit(solution)/shard_map/all_to_all | solution.py:410
  66.4 2.0 %collective-permute-start.2 = (bf16[2096,128]{1,0:T(8,128)(2,1)}, bf16[2096,128]{1,0:T(8,128)(2,1)}, u32[]{:S(2)}, u32[]{:S(2)}) collective-permute-start(bf16[2096,128]{1,0:T(8,128)(2,1)} %get-tuple-element.38), channel_id=1, source_target_pairs={{0,1},{1,0},{2,3},{3,2},{4,5},{5,4},{6,7},{7,6},{8,9},{9,8},{10,11... | collective-permute-start | bytes 1609736 | tf_op jit(solution)/shard_map/ppermute | solution.py:406
  68.4 2.2 %collective-permute-done.2.got_ref = bf16[2096,128]{1,0:T(8,128)(2,1)} collective-permute-done((bf16[2096,128]{1,0:T(8,128)(2,1)}, bf16[2096,128]{1,0:T(8,128)(2,1)}, u32[]{:S(2)}, u32[]{:S(2)}) %collective-permute-start.2) | collective-permute-done | bytes 536608 | tf_op jit(solution)/shard_map/ppermute | solution.py:406
  70.6 0.0 collective-permute-done.4.far_high_ref
  70.6 1.0 copy-done.2
  71.7 5.5 %shard_map.222 = (f32[8,6272]{1,0:T(8,128)S(1)}, bf16[8,6272]{1,0:T(8,128)(2,1)S(1)}, bf16[8,6272]{1,0:T(8,128)(2,1)S(1)}, bf16[8,6272]{1,0:T(8,128)(2,1)S(1)}) custom-call(s32[1]{0:T(128)} %bitcast.rep_ref, bf16[2096,128]{1,0:T(8,128)(2,1)S(1)} %copy-done.2, bf16[2096,128]{1,0:T(8,128)(2,1)} %collective-permute-done.2.got_ref, ...), custom_call_target="tpu_custom_call" | custom-call | flops 4294967296 | bytes 4096 | tf_op jit(solution)/shard_map/pallas_call | solution.py:377
  77.2 2.0 %collective-permute-start.5 = (bf16[8,6272]{1,0:T(8,128)(2,1)S(1)}, bf16[8,6272]{1,0:T(8,128)(2,1)S(1)}, u32[]{:S(2)}, u32[]{:S(2)}) collective-permute-start(bf16[8,6272]{1,0:T(8,128)(2,1)S(1)} %get-tuple-element.43), channel_id=1, source_target_pairs={{0,1},{1,0},{2,3},{3,2},{4,5},{5,4},{6,7},{7,6},{8,9},{9,8},{10,11... | collective-permute-start | bytes 301064 | tf_op jit(solution)/shard_map/ppermute | solution.py:406
  79.2 2.3 %collective-permute-start.6 = (bf16[8,6272]{1,0:T(8,128)(2,1)S(1)}, bf16[8,6272]{1,0:T(8,128)(2,1)S(1)}, u32[]{:S(2)}, u32[]{:S(2)}) collective-permute-start(bf16[8,6272]{1,0:T(8,128)(2,1)S(1)} %get-tuple-element.44), channel_id=1, source_target_pairs={{0,2},{1,3},{2,0},{3,1},{4,6},{5,7},{6,4},{7,5},{8,10},{9,11},{10,... | collective-permute-start | bytes 301064 | tf_op jit(solution)/shard_map/ppermute | solution.py:406
  81.5 3.5 %collective-permute-start.7 = (bf16[8,6272]{1,0:T(8,128)(2,1)S(1)}, bf16[8,6272]{1,0:T(8,128)(2,1)S(1)}, u32[]{:S(2)}, u32[]{:S(2)}) collective-permute-start(bf16[8,6272]{1,0:T(8,128)(2,1)S(1)} %get-tuple-element.45), channel_id=1, source_target_pairs={{0,3},{1,2},{2,1},{3,0},{4,7},{5,6},{6,5},{7,4},{8,11},{9,10},{10,... | collective-permute-start | bytes 301064 | tf_op jit(solution)/shard_map/ppermute | solution.py:406
  85.1 0.9 shard_map.224
  86.0 6.3 %all-to-all-start.3 = ((bf16[32,32,256]{2,1,0:T(8,128)(2,1)}), bf16[32,32,256]{2,1,0:T(8,128)(2,1)S(1)}, u32[]{:S(2)}, u32[]{:S(2)}) async-start(bf16[32,32,256]{2,1,0:T(8,128)(2,1)} %shard_map.224), calls=%async_computation.3 | async-start | bytes 1048576 | tf_op jit(solution)/shard_map/all_to_all | solution.py:410
  92.3 0.9 constant_dynamic-slice_fusion.own_ref
  93.2 0.0 collective-permute-done.5.s1_ref
  93.2 0.7 shard_map.223
  94.0 10.0 %all-to-all-done.3.all_ref = bf16[32,32,256]{2,1,0:T(8,128)(2,1)S(1)} async-done(((bf16[32,32,256]{2,1,0:T(8,128)(2,1)}), bf16[32,32,256]{2,1,0:T(8,128)(2,1)S(1)}, u32[]{:S(2)}, u32[]{:S(2)}) %all-to-all-start.3) | async-done | bytes 524320 | tf_op jit(solution)/shard_map/all_to_all | solution.py:410
  103.9 1.0 shard_map.225
  (14 shorter events, 0.0 us)
Async XLA Ops:
  3.6 27.5 %all-to-all-start = ((bf16[4,416,128]{2,1,0:T(8,128)(2,1)}), bf16[4,416,128]{2,1,0:T(8,128)(2,1)S(1)}, u32[]{:S(2)}, u32[]{:S(2)}) async-start(bf16[4,416,128]{2,1,0:T(8,128)(2,1)} %get-tuple-element.31), calls=%async_computation | async-start | bytes 851968 | tf_op jit(solution)/shard_map/all_to_all | solution.py:410
  13.9 16.2 %collective-permute-start = (bf16[16,6528]{1,0:T(8,128)(2,1)}, bf16[16,6528]{1,0:T(8,128)(2,1)S(1)}, u32[]{:S(2)}, u32[]{:S(2)}) collective-permute-start(bf16[16,6528]{1,0:T(8,128)(2,1)} %get-tuple-element.32), channel_id=1, source_target_pairs={{0,6},{1,7},{2,4},{3,5},{4,10},{5,11},{6,8},{7,9},{8,14},{9,15},{1... | collective-permute-start | bytes 626696 | tf_op jit(solution)/shard_map/ppermute | solution.py:402
  15.8 15.3 %collective-permute-start.1 = (bf16[16,6528]{1,0:T(8,128)(2,1)}, bf16[16,6528]{1,0:T(8,128)(2,1)S(1)}, u32[]{:S(2)}, u32[]{:S(2)}) collective-permute-start(bf16[16,6528]{1,0:T(8,128)(2,1)} %get-tuple-element.33), channel_id=1, source_target_pairs={{0,510},{1,511},{2,508},{3,509},{4,2},{5,3},{6,0},{7,1},{8,6},{9,7... | collective-permute-start | bytes 626696 | tf_op jit(solution)/shard_map/ppermute | solution.py:402
  30.1 2.4 %copy-start.4 = (bf16[16,6528]{1,0:T(8,128)(2,1)}, bf16[16,6528]{1,0:T(8,128)(2,1)S(1)}, u32[]{:S(2)}) copy-start(bf16[16,6528]{1,0:T(8,128)(2,1)S(1)} %collective-permute-done.refs_3_.refs_1_) | copy-start | bytes 626692
  31.1 0.7 copy-start.5
  31.8 0.8 copy-start.3
  32.5 14.9 %copy-start.1 = (bf16[2720,128]{1,0:T(8,128)(2,1)S(1)}, bf16[2720,128]{1,0:T(8,128)(2,1)}, u32[]{:S(2)}) copy-start(bf16[2720,128]{1,0:T(8,128)(2,1)} %get-tuple-element.39.low_ref) | copy-start | bytes 2088964
  38.0 4.9 %copy-start = (bf16[2752,128]{1,0:T(8,128)(2,1)S(1)}, bf16[2752,128]{1,0:T(8,128)(2,1)}, u32[]{:S(2)}) copy-start(bf16[2752,128]{1,0:T(8,128)(2,1)} %get-tuple-element.40.high_ref) | copy-start | bytes 2113540
  38.0 16.6 %all-to-all-start.1 = ((bf16[32,32,256]{2,1,0:T(8,128)(2,1)}), bf16[32,32,256]{2,1,0:T(8,128)(2,1)S(1)}, u32[]{:S(2)}, u32[]{:S(2)}) async-start(bf16[32,32,256]{2,1,0:T(8,128)(2,1)} %shard_map.219.refs_8_), calls=%async_computation.1 | async-start | bytes 1048576 | tf_op jit(solution)/shard_map/all_to_all | solution.py:410
  42.9 27.7 %collective-permute-start.4 = (bf16[2752,128]{1,0:T(8,128)(2,1)S(1)}, bf16[2752,128]{1,0:T(8,128)(2,1)S(1)}, u32[]{:S(2)}, u32[]{:S(2)}) collective-permute-start(bf16[2752,128]{1,0:T(8,128)(2,1)S(1)} %copy-done), channel_id=1, source_target_pairs={{0,6},{2,0},{4,2},{6,4},{1,7},{3,1},{5,3},{7,5},{8,14},{10,8},{12,... | collective-permute-start | bytes 2113544 | tf_op jit(solution)/shard_map/ppermute | solution.py:394
  47.4 23.2 %collective-permute-start.3 = (bf16[2720,128]{1,0:T(8,128)(2,1)S(1)}, bf16[2720,128]{1,0:T(8,128)(2,1)}, u32[]{:S(2)}, u32[]{:S(2)}) collective-permute-start(bf16[2720,128]{1,0:T(8,128)(2,1)S(1)} %copy-done.1), channel_id=1, source_target_pairs={{0,2},{2,4},{4,6},{6,0},{1,3},{3,5},{5,7},{7,1},{8,10},{10,12},{12... | collective-permute-start | bytes 2088968 | tf_op jit(solution)/shard_map/ppermute | solution.py:394
  55.4 29.7 %all-to-all-start.2 = ((bf16[16,32,256]{2,1,0:T(8,128)(2,1)}), bf16[16,32,256]{2,1,0:T(8,128)(2,1)S(1)}, u32[]{:S(2)}, u32[]{:S(2)}) async-start(bf16[16,32,256]{2,1,0:T(8,128)(2,1)} %shard_map.221.after_ref), calls=%async_computation.2 | async-start | bytes 524288 | tf_op jit(solution)/shard_map/all_to_all | solution.py:410
  66.4 4.2 %collective-permute-start.2 = (bf16[2096,128]{1,0:T(8,128)(2,1)}, bf16[2096,128]{1,0:T(8,128)(2,1)}, u32[]{:S(2)}, u32[]{:S(2)}) collective-permute-start(bf16[2096,128]{1,0:T(8,128)(2,1)} %get-tuple-element.38), channel_id=1, source_target_pairs={{0,1},{1,0},{2,3},{3,2},{4,5},{5,4},{6,7},{7,6},{8,9},{9,8},{10,11... | collective-permute-start | bytes 1609736 | tf_op jit(solution)/shard_map/ppermute | solution.py:406
  70.6 1.0 copy-start.2
  77.2 16.1 %collective-permute-start.5 = (bf16[8,6272]{1,0:T(8,128)(2,1)S(1)}, bf16[8,6272]{1,0:T(8,128)(2,1)S(1)}, u32[]{:S(2)}, u32[]{:S(2)}) collective-permute-start(bf16[8,6272]{1,0:T(8,128)(2,1)S(1)} %get-tuple-element.43), channel_id=1, source_target_pairs={{0,1},{1,0},{2,3},{3,2},{4,5},{5,4},{6,7},{7,6},{8,9},{9,8},{10,11... | collective-permute-start | bytes 301064 | tf_op jit(solution)/shard_map/ppermute | solution.py:406
  79.2 14.0 %collective-permute-start.6 = (bf16[8,6272]{1,0:T(8,128)(2,1)S(1)}, bf16[8,6272]{1,0:T(8,128)(2,1)S(1)}, u32[]{:S(2)}, u32[]{:S(2)}) collective-permute-start(bf16[8,6272]{1,0:T(8,128)(2,1)S(1)} %get-tuple-element.44), channel_id=1, source_target_pairs={{0,2},{1,3},{2,0},{3,1},{4,6},{5,7},{6,4},{7,5},{8,10},{9,11},{10,... | collective-permute-start | bytes 301064 | tf_op jit(solution)/shard_map/ppermute | solution.py:406
  81.5 11.7 %collective-permute-start.7 = (bf16[8,6272]{1,0:T(8,128)(2,1)S(1)}, bf16[8,6272]{1,0:T(8,128)(2,1)S(1)}, u32[]{:S(2)}, u32[]{:S(2)}) collective-permute-start(bf16[8,6272]{1,0:T(8,128)(2,1)S(1)} %get-tuple-element.45), channel_id=1, source_target_pairs={{0,3},{1,2},{2,1},{3,0},{4,7},{5,6},{6,5},{7,4},{8,11},{9,10},{10,... | collective-permute-start | bytes 301064 | tf_op jit(solution)/shard_map/ppermute | solution.py:406
  86.0 18.0 %all-to-all-start.3 = ((bf16[32,32,256]{2,1,0:T(8,128)(2,1)}), bf16[32,32,256]{2,1,0:T(8,128)(2,1)S(1)}, u32[]{:S(2)}, u32[]{:S(2)}) async-start(bf16[32,32,256]{2,1,0:T(8,128)(2,1)} %shard_map.224), calls=%async_computation.3 | async-start | bytes 1048576 | tf_op jit(solution)/shard_map/all_to_all | solution.py:410

commit v6 on v5

--- a/solution.py
+++ b/solution.py
@@ -102,8 +102,23 @@
     return jnp.where(live_row(count), dst_row, EXT).astype(F32)
 
 
-def pack_body(m0_hbm, m1_hbm, m2_hbm, low_ref, high_ref, m0_ref, m1_ref, m2_ref, sems):
-    copies = fetch(((m0_hbm, m0_ref), (m1_hbm, m1_ref), (m2_hbm, m2_ref)), sems)
+def pack_body(
+    m0_hbm, m1_hbm, m2_hbm, student_hbm, wsrc_hbm, wdst_hbm, wout_hbm, wrad_hbm, whead_hbm,
+    radial_hbm, low_ref, high_ref, bundle_hbm, m0_ref, m1_ref, m2_ref, sems,
+):
+    copies = fetch(
+        (
+            (m0_hbm, m0_ref), (m1_hbm, m1_ref), (m2_hbm, m2_ref),
+            (student_hbm, bundle_hbm.at[0:32]), (wsrc_hbm, bundle_hbm.at[32:288]),
+            (wdst_hbm, bundle_hbm.at[288:544]), (wout_hbm, bundle_hbm.at[544:800]),
+            (wrad_hbm, bundle_hbm.at[800:928]),
+            (whead_hbm.at[:C], bundle_hbm.at[928:1056, :C]),
+            (whead_hbm.at[C:], bundle_hbm.at[928:1056, C:]),
+            (radial_hbm, bundle_hbm.at[1056:1184, :C]),
+            (radial_hbm, bundle_hbm.at[1056:1184, C:]),
+        ),
+        sems,
+    )
     at = 0
     for part, wide, high, ready in (
         (m0_ref, 7, 224, 0), (m1_ref.at[0], 6, 192, 1), (m1_ref.at[1], 6, 192, None),
@@ -118,6 +133,8 @@
             else:
                 high_ref[at - LOW : at - LOW + high] = block
             at += high
+    for copy in copies[3:]:
+        copy.wait()
 
 
 def coefficients(refs, degree):
@@ -142,19 +159,18 @@
         row += size
 
 
-def early_body(inv_atoms, atoms_ref, rep_ref, *refs):
-    raw = refs[:11]
-    grad_ref = refs[11]
-    held = refs[12:23]
-    turn_ref, rotated_ref, hidden_ref, ssrc_ref, sdst_ref, target_ref, sems = refs[23:]
-    (
-        meta_ref, radial_ref, teacher_ref, left_ref, right_ref, student_ref, wsrc_ref, wdst_ref,
-        wrad_ref, wout_ref, whead_ref,
-    ) = held
-    copies = fetch(tuple(zip(raw, held)), sems)
-    for copy in copies[:2]:
-        copy.wait()
-    every = 4 * EDGE
+def early_body(
+    inv_atoms, atoms_ref, rep_ref, meta_ref, bundle_ref, teacher_ref, left_ref, right_ref,
+    grad_ref,
+    turn_ref, rotated_ref, hidden_ref, ssrc_ref, sdst_ref, target_ref,
+):
+    student_ref = bundle_ref.at[0:32]
+    wsrc_ref = bundle_ref.at[32:288]
+    wdst_ref = bundle_ref.at[288:544]
+    wout_ref = bundle_ref.at[544:800]
+    wrad_ref = bundle_ref.at[800:928]
+    head = jnp.concatenate([bundle_ref[928:1056, :C], bundle_ref[928:1056, C:]], axis=0)
+    radial_ref = bundle_ref.at[1056:1184, :C]
     edges = [meta_ref[q, 352:416].astype(F32) for q in range(4)]
     ext_rows = lax.broadcasted_iota(jnp.int32, (EXT, EDGE), 0).astype(F32)
     sources = [(edges[q][49:50] == ext_rows).astype(F32) for q in range(4)]
@@ -170,9 +186,6 @@
                 turn_ref[j * EXT : (j + 1) * EXT, q * EDGE : (q + 1) * EDGE] = (
                     sources[q] * edges[q][row : row + 1]
                 ).astype(BF)
-        if degree == 0:
-            for copy in copies[2:]:
-                copy.wait()
         stacked = coefficients((teacher_ref, left_ref, right_ref), degree)
         turned = dot(stacked, turn_ref[: span * EXT], ((0,), (0,)))
         rotated_ref[degree * C : (degree + 1) * C] = (turned * gains).astype(BF)
@@ -200,11 +213,11 @@
     target = (teacher_ref[:, :C].astype(F32) + inv_degree * invariants).astype(BF)
     pooled = (dot(onehot, gated) * inv_degree).astype(BF)
     updated = (student_ref[...].astype(F32) + dot(pooled, wout_ref[...])).astype(BF)
-    predicted = dot(updated, whead_ref[...])
+    predicted = dot(updated, head)
     rows = lax.broadcasted_iota(jnp.int32, (OWN, 1), 0)
     residual = jnp.where(rows < atoms_ref[0], predicted - target.astype(F32), 0.0)
     scaled = (residual * inv_atoms).astype(BF)
-    upstream = dot(scaled, whead_ref[...], ((1,), (1,))).astype(BF)
+    upstream = dot(scaled, head, ((1,), (1,))).astype(BF)
     rep = rep_ref[0]
     mine = (rows >= rep * 8) & (rows < rep * 8 + 8)
     scaled_part = jnp.where(mine, scaled.astype(F32), 0.0).astype(BF)
@@ -372,13 +385,13 @@
     out_ref[...] = (own_ref[...].astype(F32) + total * (1.0 / math.sqrt(DEG))).astype(BF)
 
 
-def call(body, outs, ins, scratch=(), scalars=0, raws=0, after=0, flops=0, room=24 << 10):
+def call(body, outs, ins, scratch=(), scalars=0, raws=0, after=0, flops=0, room=24 << 10, outs_hbm=0):
     specs = [SMEM] * scalars + [VMEM] * (len(ins) - scalars - raws - after)
     return pl.pallas_call(
         body,
         out_shape=tuple(jax.ShapeDtypeStruct(shape, dtype) for shape, dtype in outs),
         in_specs=specs + [HBM] * raws + [ANY] * after,
-        out_specs=tuple(VMEM for _ in outs),
+        out_specs=(VMEM,) * (len(outs) - outs_hbm) + (HBM,) * outs_hbm,
         scratch_shapes=list(scratch),
         compiler_params=pltpu.CompilerParams(vmem_limit_bytes=(FULL - room) << 10),
         cost_estimate=pl.CostEstimate(flops=flops, bytes_accessed=4096, transcendentals=0),
@@ -442,34 +455,29 @@
     from_right = to_brick(to_prev, -1)
     meta = exchange(own_meta, REP)
     mixings = (so2_m0, so2_m1, so2_m2)
-    low, high = call(
+    raw = (*mixings, student_in, w_src, w_dst, w_out, w_radial, w_head, teacher_radial)
+    low, high, bundle = call(
         pack_body,
-        [((LOW, C), BF), ((HIGH, C), BF)],
-        mixings,
-        held(mixings) + [pltpu.SemaphoreType.DMA((3,))],
-        raws=3,
+        [((LOW, C), BF), ((HIGH, C), BF), ((1184, SW), BF)],
+        raw,
+        held(mixings) + [pltpu.SemaphoreType.DMA((12,))],
+        raws=10,
         flops=1 << 30,
         room=1024,
-    )
-    raw = (
-        meta, teacher_radial, teacher_in, from_left, from_right, student_in, w_src, w_dst,
-        w_radial, w_out, w_head,
+        outs_hbm=1,
     )
     (grads,) = call(
         functools.partial(early_body, 1.0 / (OWN * bricks)),
         [((plane, chunk, SW), BF)],
-        (atom_count, rep1, *raw),
-        held(raw)
-        + [
+        (atom_count, rep1, meta, bundle, teacher_in, from_left, from_right),
+        [
             pltpu.VMEM((13 * EXT, 4 * EDGE), BF), pltpu.VMEM((896, 4 * EDGE), BF),
             pltpu.VMEM((4 * EDGE, SW), F32), pltpu.VMEM((4 * EDGE, SW), BF),
             pltpu.VMEM((4 * EDGE, SW), BF), pltpu.VMEM((4, OWN, EDGE), BF),
-            pltpu.SemaphoreType.DMA((11,)),
         ],
         scalars=2,
-        raws=11,
         flops=1 << 31,
-        room=1024,
+        room=12288,
     )
     low, high, grads = lax.optimization_barrier((low, high, grads))
     across_low = shifted(low, ("yh", "yl"), 1)

time: 106 us -> 117 us (1.10)
  Pallas kernels: 22.8 us -> 40.6 us
  starting transfers between devices: 61.6 us -> 55.5 us
  local copies, waits for them, and re-layouts: 3.42 us -> 1.97 us
    pallas_call x9, Pallas kernels: 22.8 us -> 40.6 us  [call(): pl.pallas_call(body, out_shape=tuple((jax.ShapeDtypeStruct(shape, dtype)...]
    all_to_all x4, starting transfers between devices: 32.6 us -> 26.2 us  [exchange(): return lax.all_to_all(x, axes, 0, 0, tiled=True)]
    ppermute x2, waiting for transfers between devices: 0.01 us -> 2.2 us  [shifted(): lax.ppermute(x, axes, [(i, (i + by) % length) for i in range(length)])]
    unnamed x12 -> x8, local copies, waits for them, and re-layouts: 2.51 us -> 1.06 us
    ppermute x2, waiting for transfers between devices: 1.38 us -> 0.01 us  [to_brick(): return lax.ppermute(x, BRICK + REP, pairs)]
  transfers between devices with their start and end apart: 12 -> 12, of which waited for: 5 -> 4; matrix products, arithmetic and copies ran while one was open for 1% -> 1% of each run, Pallas kernels for 13% -> 28%
where the time goes in v6:
time: 117 us; the launch traced here: 116 us
  starting transfers between devices  55.5 us (47%)
  Pallas kernels  40.6 us (35%)
  waiting for transfers between devices  15.7 us (13%)
  between operations  2.14 us (2%)
  local copies, waits for them, and re-layouts  1.97 us (2%)
    pallas_call x9, Pallas kernels, call(): pl.pallas_call(body, out_shape=tuple((jax.ShapeDtypeStruct(shape, dtype)...  40.6 us
    all_to_all x4, starting transfers between devices, exchange(): return lax.all_to_all(x, axes, 0, 0, tiled=True)  26.2 us
    ppermute x2, starting transfers between devices, to_brick(): return lax.ppermute(x, BRICK + REP, pairs)  12.7 us
    all_to_all x4, waiting for transfers between devices, exchange(): return lax.all_to_all(x, axes, 0, 0, tiled=True)  11.5 us
    ppermute x4, starting transfers between devices, swapped(): lax.ppermute(x, axes, [(i, i ^ mask) for i in range(lax.axis_size(axes))])  10.1 us
    ppermute x2, starting transfers between devices, shifted(): lax.ppermute(x, axes, [(i, (i + by) % length) for i in range(length)])  6.46 us
  transfers between devices with their start and end apart: 12, of which 4 were waited for; matrix products, arithmetic and copies ran while one was open for 1% of the time, Pallas kernels for 28%

profile of v6, /device:TPU:1, one launch (start us, length us, event | category | flops | bytes accessed | tf_op | source)
XLA Modules:
  0.0 115.9 jit_solution(10494493169110718088)
XLA Ops:
  1.3 2.3 %shard_map.218 = (bf16[16,6528]{1,0:T(8,128)(2,1)}, bf16[16,6528]{1,0:T(8,128)(2,1)}, bf16[4,416,128]{2,1,0:T(8,128)(2,1)}) custom-call(s32[1]{0:T(128)S(6)} %copy.24.count_ref, s32[1,2,16]{2,1,0:T(2,128)} %lists_hbm.1, bf16[32,6272]{1,0:T(8,128)(2,1)} %refs_0_.1, bf16[32,256]{1,0:T(8,128)(2,1)} %student_hbm.3, bf16[224,896]{1,0:T(8,128)(2,1)} %m0_hbm.3, ...), custom_call_target="tpu_custom_call" | custom-call | bytes 4096 | tf_op jit(solution)/shard_map/pallas_call | solution.py:390
  3.6 10.3 %all-to-all-start = ((bf16[4,416,128]{2,1,0:T(8,128)(2,1)}), bf16[4,416,128]{2,1,0:T(8,128)(2,1)S(1)}, u32[]{:S(2)}, u32[]{:S(2)}) async-start(bf16[4,416,128]{2,1,0:T(8,128)(2,1)} %get-tuple-element.32), calls=%async_computation | async-start | bytes 851968 | tf_op jit(solution)/shard_map/all_to_all | solution.py:423
  13.9 1.9 %collective-permute-start = (bf16[16,6528]{1,0:T(8,128)(2,1)}, bf16[16,6528]{1,0:T(8,128)(2,1)}, u32[]{:S(2)}, u32[]{:S(2)}) collective-permute-start(bf16[16,6528]{1,0:T(8,128)(2,1)} %get-tuple-element.34), channel_id=1, source_target_pairs={{0,6},{1,7},{2,4},{3,5},{4,10},{5,11},{6,8},{7,9},{8,14},{9,15},{1... | collective-permute-start | bytes 626696 | tf_op jit(solution)/shard_map/ppermute | solution.py:415
  15.8 10.8 %collective-permute-start.1 = (bf16[16,6528]{1,0:T(8,128)(2,1)}, bf16[16,6528]{1,0:T(8,128)(2,1)}, u32[]{:S(2)}, u32[]{:S(2)}) collective-permute-start(bf16[16,6528]{1,0:T(8,128)(2,1)} %get-tuple-element.35), channel_id=1, source_target_pairs={{0,510},{1,511},{2,508},{3,509},{4,2},{5,3},{6,0},{7,1},{8,6},{9,7... | collective-permute-start | bytes 626696 | tf_op jit(solution)/shard_map/ppermute | solution.py:415
  27.2 0.0 copy-start
  27.3 20.7 %shard_map.217 = (bf16[2720,128]{1,0:T(8,128)(2,1)}, bf16[2752,128]{1,0:T(8,128)(2,1)}, bf16[1184,256]{1,0:T(8,128)(2,1)}) custom-call(bf16[224,896]{1,0:T(8,128)(2,1)} %m0_hbm.3, bf16[2,192,768]{2,1,0:T(8,128)(2,1)} %m1_hbm.1, bf16[2,160,640]{2,1,0:T(8,128)(2,1)} %m2_hbm.1, bf16[32,256]{1,0:T(8,128)(2,1)} %student_hbm.3, bf16[256,256]{1,0:T(8,128)(2,1)} %wsrc_hbm.1, ...), custom_call_target="tpu_custom_call" | custom-call | flops 1073741824 | bytes 4096 | tf_op jit(solution)/shard_map/pallas_call | solution.py:390
  48.0 0.0 collective-permute-done.left_ref.refs_1_
  48.0 0.0 all-to-all-done.meta_ref
  48.0 5.2 %shard_map.219.refs_8_ = bf16[32,32,256]{2,1,0:T(8,128)(2,1)} custom-call(s32[1]{0:T(128)S(6)} %copy.25.atoms_ref, s32[1]{0:T(128)} %bitcast.rep_ref, bf16[4,416,128]{2,1,0:T(8,128)(2,1)S(1)} %all-to-all-done.meta_ref, bf16[1184,256]{1,0:T(8,128)(2,1)} %get-tuple-element.33.bundle_ref, bf16[32,6272]{1,0:T(8,128)(2,1)S(1)} %copy-done, ...), custom_call_target="tpu_custom_call" | custom-call | flops 2147483648 | bytes 4096 | tf_op jit(solution)/shard_map/pallas_call | solution.py:390
  53.2 4.3 %all-to-all-start.1 = ((bf16[32,32,256]{2,1,0:T(8,128)(2,1)}), bf16[32,32,256]{2,1,0:T(8,128)(2,1)S(1)}, u32[]{:S(2)}, u32[]{:S(2)}) async-start(bf16[32,32,256]{2,1,0:T(8,128)(2,1)} %shard_map.219.refs_8_), calls=%async_computation.1 | async-start | bytes 1048576 | tf_op jit(solution)/shard_map/all_to_all | solution.py:423
  57.5 4.5 %collective-permute-start.4 = (bf16[2752,128]{1,0:T(8,128)(2,1)S(1)}, bf16[2752,128]{1,0:T(8,128)(2,1)S(1)}, u32[]{:S(2)}, u32[]{:S(2)}) collective-permute-start(bf16[2752,128]{1,0:T(8,128)(2,1)S(1)} %copy-done.1), channel_id=1, source_target_pairs={{0,6},{2,0},{4,2},{6,4},{1,7},{3,1},{5,3},{7,5},{8,14},{10,8},{12,... | collective-permute-start | bytes 2113544 | tf_op jit(solution)/shard_map/ppermute | solution.py:407
  62.0 1.9 %collective-permute-start.3 = (bf16[2720,128]{1,0:T(8,128)(2,1)}, bf16[2720,128]{1,0:T(8,128)(2,1)}, u32[]{:S(2)}, u32[]{:S(2)}) collective-permute-start(bf16[2720,128]{1,0:T(8,128)(2,1)} %get-tuple-element.41.low_ref), channel_id=1, source_target_pairs={{0,2},{2,4},{4,6},{6,0},{1,3},{3,5},{5,7},{7,1},{8,10},{10,12},{12... | collective-permute-start | bytes 2088968 | tf_op jit(solution)/shard_map/ppermute | solution.py:407
  64.0 3.7 %shard_map.220 = (bf16[2096,128]{1,0:T(8,128)(2,1)}, bf16[2096,128]{1,0:T(8,128)(2,1)}) custom-call(s32[1]{0:T(128)S(6)} %copy.24.count_ref, s32[1]{0:T(128)} %bitcast.rep_ref, bf16[32,6272]{1,0:T(8,128)(2,1)} %refs_0_.1, bf16[16,6528]{1,0:T(8,128)(2,1)} %collective-permute-done.left_ref.refs_1_, bf16[16,6528]{1,0:T(8,128)(2,1)} %collective-permute-done.1.right_ref.refs_2_, ...), custom_call_target="tpu_custom_call" | custom-call | flops 2147483648 | bytes 4096 | tf_op jit(solution)/shard_map/pallas_call | solution.py:390
  67.7 1.6 %all-to-all-done.1.parts_ref = bf16[32,32,256]{2,1,0:T(8,128)(2,1)S(1)} async-done(((bf16[32,32,256]{2,1,0:T(8,128)(2,1)}), bf16[32,32,256]{2,1,0:T(8,128)(2,1)S(1)}, u32[]{:S(2)}, u32[]{:S(2)}) %all-to-all-start.1) | async-done | bytes 524320 | tf_op jit(solution)/shard_map/all_to_all | solution.py:423
  69.2 0.8 shard_map.221.after_ref
  70.0 7.5 %all-to-all-start.2 = ((bf16[16,32,256]{2,1,0:T(8,128)(2,1)}), bf16[16,32,256]{2,1,0:T(8,128)(2,1)S(1)}, u32[]{:S(2)}, u32[]{:S(2)}) async-start(bf16[16,32,256]{2,1,0:T(8,128)(2,1)} %shard_map.221.after_ref), calls=%async_computation.2 | async-start | bytes 524288 | tf_op jit(solution)/shard_map/all_to_all | solution.py:423
  77.6 2.0 %collective-permute-start.2 = (bf16[2096,128]{1,0:T(8,128)(2,1)}, bf16[2096,128]{1,0:T(8,128)(2,1)S(1)}, u32[]{:S(2)}, u32[]{:S(2)}) collective-permute-start(bf16[2096,128]{1,0:T(8,128)(2,1)} %get-tuple-element.40), channel_id=1, source_target_pairs={{0,1},{1,0},{2,3},{3,2},{4,5},{5,4},{6,7},{7,6},{8,9},{9,8},{10,11... | collective-permute-start | bytes 1609736 | tf_op jit(solution)/shard_map/ppermute | solution.py:419
  79.6 2.0 %collective-permute-done.2.got_ref = bf16[2096,128]{1,0:T(8,128)(2,1)S(1)} collective-permute-done((bf16[2096,128]{1,0:T(8,128)(2,1)}, bf16[2096,128]{1,0:T(8,128)(2,1)S(1)}, u32[]{:S(2)}, u32[]{:S(2)}) %collective-permute-start.2) | collective-permute-done | bytes 536608 | tf_op jit(solution)/shard_map/ppermute | solution.py:419
  81.6 2.2 %collective-permute-done.3.far_low_ref = bf16[2720,128]{1,0:T(8,128)(2,1)} collective-permute-done((bf16[2720,128]{1,0:T(8,128)(2,1)}, bf16[2720,128]{1,0:T(8,128)(2,1)}, u32[]{:S(2)}, u32[]{:S(2)}) %collective-permute-start.3) | collective-permute-done | bytes 696352 | tf_op jit(solution)/shard_map/ppermute | solution.py:407
  83.8 0.0 collective-permute-done.4.far_high_ref
  83.8 1.0 copy-done.3
  84.8 5.3 %shard_map.222 = (f32[8,6272]{1,0:T(8,128)S(1)}, bf16[8,6272]{1,0:T(8,128)(2,1)S(1)}, bf16[8,6272]{1,0:T(8,128)(2,1)S(1)}, bf16[8,6272]{1,0:T(8,128)(2,1)S(1)}) custom-call(s32[1]{0:T(128)} %bitcast.rep_ref, bf16[2096,128]{1,0:T(8,128)(2,1)S(1)} %copy-done.3, bf16[2096,128]{1,0:T(8,128)(2,1)S(1)} %collective-permute-done.2.got_ref, ...), custom_call_target="tpu_custom_call" | custom-call | flops 4294967296 | bytes 4096 | tf_op jit(solution)/shard_map/pallas_call | solution.py:390
  90.2 2.6 %collective-permute-start.5 = (bf16[8,6272]{1,0:T(8,128)(2,1)S(1)}, bf16[8,6272]{1,0:T(8,128)(2,1)S(1)}, u32[]{:S(2)}, u32[]{:S(2)}) collective-permute-start(bf16[8,6272]{1,0:T(8,128)(2,1)S(1)} %get-tuple-element.45), channel_id=1, source_target_pairs={{0,1},{1,0},{2,3},{3,2},{4,5},{5,4},{6,7},{7,6},{8,9},{9,8},{10,11... | collective-permute-start | bytes 301064 | tf_op jit(solution)/shard_map/ppermute | solution.py:419
  92.8 1.9 %collective-permute-start.6 = (bf16[8,6272]{1,0:T(8,128)(2,1)S(1)}, bf16[8,6272]{1,0:T(8,128)(2,1)S(1)}, u32[]{:S(2)}, u32[]{:S(2)}) collective-permute-start(bf16[8,6272]{1,0:T(8,128)(2,1)S(1)} %get-tuple-element.46), channel_id=1, source_target_pairs={{0,2},{1,3},{2,0},{3,1},{4,6},{5,7},{6,4},{7,5},{8,10},{9,11},{10,... | collective-permute-start | bytes 301064 | tf_op jit(solution)/shard_map/ppermute | solution.py:419
  94.7 3.5 %collective-permute-start.7 = (bf16[8,6272]{1,0:T(8,128)(2,1)S(1)}, bf16[8,6272]{1,0:T(8,128)(2,1)S(1)}, u32[]{:S(2)}, u32[]{:S(2)}) collective-permute-start(bf16[8,6272]{1,0:T(8,128)(2,1)S(1)} %get-tuple-element.47), channel_id=1, source_target_pairs={{0,3},{1,2},{2,1},{3,0},{4,7},{5,6},{6,5},{7,4},{8,11},{9,10},{10,... | collective-permute-start | bytes 301064 | tf_op jit(solution)/shard_map/ppermute | solution.py:419
  98.3 0.0 all-to-all-done.2.parts_ref
  98.3 0.9 shard_map.224
  99.2 4.1 %all-to-all-start.3 = ((bf16[32,32,256]{2,1,0:T(8,128)(2,1)}), bf16[32,32,256]{2,1,0:T(8,128)(2,1)S(1)}, u32[]{:S(2)}, u32[]{:S(2)}) async-start(bf16[32,32,256]{2,1,0:T(8,128)(2,1)} %shard_map.224), calls=%async_computation.3 | async-start | bytes 1048576 | tf_op jit(solution)/shard_map/all_to_all | solution.py:423
  103.3 0.9 constant_dynamic-slice_fusion.own_ref
  104.2 0.7 shard_map.223
  104.9 10.0 %all-to-all-done.3.all_ref = bf16[32,32,256]{2,1,0:T(8,128)(2,1)S(1)} async-done(((bf16[32,32,256]{2,1,0:T(8,128)(2,1)}), bf16[32,32,256]{2,1,0:T(8,128)(2,1)S(1)}, u32[]{:S(2)}, u32[]{:S(2)}) %all-to-all-start.3) | async-done | bytes 524320 | tf_op jit(solution)/shard_map/all_to_all | solution.py:423
  114.9 1.0 shard_map.225
  (10 shorter events, 0.0 us)
Async XLA Ops:
  3.6 44.4 %all-to-all-start = ((bf16[4,416,128]{2,1,0:T(8,128)(2,1)}), bf16[4,416,128]{2,1,0:T(8,128)(2,1)S(1)}, u32[]{:S(2)}, u32[]{:S(2)}) async-start(bf16[4,416,128]{2,1,0:T(8,128)(2,1)} %get-tuple-element.32), calls=%async_computation | async-start | bytes 851968 | tf_op jit(solution)/shard_map/all_to_all | solution.py:423
  13.9 34.1 %collective-permute-start = (bf16[16,6528]{1,0:T(8,128)(2,1)}, bf16[16,6528]{1,0:T(8,128)(2,1)}, u32[]{:S(2)}, u32[]{:S(2)}) collective-permute-start(bf16[16,6528]{1,0:T(8,128)(2,1)} %get-tuple-element.34), channel_id=1, source_target_pairs={{0,6},{1,7},{2,4},{3,5},{4,10},{5,11},{6,8},{7,9},{8,14},{9,15},{1... | collective-permute-start | bytes 626696 | tf_op jit(solution)/shard_map/ppermute | solution.py:415
  15.8 32.2 %collective-permute-start.1 = (bf16[16,6528]{1,0:T(8,128)(2,1)}, bf16[16,6528]{1,0:T(8,128)(2,1)}, u32[]{:S(2)}, u32[]{:S(2)}) collective-permute-start(bf16[16,6528]{1,0:T(8,128)(2,1)} %get-tuple-element.35), channel_id=1, source_target_pairs={{0,510},{1,511},{2,508},{3,509},{4,2},{5,3},{6,0},{7,1},{8,6},{9,7... | collective-permute-start | bytes 626696 | tf_op jit(solution)/shard_map/ppermute | solution.py:415
  27.2 20.7 %copy-start = (bf16[32,6272]{1,0:T(8,128)(2,1)S(1)}, bf16[32,6272]{1,0:T(8,128)(2,1)}, u32[]{:S(2)}) copy-start(bf16[32,6272]{1,0:T(8,128)(2,1)} %refs_0_.1) | copy-start | bytes 1204228
  53.2 4.3 %copy-start.1 = (bf16[2752,128]{1,0:T(8,128)(2,1)S(1)}, bf16[2752,128]{1,0:T(8,128)(2,1)}, u32[]{:S(2)}) copy-start(bf16[2752,128]{1,0:T(8,128)(2,1)} %get-tuple-element.42.high_ref) | copy-start | bytes 2113540
  53.2 16.1 %all-to-all-start.1 = ((bf16[32,32,256]{2,1,0:T(8,128)(2,1)}), bf16[32,32,256]{2,1,0:T(8,128)(2,1)S(1)}, u32[]{:S(2)}, u32[]{:S(2)}) async-start(bf16[32,32,256]{2,1,0:T(8,128)(2,1)} %shard_map.219.refs_8_), calls=%async_computation.1 | async-start | bytes 1048576 | tf_op jit(solution)/shard_map/all_to_all | solution.py:423
  57.5 26.3 %collective-permute-start.4 = (bf16[2752,128]{1,0:T(8,128)(2,1)S(1)}, bf16[2752,128]{1,0:T(8,128)(2,1)S(1)}, u32[]{:S(2)}, u32[]{:S(2)}) collective-permute-start(bf16[2752,128]{1,0:T(8,128)(2,1)S(1)} %copy-done.1), channel_id=1, source_target_pairs={{0,6},{2,0},{4,2},{6,4},{1,7},{3,1},{5,3},{7,5},{8,14},{10,8},{12,... | collective-permute-start | bytes 2113544 | tf_op jit(solution)/shard_map/ppermute | solution.py:407
  62.0 21.7 %collective-permute-start.3 = (bf16[2720,128]{1,0:T(8,128)(2,1)}, bf16[2720,128]{1,0:T(8,128)(2,1)}, u32[]{:S(2)}, u32[]{:S(2)}) collective-permute-start(bf16[2720,128]{1,0:T(8,128)(2,1)} %get-tuple-element.41.low_ref), channel_id=1, source_target_pairs={{0,2},{2,4},{4,6},{6,0},{1,3},{3,5},{5,7},{7,1},{8,10},{10,12},{12... | collective-permute-start | bytes 2088968 | tf_op jit(solution)/shard_map/ppermute | solution.py:407
  67.7 16.1 %copy-start.2 = (bf16[2720,128]{1,0:T(8,128)(2,1)S(1)}, bf16[2720,128]{1,0:T(8,128)(2,1)}, u32[]{:S(2)}) copy-start(bf16[2720,128]{1,0:T(8,128)(2,1)} %get-tuple-element.41.low_ref) | copy-start | bytes 2088964
  70.0 28.2 %all-to-all-start.2 = ((bf16[16,32,256]{2,1,0:T(8,128)(2,1)}), bf16[16,32,256]{2,1,0:T(8,128)(2,1)S(1)}, u32[]{:S(2)}, u32[]{:S(2)}) async-start(bf16[16,32,256]{2,1,0:T(8,128)(2,1)} %shard_map.221.after_ref), calls=%async_computation.2 | async-start | bytes 524288 | tf_op jit(solution)/shard_map/all_to_all | solution.py:423
  77.6 4.0 %collective-permute-start.2 = (bf16[2096,128]{1,0:T(8,128)(2,1)}, bf16[2096,128]{1,0:T(8,128)(2,1)S(1)}, u32[]{:S(2)}, u32[]{:S(2)}) collective-permute-start(bf16[2096,128]{1,0:T(8,128)(2,1)} %get-tuple-element.40), channel_id=1, source_target_pairs={{0,1},{1,0},{2,3},{3,2},{4,5},{5,4},{6,7},{7,6},{8,9},{9,8},{10,11... | collective-permute-start | bytes 1609736 | tf_op jit(solution)/shard_map/ppermute | solution.py:419
  83.8 1.0 copy-start.3
  90.2 14.0 %collective-permute-start.5 = (bf16[8,6272]{1,0:T(8,128)(2,1)S(1)}, bf16[8,6272]{1,0:T(8,128)(2,1)S(1)}, u32[]{:S(2)}, u32[]{:S(2)}) collective-permute-start(bf16[8,6272]{1,0:T(8,128)(2,1)S(1)} %get-tuple-element.45), channel_id=1, source_target_pairs={{0,1},{1,0},{2,3},{3,2},{4,5},{5,4},{6,7},{7,6},{8,9},{9,8},{10,11... | collective-permute-start | bytes 301064 | tf_op jit(solution)/shard_map/ppermute | solution.py:419
  92.8 11.4 %collective-permute-start.6 = (bf16[8,6272]{1,0:T(8,128)(2,1)S(1)}, bf16[8,6272]{1,0:T(8,128)(2,1)S(1)}, u32[]{:S(2)}, u32[]{:S(2)}) collective-permute-start(bf16[8,6272]{1,0:T(8,128)(2,1)S(1)} %get-tuple-element.46), channel_id=1, source_target_pairs={{0,2},{1,3},{2,0},{3,1},{4,6},{5,7},{6,4},{7,5},{8,10},{9,11},{10,... | collective-permute-start | bytes 301064 | tf_op jit(solution)/shard_map/ppermute | solution.py:419
  94.7 9.5 %collective-permute-start.7 = (bf16[8,6272]{1,0:T(8,128)(2,1)S(1)}, bf16[8,6272]{1,0:T(8,128)(2,1)S(1)}, u32[]{:S(2)}, u32[]{:S(2)}) collective-permute-start(bf16[8,6272]{1,0:T(8,128)(2,1)S(1)} %get-tuple-element.47), channel_id=1, source_target_pairs={{0,3},{1,2},{2,1},{3,0},{4,7},{5,6},{6,5},{7,4},{8,11},{9,10},{10,... | collective-permute-start | bytes 301064 | tf_op jit(solution)/shard_map/ppermute | solution.py:419
  99.2 15.7 %all-to-all-start.3 = ((bf16[32,32,256]{2,1,0:T(8,128)(2,1)}), bf16[32,32,256]{2,1,0:T(8,128)(2,1)S(1)}, u32[]{:S(2)}, u32[]{:S(2)}) async-start(bf16[32,32,256]{2,1,0:T(8,128)(2,1)} %shard_map.224), calls=%async_computation.3 | async-start | bytes 1048576 | tf_op jit(solution)/shard_map/all_to_all | solution.py:423

commit v7 on v6

--- a/solution.py
+++ b/solution.py
@@ -104,18 +104,18 @@
 
 def pack_body(
     m0_hbm, m1_hbm, m2_hbm, student_hbm, wsrc_hbm, wdst_hbm, wout_hbm, wrad_hbm, whead_hbm,
-    radial_hbm, low_ref, high_ref, bundle_hbm, m0_ref, m1_ref, m2_ref, sems,
+    radial_hbm, low_ref, high_ref, bundle_ref, m0_ref, m1_ref, m2_ref, sems,
 ):
     copies = fetch(
         (
             (m0_hbm, m0_ref), (m1_hbm, m1_ref), (m2_hbm, m2_ref),
-            (student_hbm, bundle_hbm.at[0:32]), (wsrc_hbm, bundle_hbm.at[32:288]),
-            (wdst_hbm, bundle_hbm.at[288:544]), (wout_hbm, bundle_hbm.at[544:800]),
-            (wrad_hbm, bundle_hbm.at[800:928]),
-            (whead_hbm.at[:C], bundle_hbm.at[928:1056, :C]),
-            (whead_hbm.at[C:], bundle_hbm.at[928:1056, C:]),
-            (radial_hbm, bundle_hbm.at[1056:1184, :C]),
-            (radial_hbm, bundle_hbm.at[1056:1184, C:]),
+            (student_hbm, bundle_ref.at[0:32]), (wsrc_hbm, bundle_ref.at[32:288]),
+            (wdst_hbm, bundle_ref.at[288:544]), (wout_hbm, bundle_ref.at[544:800]),
+            (wrad_hbm, bundle_ref.at[800:928]),
+            (whead_hbm.at[:C], bundle_ref.at[928:1056, :C]),
+            (whead_hbm.at[C:], bundle_ref.at[928:1056, C:]),
+            (radial_hbm, bundle_ref.at[1056:1184, :C]),
+            (radial_hbm, bundle_ref.at[1056:1184, C:]),
         ),
         sems,
     )
@@ -385,13 +385,13 @@
     out_ref[...] = (own_ref[...].astype(F32) + total * (1.0 / math.sqrt(DEG))).astype(BF)
 
 
-def call(body, outs, ins, scratch=(), scalars=0, raws=0, after=0, flops=0, room=24 << 10, outs_hbm=0):
+def call(body, outs, ins, scratch=(), scalars=0, raws=0, after=0, flops=0, room=24 << 10):
     specs = [SMEM] * scalars + [VMEM] * (len(ins) - scalars - raws - after)
     return pl.pallas_call(
         body,
         out_shape=tuple(jax.ShapeDtypeStruct(shape, dtype) for shape, dtype in outs),
         in_specs=specs + [HBM] * raws + [ANY] * after,
-        out_specs=(VMEM,) * (len(outs) - outs_hbm) + (HBM,) * outs_hbm,
+        out_specs=(VMEM,) * len(outs),
         scratch_shapes=list(scratch),
         compiler_params=pltpu.CompilerParams(vmem_limit_bytes=(FULL - room) << 10),
         cost_estimate=pl.CostEstimate(flops=flops, bytes_accessed=4096, transcendentals=0),
@@ -464,7 +464,6 @@
         raws=10,
         flops=1 << 30,
         room=1024,
-        outs_hbm=1,
     )
     (grads,) = call(
         functools.partial(early_body, 1.0 / (OWN * bricks)),

time: 117 us -> 104 us (0.89)
  Pallas kernels: 40.6 us -> 22.8 us
  starting transfers between devices: 55.5 us -> 61.8 us
  waiting for transfers between devices: 15.7 us -> 14.4 us
    pallas_call x9, Pallas kernels: 40.6 us -> 22.8 us  [call(): pl.pallas_call(body, out_shape=tuple((jax.ShapeDtypeStruct(shape, dtype)...]
    all_to_all x4, starting transfers between devices: 26.2 us -> 32.8 us  [exchange(): return lax.all_to_all(x, axes, 0, 0, tiled=True)]
    ppermute x2, waiting for transfers between devices: 2.2 us -> 0.01 us  [shifted(): lax.ppermute(x, axes, [(i, (i + by) % length) for i in range(length)])]
  transfers between devices with their start and end apart: 12 -> 12, of which waited for: 4 -> 4; matrix products, arithmetic and copies ran while one was open for 1% -> 1% of each run, Pallas kernels for 28% -> 14%
where the time goes in v7:
time: 104 us; the launch traced here: 103 us
  starting transfers between devices  61.8 us (59%)
  Pallas kernels  22.8 us (22%)
  waiting for transfers between devices  14.4 us (14%)
  between operations  2.12 us (2%)
  local copies, waits for them, and re-layouts  1.96 us (2%)
    all_to_all x4, starting transfers between devices, exchange(): return lax.all_to_all(x, axes, 0, 0, tiled=True)  32.8 us
    pallas_call x9, Pallas kernels, call(): pl.pallas_call(body, out_shape=tuple((jax.ShapeDtypeStruct(shape, dtype)...  22.8 us
    ppermute x2, starting transfers between devices, to_brick(): return lax.ppermute(x, BRICK + REP, pairs)  12.7 us
    all_to_all x4, waiting for transfers between devices, exchange(): return lax.all_to_all(x, axes, 0, 0, tiled=True)  11.5 us
    ppermute x4, starting transfers between devices, swapped(): lax.ppermute(x, axes, [(i, i ^ mask) for i in range(lax.axis_size(axes))])  9.9 us
    ppermute x2, starting transfers between devices, shifted(): lax.ppermute(x, axes, [(i, (i + by) % length) for i in range(length)])  6.46 us
  transfers between devices with their start and end apart: 12, of which 4 were waited for; matrix products, arithmetic and copies ran while one was open for 1% of the time, Pallas kernels for 14%

profile of v7, /device:TPU:1, one launch (start us, length us, event | category | flops | bytes accessed | tf_op | source)
XLA Modules:
  0.0 103.1 jit_solution(4966173994771957664)
XLA Ops:
  1.3 2.3 %shard_map.218 = (bf16[16,6528]{1,0:T(8,128)(2,1)}, bf16[16,6528]{1,0:T(8,128)(2,1)}, bf16[4,416,128]{2,1,0:T(8,128)(2,1)}) custom-call(s32[1]{0:T(128)S(6)} %copy.24.count_ref, s32[1,2,16]{2,1,0:T(2,128)} %lists_hbm.1, bf16[32,6272]{1,0:T(8,128)(2,1)} %refs_0_.1, bf16[32,256]{1,0:T(8,128)(2,1)} %student_hbm.3, bf16[224,896]{1,0:T(8,128)(2,1)} %m0_hbm.3, ...), custom_call_target="tpu_custom_call" | custom-call | bytes 4096 | tf_op jit(solution)/shard_map/pallas_call | solution.py:390
  3.6 10.3 %all-to-all-start = ((bf16[4,416,128]{2,1,0:T(8,128)(2,1)}), bf16[4,416,128]{2,1,0:T(8,128)(2,1)S(1)}, u32[]{:S(2)}, u32[]{:S(2)}) async-start(bf16[4,416,128]{2,1,0:T(8,128)(2,1)} %get-tuple-element.32), calls=%async_computation | async-start | bytes 851968 | tf_op jit(solution)/shard_map/all_to_all | solution.py:423
  13.9 1.9 %collective-permute-start = (bf16[16,6528]{1,0:T(8,128)(2,1)}, bf16[16,6528]{1,0:T(8,128)(2,1)}, u32[]{:S(2)}, u32[]{:S(2)}) collective-permute-start(bf16[16,6528]{1,0:T(8,128)(2,1)} %get-tuple-element.34), channel_id=1, source_target_pairs={{0,6},{1,7},{2,4},{3,5},{4,10},{5,11},{6,8},{7,9},{8,14},{9,15},{1... | collective-permute-start | bytes 626696 | tf_op jit(solution)/shard_map/ppermute | solution.py:415
  15.8 10.8 %collective-permute-start.1 = (bf16[16,6528]{1,0:T(8,128)(2,1)}, bf16[16,6528]{1,0:T(8,128)(2,1)}, u32[]{:S(2)}, u32[]{:S(2)}) collective-permute-start(bf16[16,6528]{1,0:T(8,128)(2,1)} %get-tuple-element.35), channel_id=1, source_target_pairs={{0,510},{1,511},{2,508},{3,509},{4,2},{5,3},{6,0},{7,1},{8,6},{9,7... | collective-permute-start | bytes 626696 | tf_op jit(solution)/shard_map/ppermute | solution.py:415
  27.2 0.0 copy-start
  27.3 2.9 %shard_map.217 = (bf16[2720,128]{1,0:T(8,128)(2,1)}, bf16[2752,128]{1,0:T(8,128)(2,1)}, bf16[1184,256]{1,0:T(8,128)(2,1)}) custom-call(bf16[224,896]{1,0:T(8,128)(2,1)} %m0_hbm.3, bf16[2,192,768]{2,1,0:T(8,128)(2,1)} %m1_hbm.1, bf16[2,160,640]{2,1,0:T(8,128)(2,1)} %m2_hbm.1, bf16[32,256]{1,0:T(8,128)(2,1)} %student_hbm.3, bf16[256,256]{1,0:T(8,128)(2,1)} %wsrc_hbm.1, ...), custom_call_target="tpu_custom_call" | custom-call | flops 1073741824 | bytes 4096 | tf_op jit(solution)/shard_map/pallas_call | solution.py:390
  30.2 0.0 collective-permute-done.left_ref.refs_1_
  30.2 0.9 collective-permute-done.1.right_ref.refs_2_
  31.1 0.0 all-to-all-done.meta_ref
  31.1 5.2 %shard_map.219.refs_8_ = bf16[32,32,256]{2,1,0:T(8,128)(2,1)} custom-call(s32[1]{0:T(128)S(6)} %copy.25.atoms_ref, s32[1]{0:T(128)} %bitcast.rep_ref, bf16[4,416,128]{2,1,0:T(8,128)(2,1)S(1)} %all-to-all-done.meta_ref, bf16[1184,256]{1,0:T(8,128)(2,1)} %get-tuple-element.33.bundle_ref, bf16[32,6272]{1,0:T(8,128)(2,1)S(1)} %copy-done, ...), custom_call_target="tpu_custom_call" | custom-call | flops 2147483648 | bytes 4096 | tf_op jit(solution)/shard_map/pallas_call | solution.py:390
  36.2 4.9 %all-to-all-start.1 = ((bf16[32,32,256]{2,1,0:T(8,128)(2,1)}), bf16[32,32,256]{2,1,0:T(8,128)(2,1)S(1)}, u32[]{:S(2)}, u32[]{:S(2)}) async-start(bf16[32,32,256]{2,1,0:T(8,128)(2,1)} %shard_map.219.refs_8_), calls=%async_computation.1 | async-start | bytes 1048576 | tf_op jit(solution)/shard_map/all_to_all | solution.py:423
  41.1 4.5 %collective-permute-start.4 = (bf16[2752,128]{1,0:T(8,128)(2,1)S(1)}, bf16[2752,128]{1,0:T(8,128)(2,1)S(1)}, u32[]{:S(2)}, u32[]{:S(2)}) collective-permute-start(bf16[2752,128]{1,0:T(8,128)(2,1)S(1)} %copy-done.1), channel_id=1, source_target_pairs={{0,6},{2,0},{4,2},{6,4},{1,7},{3,1},{5,3},{7,5},{8,14},{10,8},{12,... | collective-permute-start | bytes 2113544 | tf_op jit(solution)/shard_map/ppermute | solution.py:407
  45.7 1.9 %collective-permute-start.3 = (bf16[2720,128]{1,0:T(8,128)(2,1)}, bf16[2720,128]{1,0:T(8,128)(2,1)}, u32[]{:S(2)}, u32[]{:S(2)}) collective-permute-start(bf16[2720,128]{1,0:T(8,128)(2,1)} %get-tuple-element.41.low_ref), channel_id=1, source_target_pairs={{0,2},{2,4},{4,6},{6,0},{1,3},{3,5},{5,7},{7,1},{8,10},{10,12},{12... | collective-permute-start | bytes 2088968 | tf_op jit(solution)/shard_map/ppermute | solution.py:407
  47.6 3.7 %shard_map.220 = (bf16[2096,128]{1,0:T(8,128)(2,1)}, bf16[2096,128]{1,0:T(8,128)(2,1)}) custom-call(s32[1]{0:T(128)S(6)} %copy.24.count_ref, s32[1]{0:T(128)} %bitcast.rep_ref, bf16[32,6272]{1,0:T(8,128)(2,1)} %refs_0_.1, bf16[16,6528]{1,0:T(8,128)(2,1)} %collective-permute-done.left_ref.refs_1_, bf16[16,6528]{1,0:T(8,128)(2,1)} %collective-permute-done.1.right_ref.refs_2_, ...), custom_call_target="tpu_custom_call" | custom-call | flops 2147483648 | bytes 4096 | tf_op jit(solution)/shard_map/pallas_call | solution.py:390
  51.3 1.6 %all-to-all-done.1.parts_ref = bf16[32,32,256]{2,1,0:T(8,128)(2,1)S(1)} async-done(((bf16[32,32,256]{2,1,0:T(8,128)(2,1)}), bf16[32,32,256]{2,1,0:T(8,128)(2,1)S(1)}, u32[]{:S(2)}, u32[]{:S(2)}) %all-to-all-start.1) | async-done | bytes 524320 | tf_op jit(solution)/shard_map/all_to_all | solution.py:423
  52.9 0.8 shard_map.221.after_ref
  53.7 11.1 %all-to-all-start.2 = ((bf16[16,32,256]{2,1,0:T(8,128)(2,1)}), bf16[16,32,256]{2,1,0:T(8,128)(2,1)S(1)}, u32[]{:S(2)}, u32[]{:S(2)}) async-start(bf16[16,32,256]{2,1,0:T(8,128)(2,1)} %shard_map.221.after_ref), calls=%async_computation.2 | async-start | bytes 524288 | tf_op jit(solution)/shard_map/all_to_all | solution.py:423
  64.8 2.0 %collective-permute-start.2 = (bf16[2096,128]{1,0:T(8,128)(2,1)}, bf16[2096,128]{1,0:T(8,128)(2,1)S(1)}, u32[]{:S(2)}, u32[]{:S(2)}) collective-permute-start(bf16[2096,128]{1,0:T(8,128)(2,1)} %get-tuple-element.40), channel_id=1, source_target_pairs={{0,1},{1,0},{2,3},{3,2},{4,5},{5,4},{6,7},{7,6},{8,9},{9,8},{10,11... | collective-permute-start | bytes 1609736 | tf_op jit(solution)/shard_map/ppermute | solution.py:419
  66.8 2.0 %collective-permute-done.2.got_ref = bf16[2096,128]{1,0:T(8,128)(2,1)S(1)} collective-permute-done((bf16[2096,128]{1,0:T(8,128)(2,1)}, bf16[2096,128]{1,0:T(8,128)(2,1)S(1)}, u32[]{:S(2)}, u32[]{:S(2)}) %collective-permute-start.2) | collective-permute-done | bytes 536608 | tf_op jit(solution)/shard_map/ppermute | solution.py:419
  68.8 0.0 collective-permute-done.3.far_low_ref
  68.8 0.0 collective-permute-done.4.far_high_ref
  68.9 1.0 %copy-done.3 = bf16[2096,128]{1,0:T(8,128)(2,1)S(1)} copy-done((bf16[2096,128]{1,0:T(8,128)(2,1)S(1)}, bf16[2096,128]{1,0:T(8,128)(2,1)}, u32[]{:S(2)}) %copy-start.3) | copy-done | bytes 536600
  69.9 5.3 %shard_map.222 = (f32[8,6272]{1,0:T(8,128)S(1)}, bf16[8,6272]{1,0:T(8,128)(2,1)S(1)}, bf16[8,6272]{1,0:T(8,128)(2,1)S(1)}, bf16[8,6272]{1,0:T(8,128)(2,1)S(1)}) custom-call(s32[1]{0:T(128)} %bitcast.rep_ref, bf16[2096,128]{1,0:T(8,128)(2,1)S(1)} %copy-done.3, bf16[2096,128]{1,0:T(8,128)(2,1)S(1)} %collective-permute-done.2.got_ref, ...), custom_call_target="tpu_custom_call" | custom-call | flops 4294967296 | bytes 4096 | tf_op jit(solution)/shard_map/pallas_call | solution.py:390
  75.2 2.0 %collective-permute-start.5 = (bf16[8,6272]{1,0:T(8,128)(2,1)S(1)}, bf16[8,6272]{1,0:T(8,128)(2,1)S(1)}, u32[]{:S(2)}, u32[]{:S(2)}) collective-permute-start(bf16[8,6272]{1,0:T(8,128)(2,1)S(1)} %get-tuple-element.45), channel_id=1, source_target_pairs={{0,1},{1,0},{2,3},{3,2},{4,5},{5,4},{6,7},{7,6},{8,9},{9,8},{10,11... | collective-permute-start | bytes 301064 | tf_op jit(solution)/shard_map/ppermute | solution.py:419
  77.3 2.3 %collective-permute-start.6 = (bf16[8,6272]{1,0:T(8,128)(2,1)S(1)}, bf16[8,6272]{1,0:T(8,128)(2,1)S(1)}, u32[]{:S(2)}, u32[]{:S(2)}) collective-permute-start(bf16[8,6272]{1,0:T(8,128)(2,1)S(1)} %get-tuple-element.46), channel_id=1, source_target_pairs={{0,2},{1,3},{2,0},{3,1},{4,6},{5,7},{6,4},{7,5},{8,10},{9,11},{10,... | collective-permute-start | bytes 301064 | tf_op jit(solution)/shard_map/ppermute | solution.py:419
  79.6 3.5 %collective-permute-start.7 = (bf16[8,6272]{1,0:T(8,128)(2,1)S(1)}, bf16[8,6272]{1,0:T(8,128)(2,1)S(1)}, u32[]{:S(2)}, u32[]{:S(2)}) collective-permute-start(bf16[8,6272]{1,0:T(8,128)(2,1)S(1)} %get-tuple-element.47), channel_id=1, source_target_pairs={{0,3},{1,2},{2,1},{3,0},{4,7},{5,6},{6,5},{7,4},{8,11},{9,10},{10,... | collective-permute-start | bytes 301064 | tf_op jit(solution)/shard_map/ppermute | solution.py:419
  83.1 0.9 shard_map.224
  84.0 6.5 %all-to-all-start.3 = ((bf16[32,32,256]{2,1,0:T(8,128)(2,1)}), bf16[32,32,256]{2,1,0:T(8,128)(2,1)S(1)}, u32[]{:S(2)}, u32[]{:S(2)}) async-start(bf16[32,32,256]{2,1,0:T(8,128)(2,1)} %shard_map.224), calls=%async_computation.3 | async-start | bytes 1048576 | tf_op jit(solution)/shard_map/all_to_all | solution.py:423
  90.5 0.9 constant_dynamic-slice_fusion.own_ref
  91.5 0.7 shard_map.223
  92.2 10.0 %all-to-all-done.3.all_ref = bf16[32,32,256]{2,1,0:T(8,128)(2,1)S(1)} async-done(((bf16[32,32,256]{2,1,0:T(8,128)(2,1)}), bf16[32,32,256]{2,1,0:T(8,128)(2,1)S(1)}, u32[]{:S(2)}, u32[]{:S(2)}) %all-to-all-start.3) | async-done | bytes 524320 | tf_op jit(solution)/shard_map/all_to_all | solution.py:423
  102.1 1.0 shard_map.225
  (10 shorter events, 0.0 us)
Async XLA Ops:
  3.6 27.5 %all-to-all-start = ((bf16[4,416,128]{2,1,0:T(8,128)(2,1)}), bf16[4,416,128]{2,1,0:T(8,128)(2,1)S(1)}, u32[]{:S(2)}, u32[]{:S(2)}) async-start(bf16[4,416,128]{2,1,0:T(8,128)(2,1)} %get-tuple-element.32), calls=%async_computation | async-start | bytes 851968 | tf_op jit(solution)/shard_map/all_to_all | solution.py:423
  13.9 16.3 %collective-permute-start = (bf16[16,6528]{1,0:T(8,128)(2,1)}, bf16[16,6528]{1,0:T(8,128)(2,1)}, u32[]{:S(2)}, u32[]{:S(2)}) collective-permute-start(bf16[16,6528]{1,0:T(8,128)(2,1)} %get-tuple-element.34), channel_id=1, source_target_pairs={{0,6},{1,7},{2,4},{3,5},{4,10},{5,11},{6,8},{7,9},{8,14},{9,15},{1... | collective-permute-start | bytes 626696 | tf_op jit(solution)/shard_map/ppermute | solution.py:415
  15.8 15.3 %collective-permute-start.1 = (bf16[16,6528]{1,0:T(8,128)(2,1)}, bf16[16,6528]{1,0:T(8,128)(2,1)}, u32[]{:S(2)}, u32[]{:S(2)}) collective-permute-start(bf16[16,6528]{1,0:T(8,128)(2,1)} %get-tuple-element.35), channel_id=1, source_target_pairs={{0,510},{1,511},{2,508},{3,509},{4,2},{5,3},{6,0},{7,1},{8,6},{9,7... | collective-permute-start | bytes 626696 | tf_op jit(solution)/shard_map/ppermute | solution.py:415
  27.2 3.8 %copy-start = (bf16[32,6272]{1,0:T(8,128)(2,1)S(1)}, bf16[32,6272]{1,0:T(8,128)(2,1)}, u32[]{:S(2)}) copy-start(bf16[32,6272]{1,0:T(8,128)(2,1)} %refs_0_.1) | copy-start | bytes 1204228
  36.2 4.9 %copy-start.1 = (bf16[2752,128]{1,0:T(8,128)(2,1)S(1)}, bf16[2752,128]{1,0:T(8,128)(2,1)}, u32[]{:S(2)}) copy-start(bf16[2752,128]{1,0:T(8,128)(2,1)} %get-tuple-element.42.high_ref) | copy-start | bytes 2113540
  36.2 16.6 %all-to-all-start.1 = ((bf16[32,32,256]{2,1,0:T(8,128)(2,1)}), bf16[32,32,256]{2,1,0:T(8,128)(2,1)S(1)}, u32[]{:S(2)}, u32[]{:S(2)}) async-start(bf16[32,32,256]{2,1,0:T(8,128)(2,1)} %shard_map.219.refs_8_), calls=%async_computation.1 | async-start | bytes 1048576 | tf_op jit(solution)/shard_map/all_to_all | solution.py:423
  41.1 27.7 %collective-permute-start.4 = (bf16[2752,128]{1,0:T(8,128)(2,1)S(1)}, bf16[2752,128]{1,0:T(8,128)(2,1)S(1)}, u32[]{:S(2)}, u32[]{:S(2)}) collective-permute-start(bf16[2752,128]{1,0:T(8,128)(2,1)S(1)} %copy-done.1), channel_id=1, source_target_pairs={{0,6},{2,0},{4,2},{6,4},{1,7},{3,1},{5,3},{7,5},{8,14},{10,8},{12,... | collective-permute-start | bytes 2113544 | tf_op jit(solution)/shard_map/ppermute | solution.py:407
  45.7 23.2 %collective-permute-start.3 = (bf16[2720,128]{1,0:T(8,128)(2,1)}, bf16[2720,128]{1,0:T(8,128)(2,1)}, u32[]{:S(2)}, u32[]{:S(2)}) collective-permute-start(bf16[2720,128]{1,0:T(8,128)(2,1)} %get-tuple-element.41.low_ref), channel_id=1, source_target_pairs={{0,2},{2,4},{4,6},{6,0},{1,3},{3,5},{5,7},{7,1},{8,10},{10,12},{12... | collective-permute-start | bytes 2088968 | tf_op jit(solution)/shard_map/ppermute | solution.py:407
  51.3 17.5 %copy-start.2 = (bf16[2720,128]{1,0:T(8,128)(2,1)S(1)}, bf16[2720,128]{1,0:T(8,128)(2,1)}, u32[]{:S(2)}) copy-start(bf16[2720,128]{1,0:T(8,128)(2,1)} %get-tuple-element.41.low_ref) | copy-start | bytes 2088964
  53.7 29.5 %all-to-all-start.2 = ((bf16[16,32,256]{2,1,0:T(8,128)(2,1)}), bf16[16,32,256]{2,1,0:T(8,128)(2,1)S(1)}, u32[]{:S(2)}, u32[]{:S(2)}) async-start(bf16[16,32,256]{2,1,0:T(8,128)(2,1)} %shard_map.221.after_ref), calls=%async_computation.2 | async-start | bytes 524288 | tf_op jit(solution)/shard_map/all_to_all | solution.py:423
  64.8 4.0 %collective-permute-start.2 = (bf16[2096,128]{1,0:T(8,128)(2,1)}, bf16[2096,128]{1,0:T(8,128)(2,1)S(1)}, u32[]{:S(2)}, u32[]{:S(2)}) collective-permute-start(bf16[2096,128]{1,0:T(8,128)(2,1)} %get-tuple-element.40), channel_id=1, source_target_pairs={{0,1},{1,0},{2,3},{3,2},{4,5},{5,4},{6,7},{7,6},{8,9},{9,8},{10,11... | collective-permute-start | bytes 1609736 | tf_op jit(solution)/shard_map/ppermute | solution.py:419
  68.8 1.0 %copy-start.3 = (bf16[2096,128]{1,0:T(8,128)(2,1)S(1)}, bf16[2096,128]{1,0:T(8,128)(2,1)}, u32[]{:S(2)}) copy-start(bf16[2096,128]{1,0:T(8,128)(2,1)} %get-tuple-element.39.keep_ref) | copy-start | bytes 1609732
  75.2 16.2 %collective-permute-start.5 = (bf16[8,6272]{1,0:T(8,128)(2,1)S(1)}, bf16[8,6272]{1,0:T(8,128)(2,1)S(1)}, u32[]{:S(2)}, u32[]{:S(2)}) collective-permute-start(bf16[8,6272]{1,0:T(8,128)(2,1)S(1)} %get-tuple-element.45), channel_id=1, source_target_pairs={{0,1},{1,0},{2,3},{3,2},{4,5},{5,4},{6,7},{7,6},{8,9},{9,8},{10,11... | collective-permute-start | bytes 301064 | tf_op jit(solution)/shard_map/ppermute | solution.py:419
  77.3 14.1 %collective-permute-start.6 = (bf16[8,6272]{1,0:T(8,128)(2,1)S(1)}, bf16[8,6272]{1,0:T(8,128)(2,1)S(1)}, u32[]{:S(2)}, u32[]{:S(2)}) collective-permute-start(bf16[8,6272]{1,0:T(8,128)(2,1)S(1)} %get-tuple-element.46), channel_id=1, source_target_pairs={{0,2},{1,3},{2,0},{3,1},{4,6},{5,7},{6,4},{7,5},{8,10},{9,11},{10,... | collective-permute-start | bytes 301064 | tf_op jit(solution)/shard_map/ppermute | solution.py:419
  79.6 11.8 %collective-permute-start.7 = (bf16[8,6272]{1,0:T(8,128)(2,1)S(1)}, bf16[8,6272]{1,0:T(8,128)(2,1)S(1)}, u32[]{:S(2)}, u32[]{:S(2)}) collective-permute-start(bf16[8,6272]{1,0:T(8,128)(2,1)S(1)} %get-tuple-element.47), channel_id=1, source_target_pairs={{0,3},{1,2},{2,1},{3,0},{4,7},{5,6},{6,5},{7,4},{8,11},{9,10},{10,... | collective-permute-start | bytes 301064 | tf_op jit(solution)/shard_map/ppermute | solution.py:419
  84.0 18.1 %all-to-all-start.3 = ((bf16[32,32,256]{2,1,0:T(8,128)(2,1)}), bf16[32,32,256]{2,1,0:T(8,128)(2,1)S(1)}, u32[]{:S(2)}, u32[]{:S(2)}) async-start(bf16[32,32,256]{2,1,0:T(8,128)(2,1)} %shard_map.224), calls=%async_computation.3 | async-start | bytes 1048576 | tf_op jit(solution)/shard_map/all_to_all | solution.py:423
